TPU v7x, 32 devices: a whole 2x2x4 slice. The times are simulated.
32 devices in a mesh: store: 8 (over y, x, core), ctx: 4 (over z).
Axes of the slice: x: 2, y: 2, z: 4, core: 2. Of those that a mesh axis runs over, the one named last changes fastest.
Arguments:
- store_kv: bfloat16 [256, 32, 1024], P('store', 'ctx'), may hold values from -136 to 136, as said below
- block_slot: int32 [8, 16], P('store'), may hold values from 0 to 31, as said below
- block_owner: int32 [8, 16], P('store'), may hold values from 0 to 7, as said below
- rec_pos: int32 [8, 256], P('store'), may hold values from 0 to 511, as said below
- states: bfloat16 [8, 256, 8192], P('store', 'ctx'), may hold values from -6 to 6
- w_query: bfloat16 [8192, 4096], P('store', 'ctx'), may hold values from -0.0625 to 0.0625
- w_keyval: bfloat16 [8192, 1024], P('store', 'ctx'), may hold values from -0.125 to 0.125
Outputs:
- attended: bfloat16 [8, 256, 4096], P('store', None, 'ctx')
Inputs may be any that keep to these rules, and one draw needn't show every extreme that they name: store_kv entries lie within the stated bounds. `block_slot`: ids are distinct within a request. `block_owner`: no owner appears more than 2 times in one request's list, and in every list some owner appears exactly 2 times. `rec_pos`: positions are distinct within a request and include 0 and 511.
All inputs are finite; a program needn't handle non-finite values.
Results may differ from a plain program's by a relative error of at most 0.0033.
The roundings to bfloat16 on the way count: a program that leaves them out, or rounds other values in their place, can miss the bound.
Values may be sent and summed in bfloat16 or wider, within the bound.
No kernel may reach another device: no remote copies, remote signals or barrier semaphores. Data moves between devices by JAX's collectives and lax.ppermute only.
A program may use at most 128 MiB of HBM per device.

v0:
```python
import math

import jax
import jax.numpy as jnp
from jax import lax
from jax.sharding import PartitionSpec as P

QH = 32
KVH = 4
HD = 128
CAP = 2


def rotate(values, positions):
    midpoint = values.shape[-1] // 2
    frequency = jnp.exp(
        jnp.arange(midpoint, dtype=jnp.float32) * (-2.0 * math.log(500000.0) / values.shape[-1])
    )
    angles = positions.astype(jnp.float32)[:, None] * frequency[None, :]
    cosine = jnp.cos(angles)[:, None, :]
    sine_term = jnp.sin(angles)[:, None, :]
    leading = values[..., :midpoint]
    trailing = values[..., midpoint:]
    return jnp.concatenate(
        (leading * cosine - trailing * sine_term, trailing * cosine + leading * sine_term), axis=-1
    )


def normalize(states):
    floated = states.astype(jnp.float32)
    return (
        floated * lax.rsqrt(jnp.mean(floated * floated, axis=-1, keepdims=True) + 1e-05)
    ).astype(jnp.bfloat16)


def body(store_kv, block_slot, block_owner, rec_pos, states, w_query, w_keyval):
    store_count = lax.axis_size("store")
    ctx_count = lax.axis_size("ctx")
    my_index = lax.axis_index("ctx")
    piece_rows = store_kv.shape[1]
    row_width = store_kv.shape[2]
    block_count = block_slot.shape[1]
    rec_count = rec_pos.shape[1]
    slot_ids = block_slot[0]
    owners = block_owner[0]
    positions = rec_pos[0]
    slot_order = jnp.arange(block_count)
    earlier = slot_order[None, :] < slot_order[:, None]
    slot_ranks = jnp.sum((owners[:, None] == owners[None, :]) & earlier, axis=1)
    slot_hits = (owners[:, None, None] == jnp.arange(store_count)[None, :, None]) & (
        slot_ranks[:, None, None] == jnp.arange(CAP)[None, None, :]
    )
    wanted = jnp.sum(jnp.where(slot_hits, slot_ids[:, None, None], 0), axis=0)
    arrived = lax.all_to_all(
        store_kv[lax.all_to_all(wanted, "store", split_axis=0, concat_axis=0, tiled=True)],
        "store",
        split_axis=0,
        concat_axis=0,
        tiled=True,
    )
    shard_rows = block_count * piece_rows
    local_rows = arrived.reshape(store_count * CAP, piece_rows, row_width)[
        owners * CAP + slot_ranks
    ].reshape(shard_rows, row_width)
    normed = normalize(states[0])
    query_cols = w_query.shape[1]
    query_weight, keyval_weight = (
        lax.all_gather(w_query, "store", axis=0, tiled=True),
        lax.all_gather(w_keyval, "store", axis=0, tiled=True),
    )
    row_piece = lax.all_gather(normed, "ctx", axis=0, tiled=True)
    projected = jnp.concatenate(
        (
            jnp.dot(row_piece, query_weight, preferred_element_type=jnp.float32),
            jnp.dot(row_piece, keyval_weight, preferred_element_type=jnp.float32),
        ),
        axis=1,
    )
    query_raw = projected[:, :query_cols]
    keyval_raw = projected[:, query_cols:]
    heads_here = query_cols // HD
    group_size = QH // KVH
    queries = (
        rotate(query_raw.reshape(rec_count, heads_here, HD), positions) * HD ** (-0.5)
    ).astype(jnp.bfloat16)
    fresh_rows = lax.all_gather(keyval_raw.astype(jnp.bfloat16), "ctx", axis=1, tiled=True)
    shared_head = my_index * heads_here // group_size
    fresh_key = rotate(
        lax.dynamic_slice_in_dim(fresh_rows, shared_head * HD, HD, 1)
        .astype(jnp.float32)
        .reshape(rec_count, 1, HD),
        positions,
    )
    fresh_key = fresh_key.astype(jnp.bfloat16).reshape(rec_count, HD)
    fresh_value = lax.dynamic_slice_in_dim(fresh_rows, KVH * HD + shared_head * HD, HD, 1)
    gathered = lax.all_gather(local_rows, "ctx", axis=0, tiled=True)
    key_rows = lax.dynamic_slice_in_dim(gathered, shared_head * HD, HD, 1)
    value_rows = lax.dynamic_slice_in_dim(gathered, KVH * HD + shared_head * HD, HD, 1)
    row_ids = jnp.arange(ctx_count * shard_rows)
    block_len = piece_rows * ctx_count
    key_pos = (
        row_ids % shard_rows // piece_rows * block_len
        + row_ids // shard_rows * piece_rows
        + row_ids % piece_rows
    )
    targets = (
        positions % block_len // piece_rows * shard_rows
        + positions // block_len * piece_rows
        + positions % piece_rows
    )
    key_rows = key_rows.at[targets].set(fresh_key)
    value_rows = value_rows.at[targets].set(fresh_value)
    scores = jnp.einsum("rhd,cd->hrc", queries, key_rows, preferred_element_type=jnp.float32)
    visible = key_pos[None, None, :] <= positions[None, :, None]
    scores = jnp.where(visible, scores, -1e30)
    row_max = jnp.max(scores, axis=-1, keepdims=True)
    exponent = jnp.exp(scores - row_max)
    weights = (exponent / jnp.sum(exponent, axis=-1, keepdims=True)).astype(jnp.bfloat16)
    attended = jnp.einsum("hrc,cd->rhd", weights, value_rows, preferred_element_type=jnp.float32)
    return attended.reshape(1, rec_count, heads_here * HD).astype(jnp.bfloat16)


def solution(mesh):
    return jax.shard_map(
        body,
        mesh=mesh,
        in_specs=(
            P("store", "ctx", None),
            P("store", None),
            P("store", None),
            P("store", None),
            P("store", "ctx", None),
            P("store", "ctx"),
            P("store", "ctx"),
        ),
        out_specs=P("store", None, "ctx"),
        check_vma=False,
    )
```

profile of v0, /device:TPU:0, one launch (start us, length us, event | category | flops | bytes accessed | tf_op | source)
XLA Modules:
  0.0 291.3 jit_solution(6836046515975617017)
XLA Ops:
  6.5 0.0 copy-start
  6.5 0.9 convert_reduce_fusion
  7.4 0.7 iota_compare_fusion.1
  8.1 0.8 select_reduce_fusion
  8.9 0.7 copy.28
  9.6 5.2 %all-to-all-start = ((s32[8,1,2]{2,1,0:T(1,128)}), s32[8,1,2]{2,1,0:T(1,128)S(1)}, u32[]{:S(2)}, u32[]{:S(2)}) async-start(s32[8,1,2]{2,1,0:T(1,128)} %copy.28), calls=%async_computation | async-start | bytes 8192 | tf_op jit(solution)/shard_map/all_to_all | solution.py:55
  14.8 0.7 fusion.50
  15.4 0.0 copy-start.1
  15.4 1.5 fusion.2
  17.0 2.4 all-to-all-done
  19.4 0.1 copy.29
  19.4 0.1 copy.30
  19.5 0.1 reshape.550
  19.6 0.0 copy-done
  19.6 1.3 gather_fusion
  20.9 3.4 %all-to-all-start.1 = ((bf16[8,2,8,1024]{3,2,1,0:T(8,128)(2,1)}), bf16[8,2,8,1024]{3,2,1,0:T(8,128)(2,1)S(1)}, u32[]{:S(2)}, u32[]{:S(2)}) async-start(bf16[8,2,8,1024]{3,2,1,0:T(8,128)(2,1)} %bitcast.4), calls=%async_computation.1 | async-start | bytes 524288 | tf_op jit(solution)/shard_map/all_to_all | solution.py:54
  24.3 0.0 all-gather.5.cloned.1.call-start
  24.4 6.8 %all-to-all-done.1 = bf16[8,2,8,1024]{3,2,1,0:T(8,128)(2,1)S(1)} async-done(((bf16[8,2,8,1024]{3,2,1,0:T(8,128)(2,1)}), bf16[8,2,8,1024]{3,2,1,0:T(8,128)(2,1)S(1)}, u32[]{:S(2)}, u32[]{:S(2)}) %all-to-all-start.1) | async-done | bytes 262176 | tf_op jit(solution)/shard_map/all_to_all | solution.py:54
  31.2 1.3 gather_fusion.1
  32.5 0.0 all-gather.5.cloned.1.call-update
  32.5 0.0 all-gather.7.cloned.1.call-start
  32.5 2.4 fusion.3
  35.0 0.0 all-gather.7.cloned.1.call-update
  35.0 0.0 all-gather.9.cloned.1.call-start
  35.0 0.7 all-gather.9.cloned.1.call-update
  35.7 0.0 all-gather.11.cloned.1.call-start
  35.8 0.5 all-gather.11.cloned.1.call-update
  36.3 0.0 copy-done.1
  36.4 0.1 broadcast_compare_fusion
  36.6 0.5 multiply_cosine_fusion
  37.1 22.8 %all-gather.5.cloned.1.call-done = bf16[512,1024]{1,0:T(8,128)(2,1)} async-done(((bf16[128,1024]{1,0:T(8,128)(2,1)}), bf16[512,1024]{1,0:T(8,128)(2,1)}) %all-gather.5.cloned.1.call-update) | async-done | bytes 1048592 | tf_op jit(solution)/shard_map/all_gather | solution.py:96
  59.9 1.0 constant_dynamic-slice_fusion.1
  60.9 80.9 %all-gather.7.cloned.1.call-done = bf16[256,8192]{1,0:T(8,128)(2,1)} async-done(((bf16[64,8192]{1,0:T(8,128)(2,1)}), bf16[256,8192]{1,0:T(8,128)(2,1)}) %all-gather.7.cloned.1.call-update) | async-done | bytes 4194320 | tf_op jit(solution)/shard_map/all_gather | solution.py:71
  141.8 37.2 %all-gather.9.cloned.1.call-done = bf16[8192,256]{1,0:T(8,128)(2,1)} async-done(((bf16[1024,256]{1,0:T(8,128)(2,1)}), bf16[8192,256]{1,0:T(8,128)(2,1)}) %all-gather.9.cloned.1.call-update) | async-done | bytes 4194320 | tf_op jit(solution)/shard_map/all_gather | solution.py:69
  179.0 4.7 %convolution_convert_fusion = bf16[256,256]{1,0:T(8,128)(2,1)S(1)} fusion(bf16[256,8192]{1,0:T(8,128)(2,1)} %all-gather.7.cloned.1.call-done, bf16[8192,256]{1,0:T(8,128)(2,1)} %all-gather.9.cloned.1.call-done), kind=kOutput, calls=%fused_computation.18 | convolution fusion | flops 1073807360 | bytes 8519680 | tf_op jit(solution)/shard_map/dot_general | solution.py:75
  183.7 16.1 %all_gather.18 = bf16[256,1024]{1,0:T(8,128)(2,1)S(1)} all-gather(bf16[256,256]{1,0:T(8,128)(2,1)S(1)} %convolution_convert_fusion), channel_id=1, replica_groups=mesh['store'=8,'ctx'=4] {'ctx'}, dimensions={1}, use_global_device_ids=true | all-gather | bytes 655360 | tf_op jit(solution)/shard_map/all_gather | solution.py:86
  199.7 1.3 scatter_custom_fusion
  201.1 0.6 fusion.29
  201.6 1.4 scatter_custom_fusion.1
  203.0 67.6 %all-gather.11.cloned.1.call-done = bf16[8192,1024]{1,0:T(8,128)(2,1)} async-done(((bf16[1024,1024]{1,0:T(8,128)(2,1)}), bf16[8192,1024]{1,0:T(8,128)(2,1)}) %all-gather.11.cloned.1.call-update) | async-done | bytes 16777232 | tf_op jit(solution)/shard_map/all_gather | solution.py:68
  270.6 9.3 %convolution_bitcast_fusion = f32[32,8,8,128]{3,1,2,0:T(8,128)S(1)} fusion(bf16[256,8192]{1,0:T(8,128)(2,1)} %all-gather.7.cloned.1.call-done, bf16[8192,1024]{1,0:T(8,128)(2,1)} %all-gather.11.cloned.1.call-done), kind=kOutput, calls=%fused_computation.16 | convolution fusion | flops 4294967296 | bytes 22020096 | tf_op jit(solution)/shard_map/dot_general | solution.py:74
  279.9 0.2 copy.41
  280.1 0.3 fusion.54
  280.5 0.4 multiply_subtract_fusion
  280.9 0.8 fusion.9
  281.7 1.6 fusion.55
  283.3 0.5 fusion.7
  283.7 1.0 copy.35
  (10 shorter events, 0.1 us)
Async XLA Ops:
  6.5 13.1 %copy-start = (bf16[32,8,1024]{2,1,0:T(8,128)(2,1)S(1)}, bf16[32,8,1024]{2,1,0:T(8,128)(2,1)}, u32[]{:S(2)}) copy-start(bf16[32,8,1024]{2,1,0:T(8,128)(2,1)} %param.7) | copy-start | bytes 1572868
  9.6 9.8 %all-to-all-start = ((s32[8,1,2]{2,1,0:T(1,128)}), s32[8,1,2]{2,1,0:T(1,128)S(1)}, u32[]{:S(2)}, u32[]{:S(2)}) async-start(s32[8,1,2]{2,1,0:T(1,128)} %copy.28), calls=%async_computation | async-start | bytes 8192 | tf_op jit(solution)/shard_map/all_to_all | solution.py:55
  15.4 20.9 %copy-start.1 = (s32[1,256]{1,0:T(1,128)S(1)}, s32[1,256]{1,0:T(1,128)}, u32[]{:S(2)}) copy-start(s32[1,256]{1,0:T(1,128)} %param.10) | copy-start | bytes 3076
  20.9 10.3 %all-to-all-start.1 = ((bf16[8,2,8,1024]{3,2,1,0:T(8,128)(2,1)}), bf16[8,2,8,1024]{3,2,1,0:T(8,128)(2,1)S(1)}, u32[]{:S(2)}, u32[]{:S(2)}) async-start(bf16[8,2,8,1024]{3,2,1,0:T(8,128)(2,1)} %bitcast.4), calls=%async_computation.1 | async-start | bytes 524288 | tf_op jit(solution)/shard_map/all_to_all | solution.py:54
  24.3 35.6 %all-gather.5.cloned.1.call-start = ((), (), s32[]{:S(2)}) async-start(), calls=%async_computation.2 | async-start | bytes 1310720 | tf_op jit(solution)/shard_map/all_gather | solution.py:96
  32.5 109.3 %all-gather.7.cloned.1.call-start = ((), (), s32[]{:S(2)}) async-start(), calls=%async_computation.3 | async-start | bytes 5242880 | tf_op jit(solution)/shard_map/all_gather | solution.py:71
  35.0 144.0 %all-gather.9.cloned.1.call-start = ((), (), s32[]{:S(2)}) async-start(), calls=%async_computation.4 | async-start | bytes 4718592 | tf_op jit(solution)/shard_map/all_gather | solution.py:69
  35.7 234.9 %all-gather.11.cloned.1.call-start = ((), (), s32[]{:S(2)}) async-start(), calls=%async_computation.5 | async-start | bytes 18874368 | tf_op jit(solution)/shard_map/all_gather | solution.py:68
Sparse Core Ops, SparseCore 0:
  32.6 27.2 all-gather.4
  61.5 80.2 all-gather.6
  143.7 35.2 all-gather.8
  180.7 89.8 all-gather.10
where the time goes:
time: 292 us; the launch traced here: 291 us
  waiting for transfers between devices  219 us (75%)
  blocking collectives  16.1 us (6%)
  matrix products  15.3 us (5%)
  between operations  13.3 us (5%)
  other arithmetic  11.7 us (4%)
  starting transfers between devices  8.75 us (3%)
  local copies, waits for them, and re-layouts  7.27 us (2%)
    all_gather x1, waiting for transfers between devices, body(): row_piece = lax.all_gather(normed, 'ctx', axis=0, tiled=True)  80.9 us
    all_gather x1, waiting for transfers between devices, body(): lax.all_gather(w_query, 'store', axis=0, tiled=True)  67.6 us
    all_gather x1, waiting for transfers between devices, body(): lax.all_gather(w_keyval, 'store', axis=0, tiled=True)  37.2 us
    all_gather x1, waiting for transfers between devices, body(): gathered = lax.all_gather(local_rows, 'ctx', axis=0, tiled=True)  22.8 us
    all_gather x1, blocking collectives, body(): lax.all_gather(keyval_raw.astype(jnp.bfloat16), 'ctx', axis=1, tiled=True)  16.1 us
    dot_general x1, matrix products, body(): jnp.dot(row_piece, query_weight, preferred_element_type=jnp.float32)  9.32 us
    all_to_all x1, waiting for transfers between devices, body(): lax.all_to_all(store_kv[lax.all_to_all(wanted, 'store', split_axis=0, con...  6.79 us
  transfers between devices with their start and end apart: 6, of which 6 were waited for; matrix products, arithmetic and copies ran while one was open for 5% of the time, Pallas kernels for 0%

commit v1 on v0

--- a/solution.py
+++ b/solution.py
@@ -1,14 +1,19 @@
+import functools
 import math
 
 import jax
 import jax.numpy as jnp
 from jax import lax
+from jax.experimental import pallas as pl
+from jax.experimental.pallas import tpu as pltpu
 from jax.sharding import PartitionSpec as P
 
 QH = 32
 KVH = 4
 HD = 128
 CAP = 2
+F32 = jnp.float32
+BF16 = jnp.bfloat16
 
 
 def rotate(values, positions):
@@ -33,17 +38,11 @@
     ).astype(jnp.bfloat16)
 
 
-def body(store_kv, block_slot, block_owner, rec_pos, states, w_query, w_keyval):
+def fetch_blocks(store_kv, slot_ids, owners):
     store_count = lax.axis_size("store")
-    ctx_count = lax.axis_size("ctx")
-    my_index = lax.axis_index("ctx")
     piece_rows = store_kv.shape[1]
     row_width = store_kv.shape[2]
-    block_count = block_slot.shape[1]
-    rec_count = rec_pos.shape[1]
-    slot_ids = block_slot[0]
-    owners = block_owner[0]
-    positions = rec_pos[0]
+    block_count = slot_ids.shape[0]
     slot_order = jnp.arange(block_count)
     earlier = slot_order[None, :] < slot_order[:, None]
     slot_ranks = jnp.sum((owners[:, None] == owners[None, :]) & earlier, axis=1)
@@ -58,10 +57,20 @@
         concat_axis=0,
         tiled=True,
     )
+    return arrived.reshape(store_count * CAP, piece_rows, row_width)[
+        owners * CAP + slot_ranks
+    ].reshape(block_count * piece_rows, row_width)
+
+
+def general_body(store_kv, block_slot, block_owner, rec_pos, states, w_query, w_keyval):
+    ctx_count = lax.axis_size("ctx")
+    my_index = lax.axis_index("ctx")
+    piece_rows = store_kv.shape[1]
+    block_count = block_slot.shape[1]
+    rec_count = rec_pos.shape[1]
+    positions = rec_pos[0]
     shard_rows = block_count * piece_rows
-    local_rows = arrived.reshape(store_count * CAP, piece_rows, row_width)[
-        owners * CAP + slot_ranks
-    ].reshape(shard_rows, row_width)
+    local_rows = fetch_blocks(store_kv, block_slot[0], block_owner[0])
     normed = normalize(states[0])
     query_cols = w_query.shape[1]
     query_weight, keyval_weight = (
@@ -69,15 +78,8 @@
         lax.all_gather(w_keyval, "store", axis=0, tiled=True),
     )
     row_piece = lax.all_gather(normed, "ctx", axis=0, tiled=True)
-    projected = jnp.concatenate(
-        (
-            jnp.dot(row_piece, query_weight, preferred_element_type=jnp.float32),
-            jnp.dot(row_piece, keyval_weight, preferred_element_type=jnp.float32),
-        ),
-        axis=1,
-    )
-    query_raw = projected[:, :query_cols]
-    keyval_raw = projected[:, query_cols:]
+    query_raw = jnp.dot(row_piece, query_weight, preferred_element_type=jnp.float32)
+    keyval_raw = jnp.dot(row_piece, keyval_weight, preferred_element_type=jnp.float32)
     heads_here = query_cols // HD
     group_size = QH // KVH
     queries = (
@@ -120,9 +122,292 @@
     return attended.reshape(1, rec_count, heads_here * HD).astype(jnp.bfloat16)
 
 
+CORE, XBIT, YBIT = 1, 2, 4
+
+
+def flip(bit, count):
+    return [(s, s ^ bit) for s in range(count)]
+
+
+def norm_kernel(states_ref, keep_ref, send_ref):
+    me = lax.axis_index("store")
+    width = states_ref.shape[1]
+    depth = width // 8
+    total = jnp.zeros((states_ref.shape[0], 1), F32)
+    for s in range(8):
+        part = states_ref[:, s * depth : (s + 1) * depth].astype(F32)
+        total += jnp.sum(part * part, axis=1, keepdims=True)
+    scale = lax.rsqrt(total / width + 1e-05)
+    for r in range(4):
+        for core, out in ((0, keep_ref), (1, send_ref)):
+            s = lax.bitwise_xor(me, r * 2 + core)
+            part = states_ref[:, pl.ds(pl.multiple_of(s * depth, depth), depth)].astype(F32)
+            out[:, r * depth : (r + 1) * depth] = (part * scale).astype(BF16)
+
+
+def norm_split(states):
+    rows, width = states.shape
+    half = jax.ShapeDtypeStruct((rows, width // 2), BF16)
+    return pl.pallas_call(
+        norm_kernel,
+        out_shape=(half, half),
+        compiler_params=pltpu.CompilerParams(vmem_limit_bytes=16 << 20),
+        name="norm_split",
+    )(states)
+
+
+def project_kernel(count, rows, depth, *refs):
+    n_a = 2 * (2 * count - 1)
+    a_refs = refs[:n_a]
+    w_own, w_x, w_y, w_dx, w_dy = refs[n_a : n_a + 5]
+    out_own, out_sib, a_buf, sems = refs[n_a + 5 :]
+    me = lax.axis_index("ctx")
+
+    def copies(act):
+        index = 0
+        for side in range(2):
+            for step in range(count):
+                for sign in (-1, 1):
+                    if step == 0 and sign == 1:
+                        continue
+                    source = a_refs[index]
+                    sem = sems.at[index]
+                    index += 1
+                    shard = me + sign * step
+                    ok = (shard >= 0) & (shard < count)
+
+                    @pl.when(ok)
+                    def _():
+                        start = pl.multiple_of(side * count * rows + shard * rows, rows)
+                        act(pltpu.make_async_copy(source, a_buf.at[pl.ds(start, rows)], sem))
+
+    copies(lambda c: c.start())
+    copies(lambda c: c.wait())
+    total = jnp.dot(a_buf[:, :depth], w_own[...], preferred_element_type=F32)
+    total += jnp.dot(a_buf[:, depth : 2 * depth], w_x[...], preferred_element_type=F32)
+    total += jnp.dot(a_buf[:, 2 * depth : 3 * depth], w_y[...], preferred_element_type=F32)
+    h = depth // 2
+    total += jnp.dot(a_buf[:, 3 * depth : 3 * depth + h], w_dx[...], preferred_element_type=F32)
+    total += jnp.dot(a_buf[:, 3 * depth + h :], w_dy[...], preferred_element_type=F32)
+    half = total.shape[0] // 2
+    out_own[...] = total[:half]
+    out_sib[...] = total[half:]
+
+
+def project(a_parts, w_own, w_x, w_y, w_dx, w_dy, chunk, cols):
+    count = (len(a_parts) // 2 + 1) // 2
+    rows, width = a_parts[0].shape
+    depth = w_own.shape[0]
+    anyspec = pl.BlockSpec(memory_space=pl.ANY)
+    wspec = pl.BlockSpec((depth, cols), lambda i: (0, chunk))
+    dspec = pl.BlockSpec((depth // 2, cols), lambda i: (0, 0))
+    out = jax.ShapeDtypeStruct((count * rows, cols), F32)
+    ospec = pl.BlockSpec((count * rows, cols), lambda i: (0, 0))
+    return pl.pallas_call(
+        functools.partial(project_kernel, count, rows, depth),
+        grid=(1,),
+        in_specs=[anyspec] * len(a_parts) + [wspec] * 3 + [dspec] * 2,
+        out_specs=(ospec, ospec),
+        out_shape=(out, out),
+        scratch_shapes=[
+            pltpu.VMEM((2 * count * rows, width), BF16),
+            pltpu.SemaphoreType.DMA((len(a_parts),)),
+        ],
+        compiler_params=pltpu.CompilerParams(vmem_limit_bytes=40 << 20),
+        cost_estimate=pl.CostEstimate(
+            flops=4 * count * rows * width * cols,
+            bytes_accessed=4 * count * rows * width + 2 * width * cols,
+            transcendentals=0,
+        ),
+        name="project",
+    )(*a_parts, w_own, w_x, w_y, w_dx, w_dy)
+
+
+def turn(values, cosine, sine):
+    return values * cosine + pltpu.roll(values, HD // 2, 1) * sine
+
+
+def assemble_kernel(own_ref, sib_ref, cached_ref, cos_ref, sin_ref, target_ref, key_ref, value_ref):
+    fresh = (own_ref[...] + sib_ref[...]).astype(BF16)
+    fresh_key = turn(fresh[:, :HD].astype(F32), cos_ref[...], sin_ref[...]).astype(BF16)
+    context = cached_ref.shape[0]
+    count = fresh.shape[0]
+    hit = lax.broadcasted_iota(jnp.int32, (context, count), 0) == target_ref[...]
+    pick = jnp.where(hit, 1.0, 0.0)
+    taken = jnp.max(pick, axis=1, keepdims=True) > 0.5
+    pick = pick.astype(BF16)
+    key_new = jnp.dot(pick, fresh_key, preferred_element_type=F32).astype(BF16)
+    value_new = jnp.dot(pick, fresh[:, HD:], preferred_element_type=F32).astype(BF16)
+    key_ref[...] = jnp.where(taken, key_new, cached_ref[:, :HD])
+    value_ref[...] = jnp.where(taken, value_new, cached_ref[:, HD:])
+
+
+def assemble(own, sib, cached, cosine, sine, targets):
+    out = jax.ShapeDtypeStruct((cached.shape[0], HD), BF16)
+    return pl.pallas_call(
+        assemble_kernel,
+        out_shape=(out, out),
+        compiler_params=pltpu.CompilerParams(vmem_limit_bytes=16 << 20),
+        name="assemble",
+    )(own, sib, cached, cosine, sine, targets)
+
+
+def attend_kernel(shard_rows, piece_rows, block_len, heads, *refs):
+    own_ref, sib_ref, key_ref, value_ref, cos_ref, sin_ref, pos_ref, *rest = refs
+    out_ref = rest[-1]
+    row = lax.broadcasted_iota(jnp.int32, (1, key_ref.shape[0]), 1)
+    key_pos = (
+        row % shard_rows // piece_rows * block_len
+        + row // shard_rows * piece_rows
+        + row % piece_rows
+    )
+    visible = key_pos <= pos_ref[...]
+    for h in range(heads):
+        cols = slice(h * HD, (h + 1) * HD)
+        raw = own_ref[:, cols] + sib_ref[:, cols]
+        query = (turn(raw, cos_ref[...], sin_ref[...]) * HD ** (-0.5)).astype(BF16)
+        scores = lax.dot_general(
+            query, key_ref[...], (((1,), (1,)), ((), ())), preferred_element_type=F32
+        )
+        scores = jnp.where(visible, scores, -1e30)
+        exponent = jnp.exp(scores - jnp.max(scores, axis=1, keepdims=True))
+        weights = (exponent / jnp.sum(exponent, axis=1, keepdims=True)).astype(BF16)
+        out_ref[:, cols] = jnp.dot(weights, value_ref[...], preferred_element_type=F32).astype(BF16)
+
+
+def attend(own, sib, key_rows, value_rows, cosine, sine, pos_col, layout, chunk, width, before):
+    rec_count, cols = own.shape
+    whole = lambda a: pl.BlockSpec(a.shape, lambda i: (0, 0))
+    args = [own, sib, key_rows, value_rows, cosine, sine, pos_col]
+    specs = [whole(a) for a in args]
+    aliases = {}
+    if before is not None:
+        aliases = {len(args): 0}
+        args.append(before)
+        specs.append(pl.BlockSpec(memory_space=pl.ANY))
+    return pl.pallas_call(
+        functools.partial(attend_kernel, *layout, cols // HD),
+        grid=(1,),
+        in_specs=specs,
+        out_specs=pl.BlockSpec((rec_count, cols), lambda i: (0, chunk)),
+        out_shape=jax.ShapeDtypeStruct((rec_count, width), BF16),
+        input_output_aliases=aliases,
+        compiler_params=pltpu.CompilerParams(vmem_limit_bytes=32 << 20),
+        name="attend",
+    )(*args)
+
+
+def fast_body(store_kv, block_slot, block_owner, rec_pos, states, w_query, w_keyval):
+    store_count = lax.axis_size("store")
+    ctx_count = lax.axis_size("ctx")
+    my_index = lax.axis_index("ctx")
+    piece_rows = store_kv.shape[1]
+    block_count = block_slot.shape[1]
+    rec_count = rec_pos.shape[1]
+    query_cols = w_query.shape[1]
+    depth = w_query.shape[0]
+    positions = rec_pos[0]
+    xf, yf, cf = (flip(b, store_count) for b in (XBIT, YBIT, CORE))
+    by_x = lambda a: lax.ppermute(a, "store", xf)
+    by_y = lambda a: lax.ppermute(a, "store", yf)
+    by_core = lambda a: lax.ppermute(a, "store", cf)
+
+    wq_x = by_x(w_query)
+    wq_y = by_y(w_query)
+
+    low, high = w_keyval[:, :HD], w_keyval[:, HD:]
+    first = lax.ppermute(jnp.where(my_index == 0, high, low), "ctx", [(0, 1), (1, 2), (2, 0)])
+    second = lax.ppermute(jnp.where(my_index == 3, low, high), "ctx", [(1, 3), (2, 1), (3, 2)])
+    key_w = jnp.where(my_index == 0, low, jnp.where(my_index == 3, second, first))
+    value_w = jnp.where(my_index == 0, first, jnp.where(my_index == 3, high, second))
+    wkv = jnp.concatenate((key_w, value_w), axis=1)
+
+    keep, send = norm_split(states[0])
+    other = by_core(send)
+    a_parts = []
+    for shard in (keep, other):
+        ups, downs = [shard], [shard]
+        for step in range(1, ctx_count):
+            ups.append(
+                lax.ppermute(ups[-1], "ctx", [(i, i + 1) for i in range(step - 1, ctx_count - 1)])
+            )
+            downs.append(
+                lax.ppermute(downs[-1], "ctx", [(i, i - 1) for i in range(1, ctx_count - step + 1)])
+            )
+        a_parts.append(ups[0])
+        for step in range(1, ctx_count):
+            a_parts += [ups[step], downs[step]]
+
+    wkv_x = by_x(wkv)
+    wkv_y = by_y(wkv)
+
+    local_rows = fetch_blocks(store_kv, block_slot[0], block_owner[0])
+    shard_rows = block_count * piece_rows
+    by_head = jnp.stack(
+        [
+            jnp.concatenate(
+                (
+                    local_rows[:, h * HD : (h + 1) * HD],
+                    local_rows[:, (KVH + h) * HD : (KVH + h + 1) * HD],
+                ),
+                axis=1,
+            )
+            for h in range(ctx_count)
+        ]
+    )
+    cached = lax.all_to_all(by_head, "ctx", split_axis=0, concat_axis=0, tiled=True)
+    cached = cached.reshape(ctx_count * shard_rows, 2 * HD)
+
+    frequency = jnp.exp(
+        jnp.arange(HD // 2, dtype=F32) * (-2.0 * math.log(500000.0) / HD)
+    )
+    angles = positions.astype(F32)[:, None] * frequency[None, :]
+    cos_half, sin_half = jnp.cos(angles), jnp.sin(angles)
+    cosine = jnp.concatenate((cos_half, cos_half), axis=1)
+    sine = jnp.concatenate((-sin_half, sin_half), axis=1)
+    block_len = piece_rows * ctx_count
+    targets = (
+        positions % block_len // piece_rows * shard_rows
+        + positions // block_len * piece_rows
+        + positions % piece_rows
+    )
+
+    half = depth // 2
+    chunk_cols = 2 * HD
+
+    def diagonal(from_x, from_y, chunk):
+        cols = slice(chunk * chunk_cols, (chunk + 1) * chunk_cols)
+        return by_x(from_y[:half, cols]), by_y(from_x[half:, cols])
+
+    own, sib = project(a_parts, wkv, wkv_x, wkv_y, *diagonal(wkv_x, wkv_y, 0), 0, chunk_cols)
+    key_rows, value_rows = assemble(
+        own, by_core(sib), cached, cosine, sine, targets.reshape(1, rec_count)
+    )
+    result = None
+    for chunk in range(query_cols // chunk_cols):
+        own, sib = project(
+            a_parts, w_query, wq_x, wq_y, *diagonal(wq_x, wq_y, chunk), chunk, chunk_cols
+        )
+        result = attend(
+            own,
+            by_core(sib),
+            key_rows,
+            value_rows,
+            cosine,
+            sine,
+            positions.reshape(rec_count, 1),
+            (shard_rows, piece_rows, block_len),
+            chunk,
+            query_cols,
+            result,
+        )
+    return result.reshape(1, rec_count, query_cols)
+
+
 def solution(mesh):
+    fast = mesh.shape["store"] == 8 and mesh.shape["ctx"] == KVH
     return jax.shard_map(
-        body,
+        fast_body if fast else general_body,
         mesh=mesh,
         in_specs=(
             P("store", "ctx", None),

time: 292 us -> 202 us (0.69)
  waiting for transfers between devices: 219 us -> 72.6 us
  starting transfers between devices: 8.75 us -> 61.2 us
  Pallas kernels: 0 us -> 35.7 us
  local copies, waits for them, and re-layouts: 7.27 us -> 26.3 us
  blocking collectives: 16.1 us -> 0 us
  matrix products: 15.3 us -> 0 us
  between operations: 13.3 us -> 0.59 us
  other arithmetic: 11.7 us -> 3.1 us
    all_gather x4 -> x0, waiting for transfers between devices: 208 us -> none  [the longest x1 80.9 us: body(): row_piece = lax.all_gather(normed, 'ctx', axis=0, tiled=True)]
    ppermute x0 -> x34, waiting for transfers between devices: none -> 71.6 us  [the longest x7 37.4 us: fast_body(): by_x = lambda a: lax.ppermute(a, 'store', xf)]
    ppermute x0 -> x34, starting transfers between devices: none -> 50.5 us  [the longest x6 13.8 us: fast_body(): lax.ppermute(ups[-1], 'ctx', [(i, i + 1) for i in range(step - 1, ctx_cou...]
    pallas_call x0 -> x11, Pallas kernels: none -> 35.7 us  [the longest x5 24 us: project(): pl.pallas_call(functools.partial(project_kernel, count, rows, depth), gri...]
    unnamed x5 -> x80, local copies, waits for them, and re-layouts: 0.21 us -> 17.8 us
    all_gather x1 -> x0, blocking collectives: 16.1 us -> none  [body(): lax.all_gather(keyval_raw.astype(jnp.bfloat16), 'ctx', axis=1, tiled=True)]
    dot_general x4 -> x0, matrix products: 15.3 us -> none  [the longest x1 9.32 us: body(): jnp.dot(row_piece, query_weight, preferred_element_type=jnp.float32)]
    all_to_all x2 -> x3, waiting for transfers between devices: 9.17 us -> 0.99 us  [the longest x1 0.99 us: fetch_blocks(): lax.all_to_all(store_kv[lax.all_to_all(wanted, 'store', split_axis=0, con...]
  transfers between devices with their start and end apart: 6 -> 37, of which waited for: 6 -> 8; matrix products, arithmetic and copies ran while one was open for 5% -> 5% of each run, Pallas kernels for 0% -> 17%
where the time goes in v1:
time: 202 us; the launch traced here: 200 us
  waiting for transfers between devices  72.6 us (36%)
  starting transfers between devices  61.2 us (30%)
  Pallas kernels  35.7 us (18%)
  local copies, waits for them, and re-layouts  26.3 us (13%)
  other arithmetic  3.1 us (2%)
    ppermute x7, waiting for transfers between devices, fast_body(): by_x = lambda a: lax.ppermute(a, 'store', xf)  37.4 us
    pallas_call x5, Pallas kernels, project(): pl.pallas_call(functools.partial(project_kernel, count, rows, depth), gri...  24 us
    ppermute x6, waiting for transfers between devices, fast_body(): lax.ppermute(downs[-1], 'ctx', [(i, i - 1) for i in range(1, ctx_count -...  22.7 us
    unnamed x80, local copies, waits for them, and re-layouts  17.8 us
    ppermute x6, starting transfers between devices, fast_body(): lax.ppermute(ups[-1], 'ctx', [(i, i + 1) for i in range(step - 1, ctx_cou...  13.8 us
    pallas_call x4, Pallas kernels, attend(): pl.pallas_call(functools.partial(attend_kernel, *layout, cols // HD), gri...  9.94 us
    ppermute x7, starting transfers between devices, fast_body(): by_x = lambda a: lax.ppermute(a, 'store', xf)  9.2 us
    ppermute x7, starting transfers between devices, fast_body(): by_y = lambda a: lax.ppermute(a, 'store', yf)  9.07 us
  transfers between devices with their start and end apart: 37, of which 8 were waited for; matrix products, arithmetic and copies ran while one was open for 5% of the time, Pallas kernels for 17%

profile of v1, /device:TPU:0, one launch (start us, length us, event | category | flops | bytes accessed | tf_op | source)
XLA Modules:
  0.0 199.5 jit_solution(3069088169376295600)
XLA Ops:
  0.0 1.2 broadcast_select_fusion
  1.9 8.8 %collective-permute-start.19 = (bf16[1024,128]{1,0:T(8,128)(2,1)S(1)}, bf16[1024,128]{1,0:T(8,128)(2,1)S(1)}, u32[]{:S(2)}, u32[]{:S(2)}) collective-permute-start(bf16[1024,128]{1,0:T(8,128)(2,1)S(1)} %get-tuple-element.44), channel_id=1, source_target_pairs={{0,1},{1,2},{2,0},{4,5},{5,6},{6,4},{8,9},{9,10},{10,8},{12,13},{1... | collective-permute-start | bytes 786440 | tf_op jit(solution)/shard_map/ppermute | solution.py:319
  10.6 1.2 copy-done.21
  12.4 6.8 %collective-permute-done.19 = bf16[1024,128]{1,0:T(8,128)(2,1)S(1)} collective-permute-done((bf16[1024,128]{1,0:T(8,128)(2,1)S(1)}, bf16[1024,128]{1,0:T(8,128)(2,1)S(1)}, u32[]{:S(2)}, u32[]{:S(2)}) %collective-permute-start.19) | collective-permute-done | bytes 262176 | tf_op jit(solution)/shard_map/ppermute | solution.py:319
  19.3 1.6 collective-permute-start.21
  20.9 1.5 collective-permute-start.20
  22.9 1.3 collective-permute-start.1
  24.2 5.4 %collective-permute-start = (bf16[64,4096]{1,0:T(8,128)(2,1)S(1)}, bf16[64,4096]{1,0:T(8,128)(2,1)}, u32[]{:S(2)}, u32[]{:S(2)}) collective-permute-start(bf16[64,4096]{1,0:T(8,128)(2,1)S(1)} %get-tuple-element.19.refs_0_), channel_id=1, source_target_pairs={{0,1},{1,2},{2,3},{4,5},{5,6},{6,7},{8,9},{9,10},{10,11},{12,13},{... | collective-permute-start | bytes 1572872 | tf_op jit(solution)/shard_map/ppermute | solution.py:332
  29.6 4.7 %collective-permute-done.21.refs_16_ = bf16[1024,256]{1,0:T(8,128)(2,1)S(1)} collective-permute-done((bf16[1024,256]{1,0:T(8,128)(2,1)S(1)}, bf16[1024,256]{1,0:T(8,128)(2,1)S(1)}, u32[]{:S(2)}, u32[]{:S(2)}) %collective-permute-start.21) | collective-permute-done | bytes 524320 | tf_op jit(solution)/shard_map/ppermute | solution.py:312
  34.3 1.5 collective-permute-start.13
  36.7 0.9 copy-done.17
  38.8 0.8 copy-done.19
  39.6 1.6 collective-permute-start.23
  42.0 3.3 %all-to-all-start = ((s32[8,1,2]{2,1,0:T(1,128)}), s32[8,1,2]{2,1,0:T(1,128)S(1)}, u32[]{:S(2)}, u32[]{:S(2)}) async-start(s32[8,1,2]{2,1,0:T(1,128)} %copy.24), calls=%async_computation | async-start | bytes 8192 | tf_op jit(solution)/shard_map/all_to_all | solution.py:54
  45.3 1.3 collective-permute-start.8
  46.6 37.4 %collective-permute-done.22.refs_17_ = bf16[512,256]{1,0:T(8,128)(2,1)S(1)} collective-permute-done((bf16[512,256]{1,0:T(8,128)(2,1)}, bf16[512,256]{1,0:T(8,128)(2,1)S(1)}, u32[]{:S(2)}, u32[]{:S(2)}) %collective-permute-start.22) | collective-permute-done | bytes 262176 | tf_op jit(solution)/shard_map/ppermute | solution.py:311
  84.0 3.4 %collective-permute-start.7 = (bf16[64,4096]{1,0:T(8,128)(2,1)}, bf16[64,4096]{1,0:T(8,128)(2,1)}, u32[]{:S(2)}, u32[]{:S(2)}) collective-permute-start(bf16[64,4096]{1,0:T(8,128)(2,1)} %copy-done.1), channel_id=1, source_target_pairs={{0,1},{1,2},{2,3},{4,5},{5,6},{6,7},{8,9},{9,10},{10,11},{12,13},{... | collective-permute-start | bytes 1572872 | tf_op jit(solution)/shard_map/ppermute | solution.py:332
  87.4 1.3 collective-permute-start.3
  89.0 1.3 gather_fusion
  90.3 4.0 %all-to-all-start.1 = ((bf16[8,2,8,1024]{3,2,1,0:T(8,128)(2,1)}), bf16[8,2,8,1024]{3,2,1,0:T(8,128)(2,1)}, u32[]{:S(2)}, u32[]{:S(2)}) async-start(bf16[8,2,8,1024]{3,2,1,0:T(8,128)(2,1)} %bitcast.34), calls=%async_computation.1 | async-start | bytes 524288 | tf_op jit(solution)/shard_map/all_to_all | solution.py:53
  94.3 1.5 collective-permute-start.2
  95.8 1.3 collective-permute-start.10
  97.3 1.5 collective-permute-done.3.refs_4_
  98.8 1.5 collective-permute-start.9
  100.3 1.0 all-to-all-done.1
  101.2 1.5 gather_fusion.1
  102.8 1.3 collective-permute-start.5
  104.1 13.0 %collective-permute-done.10.refs_11_ = bf16[64,4096]{1,0:T(8,128)(2,1)} collective-permute-done((bf16[64,4096]{1,0:T(8,128)(2,1)}, bf16[64,4096]{1,0:T(8,128)(2,1)}, u32[]{:S(2)}, u32[]{:S(2)}) %collective-permute-start.10) | collective-permute-done | bytes 524320 | tf_op jit(solution)/shard_map/ppermute | solution.py:335
  117.8 1.3 collective-permute-start.12
  119.2 1.5 collective-permute-start.11
  120.6 2.2 %fusion.5 = (bf16[512,256]{1,0:T(8,128)(2,1)}, bf16[512,256]{1,0:T(8,128)(2,1)}, bf16[512,256]{1,0:T(8,128)(2,1)}, bf16[512,256]{1,0:T(8,128)(2,1)}) fusion(bf16[1024,1024]{1,0:T(8,128)(2,1)} %collective-permute-done.14.refs_16_), kind=kLoop, calls=%fused_computation.43 | loop fusion | bytes 2097152 | tf_op jit(solution)/shard_map/slice | solution.py:380
  122.8 1.9 collective-permute-start.31
  124.7 1.0 fusion.4
  125.7 2.5 %collective-permute-done.5.refs_6_ = bf16[64,4096]{1,0:T(8,128)(2,1)S(1)} collective-permute-done((bf16[64,4096]{1,0:T(8,128)(2,1)}, bf16[64,4096]{1,0:T(8,128)(2,1)S(1)}, u32[]{:S(2)}, u32[]{:S(2)}) %collective-permute-start.5) | collective-permute-done | bytes 524320 | tf_op jit(solution)/shard_map/ppermute | solution.py:335
  128.2 0.8 copy-done.6
  129.0 1.9 collective-permute-start.28
  130.9 0.8 copy-done.9
  131.8 1.5 collective-permute-start.32
  133.3 5.6 %collective-permute-done.12.refs_13_ = bf16[64,4096]{1,0:T(8,128)(2,1)S(1)} collective-permute-done((bf16[64,4096]{1,0:T(8,128)(2,1)}, bf16[64,4096]{1,0:T(8,128)(2,1)S(1)}, u32[]{:S(2)}, u32[]{:S(2)}) %collective-permute-start.12) | collective-permute-done | bytes 524320 | tf_op jit(solution)/shard_map/ppermute | solution.py:335
  138.9 0.8 copy-done.12
  139.7 1.7 collective-permute-start.29
  142.1 3.4 %all-to-all-start.2 = ((bf16[4,128,256]{2,1,0:T(8,128)(2,1)}), bf16[4,128,256]{2,1,0:T(8,128)(2,1)S(1)}, u32[]{:S(2)}, u32[]{:S(2)}) async-start(bf16[4,128,256]{2,1,0:T(8,128)(2,1)} %pad_maximum_fusion.1), calls=%async_computation.2 | async-start | bytes 524288 | tf_op jit(solution)/shard_map/all_to_all | solution.py:358
  145.6 1.5 collective-permute-start.25
  147.6 1.0 copy-done.2
  148.7 1.0 copy-done.5
  149.7 1.0 copy-done.7
  150.8 1.0 copy-done.10
  151.8 1.0 copy-done.13
  152.8 1.0 copy-done.16
  153.9 1.0 copy-done.18
  154.9 1.0 copy-done.20
  156.0 0.9 copy-done.23
  157.0 4.7 %project.6 = (f32[256,256]{1,0:T(8,128)S(1)}, f32[256,256]{1,0:T(8,128)}) custom-call(bf16[64,4096]{1,0:T(8,128)(2,1)S(1)} %get-tuple-element.19.refs_0_, bf16[64,4096]{1,0:T(8,128)(2,1)} %collective-permute-done.refs_1_, bf16[64,4096]{1,0:T(8,128)(2,1)S(1)} %copy-done.5, bf16[64,4096]{1,0:T(8,128)(2,1)} %collective-permute-done.2.refs_3_, ...), custom_call_target="tpu_custom_call" | custom-call | flops 1073741824 | bytes 6291456 | tf_op jit(solution)/shard_map/project/pallas_call | solution.py:206
  162.7 1.7 collective-permute-start.16
  164.4 4.9 %project.9 = (f32[256,256]{1,0:T(8,128)S(1)}, f32[256,256]{1,0:T(8,128)}) custom-call(bf16[64,4096]{1,0:T(8,128)(2,1)S(1)} %get-tuple-element.19.refs_0_, bf16[64,4096]{1,0:T(8,128)(2,1)} %collective-permute-done.refs_1_, bf16[64,4096]{1,0:T(8,128)(2,1)S(1)} %copy-done.5, bf16[64,4096]{1,0:T(8,128)(2,1)} %collective-permute-done.2.refs_3_, ...), custom_call_target="tpu_custom_call" | custom-call | flops 1073741824 | bytes 6291456 | tf_op jit(solution)/shard_map/project/pallas_call | solution.py:206
  170.1 4.9 %project.8 = (f32[256,256]{1,0:T(8,128)S(1)}, f32[256,256]{1,0:T(8,128)}) custom-call(bf16[64,4096]{1,0:T(8,128)(2,1)S(1)} %get-tuple-element.19.refs_0_, bf16[64,4096]{1,0:T(8,128)(2,1)} %collective-permute-done.refs_1_, bf16[64,4096]{1,0:T(8,128)(2,1)S(1)} %copy-done.5, bf16[64,4096]{1,0:T(8,128)(2,1)} %collective-permute-done.2.refs_3_, ...), custom_call_target="tpu_custom_call" | custom-call | flops 1073741824 | bytes 6291456 | tf_op jit(solution)/shard_map/project/pallas_call | solution.py:206
  176.3 4.8 %project.7 = (f32[256,256]{1,0:T(8,128)S(1)}, f32[256,256]{1,0:T(8,128)}) custom-call(bf16[64,4096]{1,0:T(8,128)(2,1)S(1)} %get-tuple-element.19.refs_0_, bf16[64,4096]{1,0:T(8,128)(2,1)} %collective-permute-done.refs_1_, bf16[64,4096]{1,0:T(8,128)(2,1)S(1)} %copy-done.5, bf16[64,4096]{1,0:T(8,128)(2,1)} %collective-permute-done.2.refs_3_, ...), custom_call_target="tpu_custom_call" | custom-call | flops 1073741824 | bytes 6291456 | tf_op jit(solution)/shard_map/project/pallas_call | solution.py:206
  181.6 4.8 %project.5 = (f32[256,256]{1,0:T(8,128)S(1)}, f32[256,256]{1,0:T(8,128)}) custom-call(bf16[64,4096]{1,0:T(8,128)(2,1)S(1)} %get-tuple-element.19.refs_0_, bf16[64,4096]{1,0:T(8,128)(2,1)} %collective-permute-done.refs_1_, bf16[64,4096]{1,0:T(8,128)(2,1)S(1)} %copy-done.5, bf16[64,4096]{1,0:T(8,128)(2,1)} %collective-permute-done.2.refs_3_, ...), custom_call_target="tpu_custom_call" | custom-call | flops 1073741824 | bytes 6291456 | tf_op jit(solution)/shard_map/project/pallas_call | solution.py:206
  187.3 0.9 copy-done.25
  188.2 1.3 assemble.1
  189.6 2.7 %attend.4.refs_7_ = bf16[256,1024]{1,0:T(8,128)(2,1)} custom-call(f32[256,256]{1,0:T(8,128)S(1)} %copy-done.33, f32[256,256]{1,0:T(8,128)} %collective-permute-done.33.refs_1_, bf16[512,128]{1,0:T(8,128)(2,1)S(1)} %get-tuple-element.25.refs_2_, bf16[512,128]{1,0:T(8,128)(2,1)S(1)} %get-tuple-element.26.refs_3_, ...), custom_call_target="tpu_custom_call" | custom-call | tf_op jit(solution)/shard_map/attend/pallas_call | solution.py:288
  192.3 2.7 %attend.5.refs_7_ = bf16[256,1024]{1,0:T(8,128)(2,1)} custom-call(f32[256,256]{1,0:T(8,128)S(1)} %copy-done.27, f32[256,256]{1,0:T(8,128)} %collective-permute-done.30.refs_1_, bf16[512,128]{1,0:T(8,128)(2,1)S(1)} %get-tuple-element.25.refs_2_, bf16[512,128]{1,0:T(8,128)(2,1)S(1)} %get-tuple-element.26.refs_3_, ...), custom_call_target="tpu_custom_call", output_to_operand_aliasing={{}: (7, {})} | custom-call | tf_op jit(solution)/shard_map/attend/pallas_call | solution.py:288
  195.1 2.7 %attend.6.refs_7_ = bf16[256,1024]{1,0:T(8,128)(2,1)} custom-call(f32[256,256]{1,0:T(8,128)S(1)} %copy-done.29, f32[256,256]{1,0:T(8,128)} %collective-permute-done.27.refs_1_, bf16[512,128]{1,0:T(8,128)(2,1)S(1)} %get-tuple-element.25.refs_2_, bf16[512,128]{1,0:T(8,128)(2,1)S(1)} %get-tuple-element.26.refs_3_, ...), custom_call_target="tpu_custom_call", output_to_operand_aliasing={{}: (7, {})} | custom-call | tf_op jit(solution)/shard_map/attend/pallas_call | solution.py:288
  197.8 1.8 attend.7
  (131 shorter events, 11.9 us)
Async XLA Ops:
  0.0 89.0 %copy-start = (bf16[32,8,1024]{2,1,0:T(8,128)(2,1)S(1)}, bf16[32,8,1024]{2,1,0:T(8,128)(2,1)}, u32[]{:S(2)}) copy-start(bf16[32,8,1024]{2,1,0:T(8,128)(2,1)} %param.7) | copy-start | bytes 1572868
  0.0 19.2 %copy-start.34 = (bf16[1024,256]{1,0:T(8,128)(2,1)S(1)}, bf16[1024,256]{1,0:T(8,128)(2,1)}, u32[]{:S(2)}) copy-start(bf16[1024,256]{1,0:T(8,128)(2,1)} %param.13) | copy-start | bytes 1572868
  1.2 34.6 %copy-start.39 = (s32[1,16]{1,0:T(1,128)S(1)}, s32[1,16]{1,0:T(1,128)}, u32[]{:S(2)}) copy-start(s32[1,16]{1,0:T(1,128)} %param.9) | copy-start | bytes 196
  1.2 11.2 %collective-permute-start.18 = (bf16[1024,128]{1,0:T(8,128)(2,1)S(1)}, bf16[1024,128]{1,0:T(8,128)(2,1)S(1)}, u32[]{:S(2)}, u32[]{:S(2)}) collective-permute-start(bf16[1024,128]{1,0:T(8,128)(2,1)S(1)} %get-tuple-element.43), channel_id=1, source_target_pairs={{1,3},{2,1},{3,2},{5,7},{6,5},{7,6},{9,11},{10,9},{11,10},{13,15},... | collective-permute-start | bytes 786440 | tf_op jit(solution)/shard_map/ppermute | solution.py:320
  1.9 17.3 %collective-permute-start.19 = (bf16[1024,128]{1,0:T(8,128)(2,1)S(1)}, bf16[1024,128]{1,0:T(8,128)(2,1)S(1)}, u32[]{:S(2)}, u32[]{:S(2)}) collective-permute-start(bf16[1024,128]{1,0:T(8,128)(2,1)S(1)} %get-tuple-element.44), channel_id=1, source_target_pairs={{0,1},{1,2},{2,0},{4,5},{5,6},{6,4},{8,9},{9,10},{10,8},{12,13},{1... | collective-permute-start | bytes 786440 | tf_op jit(solution)/shard_map/ppermute | solution.py:319
  10.6 1.2 copy-start.21
  12.3 28.9 %copy-start.38 = (s32[1,16]{1,0:T(1,128)S(1)}, s32[1,16]{1,0:T(1,128)}, u32[]{:S(2)}) copy-start(s32[1,16]{1,0:T(1,128)} %param.8) | copy-start | bytes 196
  12.3 84.8 %copy-start.37 = (s32[1,256]{1,0:T(1,128)S(1)}, s32[1,256]{1,0:T(1,128)}, u32[]{:S(2)}) copy-start(s32[1,256]{1,0:T(1,128)} %param.10) | copy-start | bytes 3076
  12.3 11.9 %collective-permute-start.6 = (bf16[64,4096]{1,0:T(8,128)(2,1)S(1)}, bf16[64,4096]{1,0:T(8,128)(2,1)S(1)}, u32[]{:S(2)}, u32[]{:S(2)}) collective-permute-start(bf16[64,4096]{1,0:T(8,128)(2,1)S(1)} %get-tuple-element.20), channel_id=1, source_target_pairs={{0,4},{4,0},{8,12},{12,8},{16,20},{20,16},{24,28},{28,24},{1,5},{5... | collective-permute-start | bytes 1572872 | tf_op jit(solution)/shard_map/ppermute | solution.py:313
  19.3 21.9 %copy-start.15 = (bf16[1024,256]{1,0:T(8,128)(2,1)}, bf16[1024,256]{1,0:T(8,128)(2,1)S(1)}, u32[]{:S(2)}) copy-start(bf16[1024,256]{1,0:T(8,128)(2,1)S(1)} %pad_maximum_fusion.refs_14_) | copy-start | bytes 1572868
  19.3 14.9 %collective-permute-start.21 = (bf16[1024,256]{1,0:T(8,128)(2,1)S(1)}, bf16[1024,256]{1,0:T(8,128)(2,1)S(1)}, u32[]{:S(2)}, u32[]{:S(2)}) collective-permute-start(bf16[1024,256]{1,0:T(8,128)(2,1)S(1)} %pad_maximum_fusion.refs_14_), channel_id=1, source_target_pairs={{0,16},{4,20},{8,24},{12,28},{16,0},{20,4},{24,8},{28,12},{1,17},{... | collective-permute-start | bytes 1572872 | tf_op jit(solution)/shard_map/ppermute | solution.py:312
  20.9 16.6 %collective-permute-start.20 = (bf16[1024,256]{1,0:T(8,128)(2,1)S(1)}, bf16[1024,256]{1,0:T(8,128)(2,1)S(1)}, u32[]{:S(2)}, u32[]{:S(2)}) collective-permute-start(bf16[1024,256]{1,0:T(8,128)(2,1)S(1)} %pad_maximum_fusion.refs_14_), channel_id=1, source_target_pairs={{0,8},{4,12},{8,0},{12,4},{16,24},{20,28},{24,16},{28,20},{1,9},{5... | collective-permute-start | bytes 1572872 | tf_op jit(solution)/shard_map/ppermute | solution.py:311
  22.4 96.7 %collective-permute-start.14 = (bf16[1024,1024]{1,0:T(8,128)(2,1)}, bf16[1024,1024]{1,0:T(8,128)(2,1)}, u32[]{:S(2)}, u32[]{:S(2)}) collective-permute-start(bf16[1024,1024]{1,0:T(8,128)(2,1)} %refs_14_.7), channel_id=1, source_target_pairs={{0,16},{4,20},{8,24},{12,28},{16,0},{20,4},{24,8},{28,12},{1,17},{... | collective-permute-start | bytes 6291464 | tf_op jit(solution)/shard_map/ppermute | solution.py:312
  22.9 16.7 %collective-permute-start.1 = (bf16[64,4096]{1,0:T(8,128)(2,1)S(1)}, bf16[64,4096]{1,0:T(8,128)(2,1)S(1)}, u32[]{:S(2)}, u32[]{:S(2)}) collective-permute-start(bf16[64,4096]{1,0:T(8,128)(2,1)S(1)} %get-tuple-element.19.refs_0_), channel_id=1, source_target_pairs={{1,0},{2,1},{3,2},{5,4},{6,5},{7,6},{9,8},{10,9},{11,10},{13,12},{... | collective-permute-start | bytes 1572872 | tf_op jit(solution)/shard_map/ppermute | solution.py:335
  24.2 15.4 %copy-start.1 = (bf16[64,4096]{1,0:T(8,128)(2,1)}, bf16[64,4096]{1,0:T(8,128)(2,1)S(1)}, u32[]{:S(2)}) copy-start(bf16[64,4096]{1,0:T(8,128)(2,1)S(1)} %collective-permute-done.6.refs_7_) | copy-start | bytes 1572868
  24.2 21.1 %collective-permute-start = (bf16[64,4096]{1,0:T(8,128)(2,1)S(1)}, bf16[64,4096]{1,0:T(8,128)(2,1)}, u32[]{:S(2)}, u32[]{:S(2)}) collective-permute-start(bf16[64,4096]{1,0:T(8,128)(2,1)S(1)} %get-tuple-element.19.refs_0_), channel_id=1, source_target_pairs={{0,1},{1,2},{2,3},{4,5},{5,6},{6,7},{8,9},{9,10},{10,11},{12,13},{... | collective-permute-start | bytes 1572872 | tf_op jit(solution)/shard_map/ppermute | solution.py:332
  34.3 88.6 %collective-permute-start.13 = (bf16[1024,1024]{1,0:T(8,128)(2,1)}, bf16[1024,1024]{1,0:T(8,128)(2,1)S(1)}, u32[]{:S(2)}, u32[]{:S(2)}) collective-permute-start(bf16[1024,1024]{1,0:T(8,128)(2,1)} %refs_14_.7), channel_id=1, source_target_pairs={{0,8},{4,12},{8,0},{12,4},{16,24},{20,28},{24,16},{28,20},{1,9},{5... | collective-permute-start | bytes 6291464 | tf_op jit(solution)/shard_map/ppermute | solution.py:311
  37.5 46.5 %collective-permute-start.22 = (bf16[512,256]{1,0:T(8,128)(2,1)}, bf16[512,256]{1,0:T(8,128)(2,1)S(1)}, u32[]{:S(2)}, u32[]{:S(2)}) collective-permute-start(bf16[512,256]{1,0:T(8,128)(2,1)} %slice.86), channel_id=1, source_target_pairs={{0,8},{4,12},{8,0},{12,4},{16,24},{20,28},{24,16},{28,20},{1,9},{5... | collective-permute-start | bytes 786440 | tf_op jit(solution)/shard_map/ppermute | solution.py:311
  39.6 1.6 copy-start.4
  39.6 47.8 %collective-permute-start.23 = (bf16[512,256]{1,0:T(8,128)(2,1)}, bf16[512,256]{1,0:T(8,128)(2,1)}, u32[]{:S(2)}, u32[]{:S(2)}) collective-permute-start(bf16[512,256]{1,0:T(8,128)(2,1)} %slice.87), channel_id=1, source_target_pairs={{0,16},{4,20},{8,24},{12,28},{16,0},{20,4},{24,8},{28,12},{1,17},{... | collective-permute-start | bytes 786440 | tf_op jit(solution)/shard_map/ppermute | solution.py:312
  42.0 46.7 %all-to-all-start = ((s32[8,1,2]{2,1,0:T(1,128)}), s32[8,1,2]{2,1,0:T(1,128)S(1)}, u32[]{:S(2)}, u32[]{:S(2)}) async-start(s32[8,1,2]{2,1,0:T(1,128)} %copy.24), calls=%async_computation | async-start | bytes 8192 | tf_op jit(solution)/shard_map/all_to_all | solution.py:54
  45.3 49.0 %collective-permute-start.8 = (bf16[64,4096]{1,0:T(8,128)(2,1)}, bf16[64,4096]{1,0:T(8,128)(2,1)}, u32[]{:S(2)}, u32[]{:S(2)}) collective-permute-start(bf16[64,4096]{1,0:T(8,128)(2,1)} %copy-done.1), channel_id=1, source_target_pairs={{1,0},{2,1},{3,2},{5,4},{6,5},{7,6},{9,8},{10,9},{11,10},{13,12},{... | collective-permute-start | bytes 1572872 | tf_op jit(solution)/shard_map/ppermute | solution.py:335
  84.0 13.1 %copy-start.22 = (bf16[512,256]{1,0:T(8,128)(2,1)}, bf16[512,256]{1,0:T(8,128)(2,1)S(1)}, u32[]{:S(2)}) copy-start(bf16[512,256]{1,0:T(8,128)(2,1)S(1)} %collective-permute-done.22.refs_17_) | copy-start | bytes 786436
  84.0 11.8 %collective-permute-start.7 = (bf16[64,4096]{1,0:T(8,128)(2,1)}, bf16[64,4096]{1,0:T(8,128)(2,1)}, u32[]{:S(2)}, u32[]{:S(2)}) collective-permute-start(bf16[64,4096]{1,0:T(8,128)(2,1)} %copy-done.1), channel_id=1, source_target_pairs={{0,1},{1,2},{2,3},{4,5},{5,6},{6,7},{8,9},{9,10},{10,11},{12,13},{... | collective-permute-start | bytes 1572872 | tf_op jit(solution)/shard_map/ppermute | solution.py:332
  87.4 11.4 %collective-permute-start.3 = (bf16[64,4096]{1,0:T(8,128)(2,1)}, bf16[64,4096]{1,0:T(8,128)(2,1)}, u32[]{:S(2)}, u32[]{:S(2)}) collective-permute-start(bf16[64,4096]{1,0:T(8,128)(2,1)} %copy-done.4), channel_id=1, source_target_pairs={{1,0},{2,1},{5,4},{6,5},{9,8},{10,9},{13,12},{14,13},{17,16},{18,1... | collective-permute-start | bytes 1572872 | tf_op jit(solution)/shard_map/ppermute | solution.py:335
  90.3 11.0 %all-to-all-start.1 = ((bf16[8,2,8,1024]{3,2,1,0:T(8,128)(2,1)}), bf16[8,2,8,1024]{3,2,1,0:T(8,128)(2,1)}, u32[]{:S(2)}, u32[]{:S(2)}) async-start(bf16[8,2,8,1024]{3,2,1,0:T(8,128)(2,1)} %bitcast.34), calls=%async_computation.1 | async-start | bytes 524288 | tf_op jit(solution)/shard_map/all_to_all | solution.py:53
  94.3 8.5 %collective-permute-start.2 = (bf16[64,4096]{1,0:T(8,128)(2,1)}, bf16[64,4096]{1,0:T(8,128)(2,1)}, u32[]{:S(2)}, u32[]{:S(2)}) collective-permute-start(bf16[64,4096]{1,0:T(8,128)(2,1)} %collective-permute-done.refs_1_), channel_id=1, source_target_pairs={{1,2},{2,3},{5,6},{6,7},{9,10},{10,11},{13,14},{14,15},{17,18},{18... | collective-permute-start | bytes 1572872 | tf_op jit(solution)/shard_map/ppermute | solution.py:332
  95.8 21.3 %collective-permute-start.10 = (bf16[64,4096]{1,0:T(8,128)(2,1)}, bf16[64,4096]{1,0:T(8,128)(2,1)}, u32[]{:S(2)}, u32[]{:S(2)}) collective-permute-start(bf16[64,4096]{1,0:T(8,128)(2,1)} %collective-permute-done.8.refs_9_), channel_id=1, source_target_pairs={{1,0},{2,1},{5,4},{6,5},{9,8},{10,9},{13,12},{14,13},{17,16},{18,1... | collective-permute-start | bytes 1572872 | tf_op jit(solution)/shard_map/ppermute | solution.py:335
  98.8 19.1 %collective-permute-start.9 = (bf16[64,4096]{1,0:T(8,128)(2,1)}, bf16[64,4096]{1,0:T(8,128)(2,1)}, u32[]{:S(2)}, u32[]{:S(2)}) collective-permute-start(bf16[64,4096]{1,0:T(8,128)(2,1)} %collective-permute-done.7.refs_8_), channel_id=1, source_target_pairs={{1,2},{2,3},{5,6},{6,7},{9,10},{10,11},{13,14},{14,15},{17,18},{18... | collective-permute-start | bytes 1572872 | tf_op jit(solution)/shard_map/ppermute | solution.py:332
  102.8 25.4 %collective-permute-start.5 = (bf16[64,4096]{1,0:T(8,128)(2,1)}, bf16[64,4096]{1,0:T(8,128)(2,1)S(1)}, u32[]{:S(2)}, u32[]{:S(2)}) collective-permute-start(bf16[64,4096]{1,0:T(8,128)(2,1)} %collective-permute-done.3.refs_4_), channel_id=1, source_target_pairs={{1,0},{5,4},{9,8},{13,12},{17,16},{21,20},{25,24},{29,28}} | collective-permute-start | bytes 1572872 | tf_op jit(solution)/shard_map/ppermute | solution.py:335
  117.1 13.8 %collective-permute-start.4 = (bf16[64,4096]{1,0:T(8,128)(2,1)}, bf16[64,4096]{1,0:T(8,128)(2,1)S(1)}, u32[]{:S(2)}, u32[]{:S(2)}) collective-permute-start(bf16[64,4096]{1,0:T(8,128)(2,1)} %collective-permute-done.2.refs_3_), channel_id=1, source_target_pairs={{2,3},{6,7},{10,11},{14,15},{18,19},{22,23},{26,27},{30,31}} | collective-permute-start | bytes 1572872 | tf_op jit(solution)/shard_map/ppermute | solution.py:332
  117.8 21.1 %collective-permute-start.12 = (bf16[64,4096]{1,0:T(8,128)(2,1)}, bf16[64,4096]{1,0:T(8,128)(2,1)S(1)}, u32[]{:S(2)}, u32[]{:S(2)}) collective-permute-start(bf16[64,4096]{1,0:T(8,128)(2,1)} %collective-permute-done.10.refs_11_), channel_id=1, source_target_pairs={{1,0},{5,4},{9,8},{13,12},{17,16},{21,20},{25,24},{29,28}} | collective-permute-start | bytes 1572872 | tf_op jit(solution)/shard_map/ppermute | solution.py:335
  119.2 26.4 %collective-permute-start.11 = (bf16[64,4096]{1,0:T(8,128)(2,1)}, bf16[64,4096]{1,0:T(8,128)(2,1)}, u32[]{:S(2)}, u32[]{:S(2)}) collective-permute-start(bf16[64,4096]{1,0:T(8,128)(2,1)} %collective-permute-done.9.refs_10_), channel_id=1, source_target_pairs={{2,3},{6,7},{10,11},{14,15},{18,19},{22,23},{26,27},{30,31}} | collective-permute-start | bytes 1572872 | tf_op jit(solution)/shard_map/ppermute | solution.py:332
  122.8 24.3 %collective-permute-start.31 = (bf16[512,256]{1,0:T(8,128)(2,1)}, bf16[512,256]{1,0:T(8,128)(2,1)}, u32[]{:S(2)}, u32[]{:S(2)}) collective-permute-start(bf16[512,256]{1,0:T(8,128)(2,1)} %get-tuple-element.37), channel_id=1, source_target_pairs={{0,8},{4,12},{8,0},{12,4},{16,24},{20,28},{24,16},{28,20},{1,9},{5... | collective-permute-start | bytes 786440 | tf_op jit(solution)/shard_map/ppermute | solution.py:311
  129.0 33.3 %collective-permute-start.28 = (bf16[512,256]{1,0:T(8,128)(2,1)}, bf16[512,256]{1,0:T(8,128)(2,1)}, u32[]{:S(2)}, u32[]{:S(2)}) collective-permute-start(bf16[512,256]{1,0:T(8,128)(2,1)} %get-tuple-element.38), channel_id=1, source_target_pairs={{0,8},{4,12},{8,0},{12,4},{16,24},{20,28},{24,16},{28,20},{1,9},{5... | collective-permute-start | bytes 786440 | tf_op jit(solution)/shard_map/ppermute | solution.py:311
  131.8 31.0 %collective-permute-start.32 = (bf16[512,256]{1,0:T(8,128)(2,1)}, bf16[512,256]{1,0:T(8,128)(2,1)}, u32[]{:S(2)}, u32[]{:S(2)}) collective-permute-start(bf16[512,256]{1,0:T(8,128)(2,1)} %get-tuple-element.33), channel_id=1, source_target_pairs={{0,16},{4,20},{8,24},{12,28},{16,0},{20,4},{24,8},{28,12},{1,17},{... | collective-permute-start | bytes 786440 | tf_op jit(solution)/shard_map/ppermute | solution.py:312
  139.7 30.4 %collective-permute-start.29 = (bf16[512,256]{1,0:T(8,128)(2,1)}, bf16[512,256]{1,0:T(8,128)(2,1)}, u32[]{:S(2)}, u32[]{:S(2)}) collective-permute-start(bf16[512,256]{1,0:T(8,128)(2,1)} %get-tuple-element.34), channel_id=1, source_target_pairs={{0,16},{4,20},{8,24},{12,28},{16,0},{20,4},{24,8},{28,12},{1,17},{... | collective-permute-start | bytes 786440 | tf_op jit(solution)/shard_map/ppermute | solution.py:312
  142.1 45.1 %all-to-all-start.2 = ((bf16[4,128,256]{2,1,0:T(8,128)(2,1)}), bf16[4,128,256]{2,1,0:T(8,128)(2,1)S(1)}, u32[]{:S(2)}, u32[]{:S(2)}) async-start(bf16[4,128,256]{2,1,0:T(8,128)(2,1)} %pad_maximum_fusion.1), calls=%async_computation.2 | async-start | bytes 524288 | tf_op jit(solution)/shard_map/all_to_all | solution.py:358
  145.6 30.2 %collective-permute-start.25 = (bf16[512,256]{1,0:T(8,128)(2,1)}, bf16[512,256]{1,0:T(8,128)(2,1)S(1)}, u32[]{:S(2)}, u32[]{:S(2)}) collective-permute-start(bf16[512,256]{1,0:T(8,128)(2,1)} %get-tuple-element.39), channel_id=1, source_target_pairs={{0,8},{4,12},{8,0},{12,4},{16,24},{20,28},{24,16},{28,20},{1,9},{5... | collective-permute-start | bytes 786440 | tf_op jit(solution)/shard_map/ppermute | solution.py:311
  147.1 29.1 %collective-permute-start.26 = (bf16[512,256]{1,0:T(8,128)(2,1)}, bf16[512,256]{1,0:T(8,128)(2,1)S(1)}, u32[]{:S(2)}, u32[]{:S(2)}) collective-permute-start(bf16[512,256]{1,0:T(8,128)(2,1)} %get-tuple-element.35), channel_id=1, source_target_pairs={{0,16},{4,20},{8,24},{12,28},{16,0},{20,4},{24,8},{28,12},{1,17},{... | collective-permute-start | bytes 786440 | tf_op jit(solution)/shard_map/ppermute | solution.py:312
  147.6 1.0 copy-start.2
  148.7 1.0 copy-start.5
  149.7 1.0 copy-start.7
  150.8 1.0 copy-start.10
  151.8 1.0 copy-start.13
  152.8 1.0 copy-start.16
  156.9 5.4 %copy-start.35 = (bf16[512,256]{1,0:T(8,128)(2,1)S(1)}, bf16[512,256]{1,0:T(8,128)(2,1)}, u32[]{:S(2)}) copy-start(bf16[512,256]{1,0:T(8,128)(2,1)} %get-tuple-element.40) | copy-start | bytes 786436
  156.9 5.8 %copy-start.36 = (bf16[512,256]{1,0:T(8,128)(2,1)S(1)}, bf16[512,256]{1,0:T(8,128)(2,1)}, u32[]{:S(2)}) copy-start(bf16[512,256]{1,0:T(8,128)(2,1)} %get-tuple-element.36) | copy-start | bytes 786436
  156.9 7.5 %copy-start.3 = (bf16[64,4096]{1,0:T(8,128)(2,1)S(1)}, bf16[64,4096]{1,0:T(8,128)(2,1)}, u32[]{:S(2)}) copy-start(bf16[64,4096]{1,0:T(8,128)(2,1)} %copy-done.1) | copy-start | bytes 1572868
  156.9 7.5 %copy-start.8 = (bf16[64,4096]{1,0:T(8,128)(2,1)S(1)}, bf16[64,4096]{1,0:T(8,128)(2,1)}, u32[]{:S(2)}) copy-start(bf16[64,4096]{1,0:T(8,128)(2,1)} %copy-done.6) | copy-start | bytes 1572868
  156.9 7.5 %copy-start.11 = (bf16[64,4096]{1,0:T(8,128)(2,1)S(1)}, bf16[64,4096]{1,0:T(8,128)(2,1)}, u32[]{:S(2)}) copy-start(bf16[64,4096]{1,0:T(8,128)(2,1)} %copy-done.9) | copy-start | bytes 1572868
  156.9 7.5 %copy-start.14 = (bf16[64,4096]{1,0:T(8,128)(2,1)S(1)}, bf16[64,4096]{1,0:T(8,128)(2,1)}, u32[]{:S(2)}) copy-start(bf16[64,4096]{1,0:T(8,128)(2,1)} %copy-done.12) | copy-start | bytes 1572868
  162.4 18.7 %collective-permute-start.15 = (bf16[512,256]{1,0:T(8,128)(2,1)S(1)}, bf16[512,256]{1,0:T(8,128)(2,1)S(1)}, u32[]{:S(2)}, u32[]{:S(2)}) collective-permute-start(bf16[512,256]{1,0:T(8,128)(2,1)S(1)} %copy-done.35), channel_id=1, source_target_pairs={{0,8},{4,12},{8,0},{12,4},{16,24},{20,28},{24,16},{28,20},{1,9},{5... | collective-permute-start | bytes 786440 | tf_op jit(solution)/shard_map/ppermute | solution.py:311
  162.7 18.9 %collective-permute-start.16 = (bf16[512,256]{1,0:T(8,128)(2,1)S(1)}, bf16[512,256]{1,0:T(8,128)(2,1)S(1)}, u32[]{:S(2)}, u32[]{:S(2)}) collective-permute-start(bf16[512,256]{1,0:T(8,128)(2,1)S(1)} %copy-done.36), channel_id=1, source_target_pairs={{0,16},{4,20},{8,24},{12,28},{16,0},{20,4},{24,8},{28,12},{1,17},{... | collective-permute-start | bytes 786440 | tf_op jit(solution)/shard_map/ppermute | solution.py:312
  170.1 17.2 %collective-permute-start.24 = (f32[256,256]{1,0:T(8,128)}, f32[256,256]{1,0:T(8,128)}, u32[]{:S(2)}, u32[]{:S(2)}) collective-permute-start(f32[256,256]{1,0:T(8,128)} %get-tuple-element.24), channel_id=1, source_target_pairs={{0,4},{4,0},{8,12},{12,8},{16,20},{20,16},{24,28},{28,24},{1,5},{5... | collective-permute-start | bytes 786440 | tf_op jit(solution)/shard_map/ppermute | solution.py:313
  175.7 13.8 %collective-permute-start.33 = (f32[256,256]{1,0:T(8,128)}, f32[256,256]{1,0:T(8,128)}, u32[]{:S(2)}, u32[]{:S(2)}) collective-permute-start(f32[256,256]{1,0:T(8,128)} %get-tuple-element.32), channel_id=1, source_target_pairs={{0,4},{4,0},{8,12},{12,8},{16,20},{20,16},{24,28},{28,24},{1,5},{5... | collective-permute-start | bytes 786440 | tf_op jit(solution)/shard_map/ppermute | solution.py:313
  176.2 16.1 %collective-permute-start.30 = (f32[256,256]{1,0:T(8,128)}, f32[256,256]{1,0:T(8,128)}, u32[]{:S(2)}, u32[]{:S(2)}) collective-permute-start(f32[256,256]{1,0:T(8,128)} %get-tuple-element.30), channel_id=1, source_target_pairs={{0,4},{4,0},{8,12},{12,8},{16,20},{20,16},{24,28},{28,24},{1,5},{5... | collective-permute-start | bytes 786440 | tf_op jit(solution)/shard_map/ppermute | solution.py:313
  181.1 5.3 %copy-start.28 = (f32[256,256]{1,0:T(8,128)}, f32[256,256]{1,0:T(8,128)S(1)}, u32[]{:S(2)}) copy-start(f32[256,256]{1,0:T(8,128)S(1)} %get-tuple-element.27.refs_0_) | copy-start | bytes 786436
  181.1 14.0 %collective-permute-start.27 = (f32[256,256]{1,0:T(8,128)}, f32[256,256]{1,0:T(8,128)}, u32[]{:S(2)}, u32[]{:S(2)}) collective-permute-start(f32[256,256]{1,0:T(8,128)} %get-tuple-element.28), channel_id=1, source_target_pairs={{0,4},{4,0},{8,12},{12,8},{16,20},{20,16},{24,28},{28,24},{1,5},{5... | collective-permute-start | bytes 786440 | tf_op jit(solution)/shard_map/ppermute | solution.py:313
  186.4 3.2 %copy-start.33 = (f32[256,256]{1,0:T(8,128)S(1)}, f32[256,256]{1,0:T(8,128)}, u32[]{:S(2)}) copy-start(f32[256,256]{1,0:T(8,128)} %copy-done.32) | copy-start | bytes 786436
  186.4 5.9 %copy-start.27 = (f32[256,256]{1,0:T(8,128)S(1)}, f32[256,256]{1,0:T(8,128)}, u32[]{:S(2)}) copy-start(f32[256,256]{1,0:T(8,128)} %copy-done.26) | copy-start | bytes 786436
  186.4 11.3 %collective-permute-start.17 = (f32[256,256]{1,0:T(8,128)}, f32[256,256]{1,0:T(8,128)S(1)}, u32[]{:S(2)}, u32[]{:S(2)}) collective-permute-start(f32[256,256]{1,0:T(8,128)} %get-tuple-element.22), channel_id=1, source_target_pairs={{0,4},{4,0},{8,12},{12,8},{16,20},{20,16},{24,28},{28,24},{1,5},{5... | collective-permute-start | bytes 786440 | tf_op jit(solution)/shard_map/ppermute | solution.py:313
  189.5 5.5 %copy-start.29 = (f32[256,256]{1,0:T(8,128)S(1)}, f32[256,256]{1,0:T(8,128)}, u32[]{:S(2)}) copy-start(f32[256,256]{1,0:T(8,128)} %copy-done.28) | copy-start | bytes 786436
  192.3 5.4 %copy-start.31 = (f32[256,256]{1,0:T(8,128)S(1)}, f32[256,256]{1,0:T(8,128)}, u32[]{:S(2)}) copy-start(f32[256,256]{1,0:T(8,128)} %copy-done.30) | copy-start | bytes 786436
  (13 other events, 10.9 us)

commit v2 on v0

--- a/solution.py
+++ b/solution.py
@@ -1,14 +1,19 @@
+import functools
 import math
 
 import jax
 import jax.numpy as jnp
 from jax import lax
+from jax.experimental import pallas as pl
+from jax.experimental.pallas import tpu as pltpu
 from jax.sharding import PartitionSpec as P
 
 QH = 32
 KVH = 4
 HD = 128
 CAP = 2
+F32 = jnp.float32
+BF16 = jnp.bfloat16
 
 
 def rotate(values, positions):
@@ -33,17 +38,8 @@
     ).astype(jnp.bfloat16)
 
 
-def body(store_kv, block_slot, block_owner, rec_pos, states, w_query, w_keyval):
-    store_count = lax.axis_size("store")
-    ctx_count = lax.axis_size("ctx")
-    my_index = lax.axis_index("ctx")
-    piece_rows = store_kv.shape[1]
-    row_width = store_kv.shape[2]
-    block_count = block_slot.shape[1]
-    rec_count = rec_pos.shape[1]
-    slot_ids = block_slot[0]
-    owners = block_owner[0]
-    positions = rec_pos[0]
+def swap_ids(slot_ids, owners, store_count):
+    block_count = slot_ids.shape[0]
     slot_order = jnp.arange(block_count)
     earlier = slot_order[None, :] < slot_order[:, None]
     slot_ranks = jnp.sum((owners[:, None] == owners[None, :]) & earlier, axis=1)
@@ -51,17 +47,26 @@
         slot_ranks[:, None, None] == jnp.arange(CAP)[None, None, :]
     )
     wanted = jnp.sum(jnp.where(slot_hits, slot_ids[:, None, None], 0), axis=0)
-    arrived = lax.all_to_all(
-        store_kv[lax.all_to_all(wanted, "store", split_axis=0, concat_axis=0, tiled=True)],
-        "store",
-        split_axis=0,
-        concat_axis=0,
-        tiled=True,
-    )
+    asked = lax.all_to_all(wanted, "store", split_axis=0, concat_axis=0, tiled=True)
+    return asked, owners * CAP + slot_ranks
+
+
+def fetch_blocks(store_kv, asked, places):
+    arrived = lax.all_to_all(store_kv[asked], "store", split_axis=0, concat_axis=0, tiled=True)
+    return arrived.reshape((-1,) + store_kv.shape[1:])[places].reshape(-1, store_kv.shape[2])
+
+
+def general_body(store_kv, block_slot, block_owner, rec_pos, states, w_query, w_keyval):
+    ctx_count = lax.axis_size("ctx")
+    my_index = lax.axis_index("ctx")
+    piece_rows = store_kv.shape[1]
+    block_count = block_slot.shape[1]
+    rec_count = rec_pos.shape[1]
+    positions = rec_pos[0]
     shard_rows = block_count * piece_rows
-    local_rows = arrived.reshape(store_count * CAP, piece_rows, row_width)[
-        owners * CAP + slot_ranks
-    ].reshape(shard_rows, row_width)
+    local_rows = fetch_blocks(
+        store_kv, *swap_ids(block_slot[0], block_owner[0], lax.axis_size("store"))
+    )
     normed = normalize(states[0])
     query_cols = w_query.shape[1]
     query_weight, keyval_weight = (
@@ -69,15 +74,8 @@
         lax.all_gather(w_keyval, "store", axis=0, tiled=True),
     )
     row_piece = lax.all_gather(normed, "ctx", axis=0, tiled=True)
-    projected = jnp.concatenate(
-        (
-            jnp.dot(row_piece, query_weight, preferred_element_type=jnp.float32),
-            jnp.dot(row_piece, keyval_weight, preferred_element_type=jnp.float32),
-        ),
-        axis=1,
-    )
-    query_raw = projected[:, :query_cols]
-    keyval_raw = projected[:, query_cols:]
+    query_raw = jnp.dot(row_piece, query_weight, preferred_element_type=jnp.float32)
+    keyval_raw = jnp.dot(row_piece, keyval_weight, preferred_element_type=jnp.float32)
     heads_here = query_cols // HD
     group_size = QH // KVH
     queries = (
@@ -120,9 +118,463 @@
     return attended.reshape(1, rec_count, heads_here * HD).astype(jnp.bfloat16)
 
 
+CORE, XBIT, YBIT = 1, 2, 4
+
+
+def flip(bit, count):
+    return [(s, s ^ bit) for s in range(count)]
+
+
+def norm_kernel(states_ref, keep_ref, send_ref):
+    me = lax.axis_index("store")
+    width = states_ref.shape[1]
+    depth = width // 8
+    total = jnp.zeros((states_ref.shape[0], 1), F32)
+    for s in range(8):
+        part = states_ref[:, s * depth : (s + 1) * depth].astype(F32)
+        total += jnp.sum(part * part, axis=1, keepdims=True)
+    scale = lax.rsqrt(total / width + 1e-05)
+    for r in range(4):
+        for core, out in ((0, keep_ref), (1, send_ref)):
+            s = lax.bitwise_xor(me, r * 2 + core)
+            part = states_ref[:, pl.ds(pl.multiple_of(s * depth, depth), depth)].astype(F32)
+            out[:, r * depth : (r + 1) * depth] = (part * scale).astype(BF16)
+
+
+def norm_split(states):
+    rows, width = states.shape
+    half = jax.ShapeDtypeStruct((rows, width // 2), BF16)
+    return pl.pallas_call(
+        norm_kernel,
+        out_shape=(half, half),
+        compiler_params=pltpu.CompilerParams(vmem_limit_bytes=16 << 20),
+        name="norm_split",
+    )(states)
+
+
+def cut_kernel(plan, n_in, *refs):
+    outs, sems = refs[n_in:-1], refs[-1]
+    copies = []
+    for out, pieces in zip(outs, plan):
+        for source, (row, col), (to_row, to_col), (rows, cols) in pieces:
+            copies.append(
+                pltpu.make_async_copy(
+                    refs[source].at[pl.ds(row, rows), pl.ds(col, cols)],
+                    out.at[pl.ds(to_row, rows), pl.ds(to_col, cols)],
+                    sems.at[len(copies)],
+                )
+            )
+    for copy in copies:
+        copy.start()
+    for copy in copies:
+        copy.wait()
+
+
+def cut(sources, plan, shapes, gates=(), near=False):
+    args = [*sources, *jax.tree.leaves(gates)]
+    hbm = pl.BlockSpec(memory_space=pltpu.HBM)
+    vmem = pl.BlockSpec(memory_space=pltpu.VMEM)
+    return pl.pallas_call(
+        functools.partial(cut_kernel, plan, len(args)),
+        in_specs=[vmem if near else hbm] * len(args),
+        out_specs=[hbm if near else vmem] * len(shapes),
+        out_shape=[jax.ShapeDtypeStruct(shape, BF16) for shape in shapes],
+        scratch_shapes=[pltpu.SemaphoreType.DMA((sum(len(p) for p in plan),))],
+        compiler_params=pltpu.CompilerParams(vmem_limit_bytes=8 << 20),
+        name="cut",
+    )(*args)
+
+
+def relay_kernel(own, two, up, down, sems):
+    me = lax.axis_index("ctx")
+
+    def moves(act):
+        for way, out in enumerate((up, down)):
+            for source, chosen in ((own, me == 1 + way), (two, me != 1 + way)):
+
+                @pl.when(chosen)
+                def _():
+                    act(pltpu.make_async_copy(source, out, sems.at[way]))
+
+    moves(lambda c: c.start())
+    moves(lambda c: c.wait())
+
+
+def relay(own, two):
+    hbm = pl.BlockSpec(memory_space=pltpu.HBM)
+    out = jax.ShapeDtypeStruct(own.shape, BF16)
+    return pl.pallas_call(
+        relay_kernel,
+        in_specs=[hbm] * 2,
+        out_shape=(out, out),
+        scratch_shapes=[pltpu.SemaphoreType.DMA((2,))],
+        compiler_params=pltpu.CompilerParams(vmem_limit_bytes=4 << 20),
+        name="relay",
+    )(own, two)
+
+
+def sort_kernel(blocks_ref, places_ref, *refs):
+    out_ref = refs[-1]
+    heads = out_ref.shape[0]
+    size = blocks_ref.shape[1]
+    for j in range(places_ref.shape[0]):
+        block = blocks_ref[places_ref[j]]
+        for h in range(heads):
+            rows = slice(j * size, (j + 1) * size)
+            out_ref[h, rows, :HD] = block[:, h * HD : (h + 1) * HD]
+            out_ref[h, rows, HD:] = block[:, (heads + h) * HD : (heads + h + 1) * HD]
+
+
+def sort_blocks(blocks, places, gates):
+    hbm = pl.BlockSpec(memory_space=pltpu.HBM)
+    count, size, _ = blocks.shape
+    return pl.pallas_call(
+        sort_kernel,
+        in_specs=[pl.BlockSpec(memory_space=pltpu.VMEM), pl.BlockSpec(memory_space=pltpu.SMEM)]
+        + [hbm] * len(gates),
+        out_shape=jax.ShapeDtypeStruct((KVH, places.shape[0] * size, 2 * HD), BF16),
+        compiler_params=pltpu.CompilerParams(vmem_limit_bytes=4 << 20),
+        name="sort_blocks",
+    )(blocks, places, *gates)
+
+
+STEP = 2 * HD
+
+
+def share(total, shards, own, sib, cols):
+    rows = own.shape[0] // shards
+    for z in range(shards):
+        here = slice(z * rows, (z + 1) * rows)
+        own[here, cols] = total[2 * z * rows : (2 * z + 1) * rows]
+        sib[here, cols] = total[(2 * z + 1) * rows : (2 * z + 2) * rows]
+
+
+def project_kernel(shards, slices, chunks, n_weights, started, n_gates, *refs):
+    a_refs, w_refs = refs[:5], refs[5 : 5 + n_weights]
+    refs = refs[5 + n_weights :]
+    before = refs[0] if started else None
+    outs = refs[started + n_gates : -5]
+    a_buf, w_buf, acc, a_sems, w_sems = refs[-5:]
+    me = lax.axis_index("ctx")
+    depth = a_buf.shape[2]
+    rows = a_buf.shape[1] // shards
+
+    def row_copies(index, act):
+        cols = pl.ds(slices[index] * depth, depth)
+        for k in range(4):
+            start = pl.multiple_of(lax.bitwise_xor(me, k) * rows, rows)
+            target = a_buf.at[index, pl.ds(start, rows)]
+            sem = a_sems.at[index * 4 + k]
+            if k < 3:
+                act(pltpu.make_async_copy(a_refs[k].at[:, cols], target, sem))
+            else:
+                for source, chosen in ((a_refs[3], me >= 2), (a_refs[4], me < 2)):
+
+                    @pl.when(chosen)
+                    def _():
+                        act(pltpu.make_async_copy(source.at[:, cols], target, sem))
+
+    weight_copies = {}
+    count = 0
+    for index in range(len(slices)):
+        row_copies(index, lambda c: c.start())
+        for c, (_, pieces) in enumerate(chunks):
+            if index >= len(pieces):
+                continue
+            here, row_to = [], 0
+            for ref, row, col, size in pieces[index]:
+                here.append(
+                    pltpu.make_async_copy(
+                        w_refs[ref].at[pl.ds(row, size), pl.ds(col, STEP)],
+                        w_buf.at[c, index, pl.ds(row_to, size)],
+                        w_sems.at[count],
+                    )
+                )
+                here[-1].start()
+                row_to += size
+                count += 1
+            weight_copies[c, index] = here
+    for index in range(len(slices)):
+        row_copies(index, lambda c: c.wait())
+        for c, (place, pieces) in enumerate(chunks):
+            if index >= len(pieces):
+                continue
+            for copy in weight_copies[c, index]:
+                copy.wait()
+            part = jnp.dot(a_buf[index], w_buf[c, index], preferred_element_type=F32)
+            if index > 0:
+                part += acc[c]
+            elif started:
+                part += before[:, c * STEP : (c + 1) * STEP]
+            if index < len(pieces) - 1:
+                acc[c] = part
+            elif place[1] is None:
+                outs[place[0]][:, place[2]] = part
+            else:
+                share(part, shards, outs[place[0]], outs[place[1]], place[2])
+
+
+def project(shard_rows, weights, slices, chunks, outs, before=None, gates=()):
+    rows, width = shard_rows[0].shape
+    depth = width // 4
+    shards = 4
+    hbm = pl.BlockSpec(memory_space=pltpu.HBM)
+    vmem = pl.BlockSpec(memory_space=pltpu.VMEM)
+    started = before is not None
+    args = [*shard_rows, *weights, *([before] if started else []), *gates]
+    n_weight_copies = sum(len(p) for _, pieces in chunks for p in pieces)
+    work = sum(len(pieces) for _, pieces in chunks)
+    return pl.pallas_call(
+        functools.partial(
+            project_kernel, shards, slices, chunks, len(weights), started, len(gates)
+        ),
+        in_specs=[hbm] * (5 + len(weights)) + [vmem] * started + [hbm] * len(gates),
+        out_shape=[jax.ShapeDtypeStruct(shape, F32) for shape in outs],
+        scratch_shapes=[
+            pltpu.VMEM((len(slices), shards * rows, depth), BF16),
+            pltpu.VMEM((len(chunks), len(slices), depth, STEP), BF16),
+            pltpu.VMEM((len(chunks), shards * rows, STEP), F32),
+            pltpu.SemaphoreType.DMA((4 * len(slices),)),
+            pltpu.SemaphoreType.DMA((n_weight_copies,)),
+        ],
+        compiler_params=pltpu.CompilerParams(vmem_limit_bytes=58 << 20),
+        cost_estimate=pl.CostEstimate(
+            flops=2 * shards * rows * depth * STEP * work,
+            bytes_accessed=8 * rows * width,
+            transcendentals=0,
+        ),
+        name="project",
+    )(*args)
+
+
+def turn(values, cosine, sine):
+    return values * cosine + pltpu.roll(values, HD // 2, 1) * sine
+
+
+def assemble_kernel(fresh_ref, first_ref, second_ref, cached_ref, cos_ref, sin_ref, target_ref, key_ref, value_ref):
+    me = lax.axis_index("ctx")
+    low, high = fresh_ref[:, :HD].astype(F32), fresh_ref[:, HD:].astype(F32)
+    first, second = first_ref[...].astype(F32), second_ref[...].astype(F32)
+    fresh_key = jnp.where(me == 0, low, jnp.where(me == 3, second, first))
+    fresh_value = jnp.where(me == 0, first, jnp.where(me == 3, high, second)).astype(BF16)
+    fresh_key = turn(fresh_key, cos_ref[...], sin_ref[...]).astype(BF16)
+    context = cached_ref.shape[0]
+    count = fresh_key.shape[0]
+    hit = lax.broadcasted_iota(jnp.int32, (context, count), 0) == target_ref[...]
+    pick = jnp.where(hit, 1.0, 0.0)
+    taken = jnp.max(pick, axis=1, keepdims=True) > 0.5
+    pick = pick.astype(BF16)
+    key_new = jnp.dot(pick, fresh_key, preferred_element_type=F32).astype(BF16)
+    value_new = jnp.dot(pick, fresh_value, preferred_element_type=F32).astype(BF16)
+    key_ref[...] = jnp.where(taken, key_new, cached_ref[:, :HD])
+    value_ref[...] = jnp.where(taken, value_new, cached_ref[:, HD:]).T
+
+
+def assemble(fresh, first, second, cached, cosine, sine, targets):
+    context = cached.shape[0]
+    return pl.pallas_call(
+        assemble_kernel,
+        out_shape=(
+            jax.ShapeDtypeStruct((context, HD), BF16),
+            jax.ShapeDtypeStruct((HD, context), BF16),
+        ),
+        compiler_params=pltpu.CompilerParams(vmem_limit_bytes=16 << 20),
+        name="assemble",
+    )(fresh, first, second, cached, cosine, sine, targets)
+
+
+def attend_kernel(heads, *refs):
+    own_ref, sib_ref, key_ref, value_ref, cos_ref, sin_ref, pos_ref, key_pos_ref, *rest = refs
+    out_ref = rest[-1]
+    visible = key_pos_ref[...] <= pos_ref[...]
+    for h in range(heads):
+        cols = slice(h * HD, (h + 1) * HD)
+        raw = own_ref[:, cols] + sib_ref[:, cols]
+        query = (turn(raw, cos_ref[...], sin_ref[...]) * HD ** (-0.5)).astype(BF16)
+        scores = lax.dot_general(
+            key_ref[...], query, (((1,), (1,)), ((), ())), preferred_element_type=F32
+        )
+        scores = jnp.where(visible, scores, -1e30)
+        exponent = jnp.exp(scores - jnp.max(scores, axis=0, keepdims=True))
+        weights = exponent * (1.0 / jnp.sum(exponent, axis=0, keepdims=True))
+        turned = jnp.dot(value_ref[...], weights.astype(BF16), preferred_element_type=F32)
+        out_ref[:, cols] = turned.T.astype(BF16)
+
+
+def attend(own, sib, shared, width, start, before):
+    rec_count, cols = own.shape
+    args = [own, sib, *shared]
+    specs = [pl.BlockSpec(a.shape, lambda i: (0, 0)) for a in args]
+    aliases = {}
+    if before is not None:
+        aliases = {len(args): 0}
+        args.append(before)
+        specs.append(pl.BlockSpec(memory_space=pltpu.HBM))
+    return pl.pallas_call(
+        functools.partial(attend_kernel, cols // HD),
+        grid=(1,),
+        in_specs=specs,
+        out_specs=pl.BlockSpec((rec_count, cols), lambda i: (0, start // cols)),
+        out_shape=jax.ShapeDtypeStruct((rec_count, width), BF16),
+        input_output_aliases=aliases,
+        compiler_params=pltpu.CompilerParams(vmem_limit_bytes=16 << 20),
+        name="attend",
+    )(*args)
+
+
+def fast_body(store_kv, block_slot, block_owner, rec_pos, states, w_query, w_keyval):
+    store_count = lax.axis_size("store")
+    ctx_count = lax.axis_size("ctx")
+    my_index = lax.axis_index("ctx")
+    piece_rows = store_kv.shape[1]
+    block_count = block_slot.shape[1]
+    rec_count = rec_pos.shape[1]
+    query_cols = w_query.shape[1]
+    depth = w_query.shape[0]
+    positions = rec_pos[0]
+    xf, yf, cf = (flip(b, store_count) for b in (XBIT, YBIT, CORE))
+    by_x = lambda a: lax.ppermute(a, "store", xf)
+    by_y = lambda a: lax.ppermute(a, "store", yf)
+    by_core = lambda a: lax.ppermute(a, "store", cf)
+
+    along = lambda a, pairs: lax.ppermute(a, "ctx", pairs)
+    kv_cols = w_keyval.shape[1]
+    late = query_cols // 2
+    early = query_cols - late
+    first_cols = kv_cols + early
+    half = depth // 2
+
+    (w_first,) = cut(
+        (w_keyval, w_query),
+        [[(0, (0, 0), (0, 0), (depth, kv_cols)), (1, (0, 0), (0, kv_cols), (depth, early))]],
+        [(depth, first_cols)],
+    )
+    first_x, first_y = by_x(w_first), by_y(w_first)
+    asked, places = swap_ids(block_slot[0], block_owner[0], store_count)
+    (w_last,) = cut(
+        (w_query,), [[(0, (0, early), (0, 0), (depth, late))]], [(depth, late)], (asked,)
+    )
+    last_x, last_y = by_x(w_last), by_y(w_last)
+
+    keep, send = norm_split(states[0])
+    shard, width = keep.shape
+    (both,) = cut(
+        (keep, by_core(send)),
+        [[(0, (0, 0), (0, 0), (shard, width)), (1, (0, 0), (shard, 0), (shard, width))]],
+        [(2 * shard, width)],
+        near=True,
+    )
+    along = lambda a, pairs: lax.ppermute(a, "ctx", pairs)
+    two = along(both, [(0, 2), (1, 3), (2, 0), (3, 1)])
+    one = along(both, [(0, 1), (1, 0), (2, 3), (3, 2)])
+    up, down = relay(both, two)
+    shard_parts = (
+        both,
+        one,
+        two,
+        along(up, [(1, 2), (2, 3)]),
+        along(down, [(2, 1), (1, 0)]),
+    )
+
+    def diagonal(from_x, from_y):
+        cols = from_x.shape[1]
+        to_x, to_y = cut(
+            (from_y, from_x),
+            [[(0, (0, 0), (0, 0), (half, cols))], [(1, (half, 0), (0, 0), (half, cols))]],
+            [(half, cols)] * 2,
+        )
+        return (by_x(to_x), by_y(to_y)), to_x
+
+    diag_first, _ = diagonal(first_x, first_y)
+    diag_last, sent_last = diagonal(last_x, last_y)
+
+    arrived = lax.all_to_all(store_kv[asked], "store", split_axis=0, concat_axis=0, tiled=True)
+    shard_rows = block_count * piece_rows
+    arrived = arrived.reshape((-1,) + store_kv.shape[1:])
+    by_head = sort_blocks(arrived, places, (up, sent_last))
+    cached = lax.all_to_all(by_head, "ctx", split_axis=0, concat_axis=0, tiled=True)
+    cached = cached.reshape(ctx_count * shard_rows, 2 * HD)
+
+    frequency = jnp.exp(
+        jnp.arange(HD // 2, dtype=F32) * (-2.0 * math.log(500000.0) / HD)
+    )
+    angles = positions.astype(F32)[:, None] * frequency[None, :]
+    cos_half, sin_half = jnp.cos(angles), jnp.sin(angles)
+    cosine = jnp.concatenate((cos_half, cos_half), axis=1)
+    sine = jnp.concatenate((-sin_half, sin_half), axis=1)
+    block_len = piece_rows * ctx_count
+    targets = (
+        positions % block_len // piece_rows * shard_rows
+        + positions // block_len * piece_rows
+        + positions % piece_rows
+    )
+
+    row_ids = jnp.arange(ctx_count * shard_rows)
+    key_pos = (
+        row_ids % shard_rows // piece_rows * block_len
+        + row_ids // shard_rows * piece_rows
+        + row_ids % piece_rows
+    )
+
+    def pieces(own, own_col, near, col):
+        whole = [[(own, 0, own_col, depth)], [(near, 0, col, depth)], [(near + 1, 0, col, depth)]]
+        return whole, whole + [[(near + 2, 0, col, half), (near + 3, 0, col, half)]]
+
+    kv_own, kv_sib = project(
+        shard_parts,
+        (w_keyval, first_x, first_y, *diag_first),
+        (0, 1, 2, 3),
+        [((0, 1, slice(0, STEP)), pieces(0, 0, 1, 0)[1])],
+        [(rec_count, kv_cols)] * 2,
+    )
+    chunks = []
+    for col in range(0, early, STEP):
+        chunks.append(((0, 1, slice(col, col + STEP)), pieces(0, col, 1, kv_cols + col)[1]))
+    for col in range(0, late, STEP):
+        chunks.append(((2, None, slice(col, col + STEP)), pieces(0, early + col, 5, col)[0]))
+    early_own, early_sib, rest = project(
+        shard_parts,
+        (w_query, first_x, first_y, *diag_first, last_x, last_y),
+        (0, 1, 2, 3),
+        chunks,
+        [(rec_count, early)] * 2 + [(2 * rec_count, late)],
+        gates=(kv_sib,),
+    )
+    fresh = (kv_own + by_core(kv_sib)).astype(BF16)
+    low, high = fresh[:, :HD], fresh[:, HD:]
+    first = along(jnp.where(my_index == 0, high, low), [(0, 1), (1, 2), (2, 0)])
+    second = along(jnp.where(my_index == 3, low, high), [(1, 3), (2, 1), (3, 2)])
+    key_rows, value_rows = assemble(
+        fresh, first, second, cached, cosine, sine, targets.reshape(1, rec_count)
+    )
+    shared = (
+        key_rows,
+        value_rows,
+        cosine,
+        sine,
+        positions.reshape(1, rec_count),
+        key_pos.reshape(-1, 1),
+    )
+    result = attend(early_own, by_core(early_sib), shared, query_cols, 0, None)
+    own, sib = project(
+        shard_parts,
+        diag_last,
+        (3,),
+        [
+            ((0, 1, slice(col, col + STEP)), [[(0, 0, col, half), (1, 0, col, half)]])
+            for col in range(0, late, STEP)
+        ],
+        [(rec_count, late)] * 2,
+        before=rest,
+    )
+    result = attend(own, by_core(sib), shared, query_cols, early, result)
+    return result.reshape(1, rec_count, query_cols)
+
+
 def solution(mesh):
+    fast = mesh.shape["store"] == 8 and mesh.shape["ctx"] == KVH
     return jax.shard_map(
-        body,
+        fast_body if fast else general_body,
         mesh=mesh,
         in_specs=(
             P("store", "ctx", None),

time: 292 us -> 146 us (0.50)
  waiting for transfers between devices: 219 us -> 27.6 us
  Pallas kernels: 0 us -> 37.1 us
  starting transfers between devices: 8.75 us -> 33.8 us
  blocking collectives: 16.1 us -> 32.2 us
  matrix products: 15.3 us -> 0 us
  between operations: 13.3 us -> 0.35 us
  other arithmetic: 11.7 us -> 2.52 us
  local copies, waits for them, and re-layouts: 7.27 us -> 11.2 us
    all_gather x4 -> x0, waiting for transfers between devices: 208 us -> none  [the longest x1 80.9 us: body(): row_piece = lax.all_gather(normed, 'ctx', axis=0, tiled=True)]
    pallas_call x0 -> x14, Pallas kernels: none -> 37.1 us  [the longest x3 22.4 us: project(): pl.pallas_call(functools.partial(project_kernel, shards, slices, chunks,...]
    all_to_all x0 -> x1, blocking collectives: none -> 32.2 us  [swap_ids(): lax.all_to_all(wanted, 'store', split_axis=0, concat_axis=0, tiled=True)]
    ppermute x0 -> x18, starting transfers between devices: none -> 25.5 us  [the longest x6 11.1 us: fast_body(): along = lambda a, pairs: lax.ppermute(a, 'ctx', pairs)]
    ppermute x0 -> x18, waiting for transfers between devices: none -> 23.9 us  [the longest x6 11.3 us: fast_body(): along = lambda a, pairs: lax.ppermute(a, 'ctx', pairs)]
    all_gather x1 -> x0, blocking collectives: 16.1 us -> none  [body(): lax.all_gather(keyval_raw.astype(jnp.bfloat16), 'ctx', axis=1, tiled=True)]
    dot_general x4 -> x0, matrix products: 15.3 us -> none  [the longest x1 9.32 us: body(): jnp.dot(row_piece, query_weight, preferred_element_type=jnp.float32)]
    unnamed x5 -> x40, local copies, waits for them, and re-layouts: 0.21 us -> 9.52 us
  transfers between devices with their start and end apart: 6 -> 20, of which waited for: 6 -> 5; matrix products, arithmetic and copies ran while one was open for 5% -> 3% of each run, Pallas kernels for 0% -> 23%
where the time goes in v2:
time: 146 us; the launch traced here: 145 us
  Pallas kernels  37.1 us (25%)
  starting transfers between devices  33.8 us (23%)
  blocking collectives  32.2 us (22%)
  waiting for transfers between devices  27.6 us (19%)
  local copies, waits for them, and re-layouts  11.2 us (8%)
  other arithmetic  2.52 us (2%)
    all_to_all x1, blocking collectives, swap_ids(): lax.all_to_all(wanted, 'store', split_axis=0, concat_axis=0, tiled=True)  32.2 us
    pallas_call x3, Pallas kernels, project(): pl.pallas_call(functools.partial(project_kernel, shards, slices, chunks,...  22.4 us
    ppermute x6, waiting for transfers between devices, fast_body(): along = lambda a, pairs: lax.ppermute(a, 'ctx', pairs)  11.3 us
    ppermute x6, starting transfers between devices, fast_body(): along = lambda a, pairs: lax.ppermute(a, 'ctx', pairs)  11.1 us
    unnamed x40, local copies, waits for them, and re-layouts  9.52 us
    ppermute x4, waiting for transfers between devices, fast_body(): by_x = lambda a: lax.ppermute(a, 'store', xf)  6.73 us
    ppermute x4, starting transfers between devices, fast_body(): by_y = lambda a: lax.ppermute(a, 'store', yf)  6.73 us
    ppermute x4, starting transfers between devices, fast_body(): by_x = lambda a: lax.ppermute(a, 'store', xf)  6.44 us
  transfers between devices with their start and end apart: 20, of which 5 were waited for; matrix products, arithmetic and copies ran while one was open for 3% of the time, Pallas kernels for 23%

profile of v2, /device:TPU:0, one launch (start us, length us, event | category | flops | bytes accessed | tf_op | source)
XLA Modules:
  0.0 144.8 jit_solution(16450325754589655246)
XLA Ops:
  0.0 1.3 copy-done.10
  1.3 0.4 norm_split.1
  1.7 0.5 collective-permute-start
  2.3 1.6 %copy-done.2 = bf16[1024,1024]{1,0:T(8,128)(2,1)S(1)} copy-done((bf16[1024,1024]{1,0:T(8,128)(2,1)S(1)}, bf16[1024,1024]{1,0:T(8,128)(2,1)}, u32[]{:S(2)}) %copy-start.2) | copy-done | bytes 2097176
  3.9 1.0 copy-done.9
  4.9 1.3 cut.8
  6.3 0.0 copy-start.18
  6.3 2.6 %collective-permute-start.10 = (bf16[1024,768]{1,0:T(8,128)(2,1)}, bf16[1024,768]{1,0:T(8,128)(2,1)}, u32[]{:S(2)}, u32[]{:S(2)}) collective-permute-start(bf16[1024,768]{1,0:T(8,128)(2,1)} %cut.8), channel_id=1, source_target_pairs={{0,16},{4,20},{8,24},{12,28},{16,0},{20,4},{24,8},{28,12},{1,17},{... | collective-permute-start | bytes 4718600 | tf_op jit(solution)/shard_map/ppermute | solution.py:437
  8.9 1.5 %collective-permute-start.9 = (bf16[1024,768]{1,0:T(8,128)(2,1)}, bf16[1024,768]{1,0:T(8,128)(2,1)}, u32[]{:S(2)}, u32[]{:S(2)}) collective-permute-start(bf16[1024,768]{1,0:T(8,128)(2,1)} %cut.8), channel_id=1, source_target_pairs={{0,8},{4,12},{8,0},{12,4},{16,24},{20,28},{24,16},{28,20},{1,9},{5... | collective-permute-start | bytes 4718600 | tf_op jit(solution)/shard_map/ppermute | solution.py:436
  10.4 0.2 convert_reduce_fusion
  10.5 0.0 collective-permute-done.refs_1_
  10.6 0.1 cut.5.own.refs_0_
  10.7 2.7 %collective-permute-start.2 = (bf16[128,4096]{1,0:T(8,128)(2,1)S(1)}, bf16[128,4096]{1,0:T(8,128)(2,1)S(1)}, u32[]{:S(2)}, u32[]{:S(2)}) collective-permute-start(bf16[128,4096]{1,0:T(8,128)(2,1)S(1)} %cut.5.own.refs_0_), channel_id=1, source_target_pairs={{0,2},{1,3},{2,0},{3,1},{4,6},{5,7},{6,4},{7,5},{8,10},{9,11},{10,... | collective-permute-start | bytes 3145736 | tf_op jit(solution)/shard_map/ppermute | solution.py:467
  13.3 0.1 select_reduce_fusion
  13.5 0.1 copy.18
  13.6 32.2 %all_to_all.24 = s32[8,1,2]{2,1,0:T(1,128)S(1)} all-to-all(s32[8,1,2]{2,1,0:T(1,128)S(1)} %copy.18), channel_id=1, replica_groups=mesh['store'=8,'ctx'=4] {'store'}, dimensions={0} | all-to-all | bytes 128 | tf_op jit(solution)/shard_map/all_to_all | solution.py:50
  45.7 0.1 copy.19
  45.8 0.1 copy.20.refs_1_
  45.9 1.6 %copy-done.3 = bf16[1024,1024]{1,0:T(8,128)(2,1)S(1)} copy-done((bf16[1024,1024]{1,0:T(8,128)(2,1)S(1)}, bf16[1024,1024]{1,0:T(8,128)(2,1)}, u32[]{:S(2)}) %copy-start.3) | copy-done | bytes 2097176
  47.5 0.1 cut.6
  47.6 0.0 copy-start.13
  47.6 1.4 collective-permute-start.5
  49.1 1.5 %collective-permute-start.6 = (bf16[1024,512]{1,0:T(8,128)(2,1)S(1)}, bf16[1024,512]{1,0:T(8,128)(2,1)S(1)}, u32[]{:S(2)}, u32[]{:S(2)}) collective-permute-start(bf16[1024,512]{1,0:T(8,128)(2,1)S(1)} %cut.6), channel_id=1, source_target_pairs={{0,8},{4,12},{8,0},{12,4},{16,24},{20,28},{24,16},{28,20},{1,9},{5... | collective-permute-start | bytes 3145736 | tf_op jit(solution)/shard_map/ppermute | solution.py:436
  50.5 8.6 %collective-permute-done.2.two.refs_2_ = bf16[128,4096]{1,0:T(8,128)(2,1)S(1)} collective-permute-done((bf16[128,4096]{1,0:T(8,128)(2,1)S(1)}, bf16[128,4096]{1,0:T(8,128)(2,1)S(1)}, u32[]{:S(2)}, u32[]{:S(2)}) %collective-permute-start.2) | collective-permute-done | bytes 1048608 | tf_op jit(solution)/shard_map/ppermute | solution.py:467
  59.1 0.7 collective-permute-start.1
  59.8 1.6 %relay.1 = (bf16[128,4096]{1,0:T(8,128)(2,1)}, bf16[128,4096]{1,0:T(8,128)(2,1)}) custom-call(bf16[128,4096]{1,0:T(8,128)(2,1)S(1)} %cut.5.own.refs_0_, bf16[128,4096]{1,0:T(8,128)(2,1)S(1)} %collective-permute-done.2.two.refs_2_), custom_call_target="tpu_custom_call" | custom-call | tf_op jit(solution)/shard_map/relay/pallas_call | solution.py:206
  61.4 1.7 %collective-permute-start.3 = (bf16[128,4096]{1,0:T(8,128)(2,1)}, bf16[128,4096]{1,0:T(8,128)(2,1)}, u32[]{:S(2)}, u32[]{:S(2)}) collective-permute-start(bf16[128,4096]{1,0:T(8,128)(2,1)} %get-tuple-element.24.refs_0_), channel_id=1, source_target_pairs={{1,2},{2,3},{5,6},{6,7},{9,10},{10,11},{13,14},{14,15},{17,18},{18... | collective-permute-start | bytes 3145736 | tf_op jit(solution)/shard_map/ppermute | solution.py:467
  63.1 0.0 collective-permute-done.9.refs_1_.refs_6_
  63.1 1.3 collective-permute-start.4
  64.5 2.5 %cut.9 = (bf16[512,768]{1,0:T(8,128)(2,1)}, bf16[512,768]{1,0:T(8,128)(2,1)}) custom-call(bf16[1024,768]{1,0:T(8,128)(2,1)} %collective-permute-done.10.refs_0_.refs_7_, bf16[1024,768]{1,0:T(8,128)(2,1)} %collective-permute-done.9.refs_1_.refs_6_), custom_call_target="tpu_custom_call" | custom-call | tf_op jit(solution)/shard_map/cut/pallas_call | solution.py:177
  67.0 5.8 %collective-permute-done.5.refs_0_.refs_11_ = bf16[1024,512]{1,0:T(8,128)(2,1)S(1)} collective-permute-done((bf16[1024,512]{1,0:T(8,128)(2,1)S(1)}, bf16[1024,512]{1,0:T(8,128)(2,1)S(1)}, u32[]{:S(2)}, u32[]{:S(2)}) %collective-permute-start.5) | collective-permute-done | bytes 1048608 | tf_op jit(solution)/shard_map/ppermute | solution.py:437
  72.9 1.0 copy-done.5
  73.8 1.5 %collective-permute-start.11 = (bf16[512,768]{1,0:T(8,128)(2,1)}, bf16[512,768]{1,0:T(8,128)(2,1)}, u32[]{:S(2)}, u32[]{:S(2)}) collective-permute-start(bf16[512,768]{1,0:T(8,128)(2,1)} %get-tuple-element.28), channel_id=1, source_target_pairs={{0,8},{4,12},{8,0},{12,4},{16,24},{20,28},{24,16},{28,20},{1,9},{5... | collective-permute-start | bytes 2359304 | tf_op jit(solution)/shard_map/ppermute | solution.py:436
  75.3 1.0 copy-done.7
  76.3 1.4 collective-permute-start.12
  77.7 1.2 fusion.21
  78.9 0.1 copy.22
  79.0 0.1 reshape.235
  79.1 1.3 gather_fusion
  80.4 3.4 %all-to-all-start.1 = ((bf16[8,2,8,1024]{3,2,1,0:T(8,128)(2,1)}), bf16[8,2,8,1024]{3,2,1,0:T(8,128)(2,1)S(1)}, u32[]{:S(2)}, u32[]{:S(2)}) async-start(bf16[8,2,8,1024]{3,2,1,0:T(8,128)(2,1)} %bitcast.6), calls=%async_computation.1 | async-start | bytes 524288 | tf_op jit(solution)/shard_map/all_to_all | solution.py:491
  83.8 1.2 copy-done.8
  85.0 0.9 cut.7
  85.9 2.0 %collective-permute-start.7 = (bf16[512,512]{1,0:T(8,128)(2,1)S(1)}, bf16[512,512]{1,0:T(8,128)(2,1)S(1)}, u32[]{:S(2)}, u32[]{:S(2)}) collective-permute-start(bf16[512,512]{1,0:T(8,128)(2,1)S(1)} %get-tuple-element.26.refs_1_), channel_id=1, source_target_pairs={{0,8},{4,12},{8,0},{12,4},{16,24},{20,28},{24,16},{28,20},{1,9},{5... | collective-permute-start | bytes 1572872 | tf_op jit(solution)/shard_map/ppermute | solution.py:436
  87.9 6.7 %collective-permute-done.11.refs_8_ = bf16[512,768]{1,0:T(8,128)(2,1)} collective-permute-done((bf16[512,768]{1,0:T(8,128)(2,1)}, bf16[512,768]{1,0:T(8,128)(2,1)}, u32[]{:S(2)}, u32[]{:S(2)}) %collective-permute-start.11) | collective-permute-done | bytes 786464 | tf_op jit(solution)/shard_map/ppermute | solution.py:436
  94.6 1.4 collective-permute-start.8
  96.0 0.1 fusion.13.refs_7_
  96.1 3.7 %all-to-all-done.1 = bf16[8,2,8,1024]{3,2,1,0:T(8,128)(2,1)S(1)} async-done(((bf16[8,2,8,1024]{3,2,1,0:T(8,128)(2,1)}), bf16[8,2,8,1024]{3,2,1,0:T(8,128)(2,1)S(1)}, u32[]{:S(2)}, u32[]{:S(2)}) %all-to-all-start.1) | async-done | bytes 262176 | tf_op jit(solution)/shard_map/all_to_all | solution.py:491
  99.8 1.3 sort_blocks.1
  101.1 4.9 %all-to-all-start.2 = ((bf16[4,128,256]{2,1,0:T(8,128)(2,1)}), bf16[4,128,256]{2,1,0:T(8,128)(2,1)S(1)}, u32[]{:S(2)}, u32[]{:S(2)}) async-start(bf16[4,128,256]{2,1,0:T(8,128)(2,1)} %sort_blocks.1), calls=%async_computation.2 | async-start | bytes 524288 | tf_op jit(solution)/shard_map/all_to_all | solution.py:495
  106.0 5.6 %project.3 = (f32[256,256]{1,0:T(8,128)}, f32[256,256]{1,0:T(8,128)}) custom-call(bf16[128,4096]{1,0:T(8,128)(2,1)} %copy-done.1, bf16[128,4096]{1,0:T(8,128)(2,1)} %collective-permute-done.1.refs_1_, bf16[128,4096]{1,0:T(8,128)(2,1)} %copy-done.4, bf16[128,4096]{1,0:T(8,128)(2,1)} %collective-permute-done.3.refs_3_, ...), custom_call_target="tpu_custom_call" | custom-call | flops 1073741824 | bytes 4194304 | tf_op jit(solution)/shard_map/project/pallas_call | solution.py:327
  111.6 0.1 collective-permute-start.14
  111.6 11.7 %project.4 = (f32[256,512]{1,0:T(8,128)}, f32[256,512]{1,0:T(8,128)}, f32[512,512]{1,0:T(8,128)}) custom-call(bf16[128,4096]{1,0:T(8,128)(2,1)} %copy-done.1, bf16[128,4096]{1,0:T(8,128)(2,1)} %collective-permute-done.1.refs_1_, bf16[128,4096]{1,0:T(8,128)(2,1)} %copy-done.4, bf16[128,4096]{1,0:T(8,128)(2,1)} %collective-permute-done.3.refs_3_, ...), custom_call_target="tpu_custom_call" | custom-call | flops 3758096384 | bytes 4194304 | tf_op jit(solution)/shard_map/project/pallas_call | solution.py:327
  123.4 0.6 collective-permute-start.17
  123.9 0.8 copy-done.14
  124.7 5.1 %project.5 = (f32[256,512]{1,0:T(8,128)}, f32[256,512]{1,0:T(8,128)}) custom-call(bf16[128,4096]{1,0:T(8,128)(2,1)} %copy-done.1, bf16[128,4096]{1,0:T(8,128)(2,1)} %collective-permute-done.1.refs_1_, bf16[128,4096]{1,0:T(8,128)(2,1)} %copy-done.4, bf16[128,4096]{1,0:T(8,128)(2,1)} %collective-permute-done.3.refs_3_, ...), custom_call_target="tpu_custom_call" | custom-call | flops 536870912 | bytes 4194304 | tf_op jit(solution)/shard_map/project/pallas_call | solution.py:327
  129.9 0.1 collective-permute-start.13
  130.0 0.6 broadcast_select_fusion
  130.7 3.9 %collective-permute-start.15 = (bf16[256,128]{1,0:T(8,128)(2,1)}, bf16[256,128]{1,0:T(8,128)(2,1)S(1)}, u32[]{:S(2)}, u32[]{:S(2)}) collective-permute-start(bf16[256,128]{1,0:T(8,128)(2,1)} %get-tuple-element.40), channel_id=1, source_target_pairs={{0,1},{1,2},{2,0},{4,5},{5,6},{6,4},{8,9},{9,10},{10,8},{12,13},{1... | collective-permute-start | bytes 196616 | tf_op jit(solution)/shard_map/ppermute | solution.py:467
  134.6 0.8 collective-permute-start.16
  135.5 0.1 pad_maximum_fusion
  135.6 2.7 %collective-permute-done.15.first_ref = bf16[256,128]{1,0:T(8,128)(2,1)S(1)} collective-permute-done((bf16[256,128]{1,0:T(8,128)(2,1)}, bf16[256,128]{1,0:T(8,128)(2,1)S(1)}, u32[]{:S(2)}, u32[]{:S(2)}) %collective-permute-start.15) | collective-permute-done | bytes 65568 | tf_op jit(solution)/shard_map/ppermute | solution.py:467
  138.3 0.4 assemble.1
  138.8 3.0 %attend.2.refs_8_ = bf16[256,1024]{1,0:T(8,128)(2,1)} custom-call(f32[256,512]{1,0:T(8,128)S(1)} %copy-done.11, f32[256,512]{1,0:T(8,128)S(1)} %collective-permute-done.17.refs_1_, bf16[512,128]{1,0:T(8,128)(2,1)S(1)} %get-tuple-element.35.refs_2_, bf16[128,512]{1,0:T(8,128)(2,1)S(1)} %get-tuple-element.36.refs_3_, ...), custom_call_target="tpu_custom_call" | custom-call | tf_op jit(solution)/shard_map/attend/pallas_call | solution.py:413
  141.8 3.0 %attend.3 = bf16[256,1024]{1,0:T(8,128)(2,1)} custom-call(f32[256,512]{1,0:T(8,128)S(1)} %copy-done.12, f32[256,512]{1,0:T(8,128)S(1)} %collective-permute-done.13.refs_1_, bf16[512,128]{1,0:T(8,128)(2,1)S(1)} %get-tuple-element.35.refs_2_, bf16[128,512]{1,0:T(8,128)(2,1)S(1)} %get-tuple-element.36.refs_3_, ...), custom_call_target="tpu_custom_call", output_to_operand_aliasing={{}: (8, {})} | custom-call | tf_op jit(solution)/shard_map/attend/pallas_call | solution.py:413
  (51 shorter events, 0.2 us)
Async XLA Ops:
  0.0 79.1 %copy-start = (bf16[32,8,1024]{2,1,0:T(8,128)(2,1)S(1)}, bf16[32,8,1024]{2,1,0:T(8,128)(2,1)}, u32[]{:S(2)}) copy-start(bf16[32,8,1024]{2,1,0:T(8,128)(2,1)} %param.7) | copy-start | bytes 1572868
  0.0 1.3 copy-start.10
  1.7 8.8 %collective-permute-start = (bf16[64,4096]{1,0:T(8,128)(2,1)S(1)}, bf16[64,4096]{1,0:T(8,128)(2,1)S(1)}, u32[]{:S(2)}, u32[]{:S(2)}) collective-permute-start(bf16[64,4096]{1,0:T(8,128)(2,1)S(1)} %get-tuple-element.23), channel_id=1, source_target_pairs={{0,4},{4,0},{8,12},{12,8},{16,20},{20,16},{24,28},{28,24},{1,5},{5... | collective-permute-start | bytes 1572872 | tf_op jit(solution)/shard_map/ppermute | solution.py:438
  2.3 1.6 %copy-start.2 = (bf16[1024,1024]{1,0:T(8,128)(2,1)S(1)}, bf16[1024,1024]{1,0:T(8,128)(2,1)}, u32[]{:S(2)}) copy-start(bf16[1024,1024]{1,0:T(8,128)(2,1)} %refs_5_.3) | copy-start | bytes 6291460
  3.9 1.0 copy-start.9
  4.9 5.5 %copy-start.19 = (s32[1,16]{1,0:T(1,128)S(1)}, s32[1,16]{1,0:T(1,128)}, u32[]{:S(2)}) copy-start(s32[1,16]{1,0:T(1,128)} %param.9) | copy-start | bytes 196
  6.3 7.1 %copy-start.18 = (s32[1,16]{1,0:T(1,128)S(1)}, s32[1,16]{1,0:T(1,128)}, u32[]{:S(2)}) copy-start(s32[1,16]{1,0:T(1,128)} %param.8) | copy-start | bytes 196
  6.3 55.1 %collective-permute-start.10 = (bf16[1024,768]{1,0:T(8,128)(2,1)}, bf16[1024,768]{1,0:T(8,128)(2,1)}, u32[]{:S(2)}, u32[]{:S(2)}) collective-permute-start(bf16[1024,768]{1,0:T(8,128)(2,1)} %cut.8), channel_id=1, source_target_pairs={{0,16},{4,20},{8,24},{12,28},{16,0},{20,4},{24,8},{28,12},{1,17},{... | collective-permute-start | bytes 4718600 | tf_op jit(solution)/shard_map/ppermute | solution.py:437
  8.9 54.3 %collective-permute-start.9 = (bf16[1024,768]{1,0:T(8,128)(2,1)}, bf16[1024,768]{1,0:T(8,128)(2,1)}, u32[]{:S(2)}, u32[]{:S(2)}) collective-permute-start(bf16[1024,768]{1,0:T(8,128)(2,1)} %cut.8), channel_id=1, source_target_pairs={{0,8},{4,12},{8,0},{12,4},{16,24},{20,28},{24,16},{28,20},{1,9},{5... | collective-permute-start | bytes 4718600 | tf_op jit(solution)/shard_map/ppermute | solution.py:436
  10.7 49.1 %copy-start.1 = (bf16[128,4096]{1,0:T(8,128)(2,1)}, bf16[128,4096]{1,0:T(8,128)(2,1)S(1)}, u32[]{:S(2)}) copy-start(bf16[128,4096]{1,0:T(8,128)(2,1)S(1)} %cut.5.own.refs_0_) | copy-start | bytes 3145732
  10.7 48.4 %collective-permute-start.2 = (bf16[128,4096]{1,0:T(8,128)(2,1)S(1)}, bf16[128,4096]{1,0:T(8,128)(2,1)S(1)}, u32[]{:S(2)}, u32[]{:S(2)}) collective-permute-start(bf16[128,4096]{1,0:T(8,128)(2,1)S(1)} %cut.5.own.refs_0_), channel_id=1, source_target_pairs={{0,2},{1,3},{2,0},{3,1},{4,6},{5,7},{6,4},{7,5},{8,10},{9,11},{10,... | collective-permute-start | bytes 3145736 | tf_op jit(solution)/shard_map/ppermute | solution.py:467
  45.9 1.6 %copy-start.3 = (bf16[1024,1024]{1,0:T(8,128)(2,1)S(1)}, bf16[1024,1024]{1,0:T(8,128)(2,1)}, u32[]{:S(2)}) copy-start(bf16[1024,1024]{1,0:T(8,128)(2,1)} %refs_5_.3) | copy-start | bytes 6291460
  47.6 16.8 %copy-start.13 = (s32[1,256]{1,0:T(1,128)S(1)}, s32[1,256]{1,0:T(1,128)}, u32[]{:S(2)}) copy-start(s32[1,256]{1,0:T(1,128)} %refs_6_.3) | copy-start | bytes 3076
  47.6 25.2 %collective-permute-start.5 = (bf16[1024,512]{1,0:T(8,128)(2,1)S(1)}, bf16[1024,512]{1,0:T(8,128)(2,1)S(1)}, u32[]{:S(2)}, u32[]{:S(2)}) collective-permute-start(bf16[1024,512]{1,0:T(8,128)(2,1)S(1)} %cut.6), channel_id=1, source_target_pairs={{0,16},{4,20},{8,24},{12,28},{16,0},{20,4},{24,8},{28,12},{1,17},{... | collective-permute-start | bytes 3145736 | tf_op jit(solution)/shard_map/ppermute | solution.py:437
  49.1 26.3 %collective-permute-start.6 = (bf16[1024,512]{1,0:T(8,128)(2,1)S(1)}, bf16[1024,512]{1,0:T(8,128)(2,1)S(1)}, u32[]{:S(2)}, u32[]{:S(2)}) collective-permute-start(bf16[1024,512]{1,0:T(8,128)(2,1)S(1)} %cut.6), channel_id=1, source_target_pairs={{0,8},{4,12},{8,0},{12,4},{16,24},{20,28},{24,16},{28,20},{1,9},{5... | collective-permute-start | bytes 3145736 | tf_op jit(solution)/shard_map/ppermute | solution.py:436
  59.1 7.9 %copy-start.4 = (bf16[128,4096]{1,0:T(8,128)(2,1)}, bf16[128,4096]{1,0:T(8,128)(2,1)S(1)}, u32[]{:S(2)}) copy-start(bf16[128,4096]{1,0:T(8,128)(2,1)S(1)} %collective-permute-done.2.two.refs_2_) | copy-start | bytes 3145732
  59.1 26.8 %collective-permute-start.1 = (bf16[128,4096]{1,0:T(8,128)(2,1)S(1)}, bf16[128,4096]{1,0:T(8,128)(2,1)}, u32[]{:S(2)}, u32[]{:S(2)}) collective-permute-start(bf16[128,4096]{1,0:T(8,128)(2,1)S(1)} %cut.5.own.refs_0_), channel_id=1, source_target_pairs={{0,1},{1,0},{2,3},{3,2},{4,5},{5,4},{6,7},{7,6},{8,9},{9,8},{10,11... | collective-permute-start | bytes 3145736 | tf_op jit(solution)/shard_map/ppermute | solution.py:467
  61.4 44.6 %collective-permute-start.3 = (bf16[128,4096]{1,0:T(8,128)(2,1)}, bf16[128,4096]{1,0:T(8,128)(2,1)}, u32[]{:S(2)}, u32[]{:S(2)}) collective-permute-start(bf16[128,4096]{1,0:T(8,128)(2,1)} %get-tuple-element.24.refs_0_), channel_id=1, source_target_pairs={{1,2},{2,3},{5,6},{6,7},{9,10},{10,11},{13,14},{14,15},{17,18},{18... | collective-permute-start | bytes 3145736 | tf_op jit(solution)/shard_map/ppermute | solution.py:467
  63.1 42.8 %collective-permute-start.4 = (bf16[128,4096]{1,0:T(8,128)(2,1)}, bf16[128,4096]{1,0:T(8,128)(2,1)}, u32[]{:S(2)}, u32[]{:S(2)}) collective-permute-start(bf16[128,4096]{1,0:T(8,128)(2,1)} %get-tuple-element.25), channel_id=1, source_target_pairs={{2,1},{1,0},{6,5},{5,4},{10,9},{9,8},{14,13},{13,12},{18,17},{17,1... | collective-permute-start | bytes 3145736 | tf_op jit(solution)/shard_map/ppermute | solution.py:467
  72.9 1.0 copy-start.5
  73.8 10.0 %copy-start.6 = (bf16[1024,512]{1,0:T(8,128)(2,1)S(1)}, bf16[1024,512]{1,0:T(8,128)(2,1)}, u32[]{:S(2)}) copy-start(bf16[1024,512]{1,0:T(8,128)(2,1)} %copy-done.5) | copy-start | bytes 3145732
  73.8 20.8 %collective-permute-start.11 = (bf16[512,768]{1,0:T(8,128)(2,1)}, bf16[512,768]{1,0:T(8,128)(2,1)}, u32[]{:S(2)}, u32[]{:S(2)}) collective-permute-start(bf16[512,768]{1,0:T(8,128)(2,1)} %get-tuple-element.28), channel_id=1, source_target_pairs={{0,8},{4,12},{8,0},{12,4},{16,24},{20,28},{24,16},{28,20},{1,9},{5... | collective-permute-start | bytes 2359304 | tf_op jit(solution)/shard_map/ppermute | solution.py:436
  75.3 1.0 copy-start.7
  76.3 29.7 %collective-permute-start.12 = (bf16[512,768]{1,0:T(8,128)(2,1)}, bf16[512,768]{1,0:T(8,128)(2,1)}, u32[]{:S(2)}, u32[]{:S(2)}) collective-permute-start(bf16[512,768]{1,0:T(8,128)(2,1)} %get-tuple-element.29), channel_id=1, source_target_pairs={{0,16},{4,20},{8,24},{12,28},{16,0},{20,4},{24,8},{28,12},{1,17},{... | collective-permute-start | bytes 2359304 | tf_op jit(solution)/shard_map/ppermute | solution.py:437
  80.4 19.5 %all-to-all-start.1 = ((bf16[8,2,8,1024]{3,2,1,0:T(8,128)(2,1)}), bf16[8,2,8,1024]{3,2,1,0:T(8,128)(2,1)S(1)}, u32[]{:S(2)}, u32[]{:S(2)}) async-start(bf16[8,2,8,1024]{3,2,1,0:T(8,128)(2,1)} %bitcast.6), calls=%async_computation.1 | async-start | bytes 524288 | tf_op jit(solution)/shard_map/all_to_all | solution.py:491
  83.8 1.2 copy-start.8
  85.9 38.0 %collective-permute-start.7 = (bf16[512,512]{1,0:T(8,128)(2,1)S(1)}, bf16[512,512]{1,0:T(8,128)(2,1)S(1)}, u32[]{:S(2)}, u32[]{:S(2)}) collective-permute-start(bf16[512,512]{1,0:T(8,128)(2,1)S(1)} %get-tuple-element.26.refs_1_), channel_id=1, source_target_pairs={{0,8},{4,12},{8,0},{12,4},{16,24},{20,28},{24,16},{28,20},{1,9},{5... | collective-permute-start | bytes 1572872 | tf_op jit(solution)/shard_map/ppermute | solution.py:436
  94.6 29.3 %collective-permute-start.8 = (bf16[512,512]{1,0:T(8,128)(2,1)}, bf16[512,512]{1,0:T(8,128)(2,1)}, u32[]{:S(2)}, u32[]{:S(2)}) collective-permute-start(bf16[512,512]{1,0:T(8,128)(2,1)} %get-tuple-element.27), channel_id=1, source_target_pairs={{0,16},{4,20},{8,24},{12,28},{16,0},{20,4},{24,8},{28,12},{1,17},{... | collective-permute-start | bytes 1572872 | tf_op jit(solution)/shard_map/ppermute | solution.py:437
  101.1 34.5 %all-to-all-start.2 = ((bf16[4,128,256]{2,1,0:T(8,128)(2,1)}), bf16[4,128,256]{2,1,0:T(8,128)(2,1)S(1)}, u32[]{:S(2)}, u32[]{:S(2)}) async-start(bf16[4,128,256]{2,1,0:T(8,128)(2,1)} %sort_blocks.1), calls=%async_computation.2 | async-start | bytes 524288 | tf_op jit(solution)/shard_map/all_to_all | solution.py:495
  111.6 18.4 %collective-permute-start.14 = (f32[256,256]{1,0:T(8,128)}, f32[256,256]{1,0:T(8,128)S(1)}, u32[]{:S(2)}, u32[]{:S(2)}) collective-permute-start(f32[256,256]{1,0:T(8,128)} %get-tuple-element.30.refs_12_), channel_id=1, source_target_pairs={{0,4},{4,0},{8,12},{12,8},{16,20},{20,16},{24,28},{28,24},{1,5},{5... | collective-permute-start | bytes 786440 | tf_op jit(solution)/shard_map/ppermute | solution.py:438
  123.4 15.4 %collective-permute-start.17 = (f32[256,512]{1,0:T(8,128)}, f32[256,512]{1,0:T(8,128)S(1)}, u32[]{:S(2)}, u32[]{:S(2)}) collective-permute-start(f32[256,512]{1,0:T(8,128)} %get-tuple-element.38), channel_id=1, source_target_pairs={{0,4},{4,0},{8,12},{12,8},{16,20},{20,16},{24,28},{28,24},{1,5},{5... | collective-permute-start | bytes 1572872 | tf_op jit(solution)/shard_map/ppermute | solution.py:438
  123.9 0.8 copy-start.14
  124.7 5.2 %copy-start.17 = (f32[256,256]{1,0:T(8,128)S(1)}, f32[256,256]{1,0:T(8,128)}, u32[]{:S(2)}) copy-start(f32[256,256]{1,0:T(8,128)} %get-tuple-element.34) | copy-start | bytes 786436
  124.7 10.7 %copy-start.15 = (f32[256,64]{1,0:T(8,128)S(1)}, f32[256,64]{1,0:T(8,128)}, u32[]{:S(2)}) copy-start(f32[256,64]{1,0:T(8,128)} %get-tuple-element.42) | copy-start | bytes 196612
  124.7 10.7 %copy-start.16 = (f32[256,64]{1,0:T(8,128)S(1)}, f32[256,64]{1,0:T(8,128)}, u32[]{:S(2)}) copy-start(f32[256,64]{1,0:T(8,128)} %get-tuple-element.43) | copy-start | bytes 196612
  129.9 8.9 %copy-start.11 = (f32[256,512]{1,0:T(8,128)S(1)}, f32[256,512]{1,0:T(8,128)}, u32[]{:S(2)}) copy-start(f32[256,512]{1,0:T(8,128)} %get-tuple-element.37.refs_0_) | copy-start | bytes 1572868
  129.9 11.9 %collective-permute-start.13 = (f32[256,512]{1,0:T(8,128)}, f32[256,512]{1,0:T(8,128)S(1)}, u32[]{:S(2)}, u32[]{:S(2)}) collective-permute-start(f32[256,512]{1,0:T(8,128)} %get-tuple-element.33), channel_id=1, source_target_pairs={{0,4},{4,0},{8,12},{12,8},{16,20},{20,16},{24,28},{28,24},{1,5},{5... | collective-permute-start | bytes 1572872 | tf_op jit(solution)/shard_map/ppermute | solution.py:438
  130.7 7.7 %collective-permute-start.15 = (bf16[256,128]{1,0:T(8,128)(2,1)}, bf16[256,128]{1,0:T(8,128)(2,1)S(1)}, u32[]{:S(2)}, u32[]{:S(2)}) collective-permute-start(bf16[256,128]{1,0:T(8,128)(2,1)} %get-tuple-element.40), channel_id=1, source_target_pairs={{0,1},{1,2},{2,0},{4,5},{5,6},{6,4},{8,9},{9,10},{10,8},{12,13},{1... | collective-permute-start | bytes 196616 | tf_op jit(solution)/shard_map/ppermute | solution.py:467
  134.6 3.8 %collective-permute-start.16 = (bf16[256,128]{1,0:T(8,128)(2,1)}, bf16[256,128]{1,0:T(8,128)(2,1)S(1)}, u32[]{:S(2)}, u32[]{:S(2)}) collective-permute-start(bf16[256,128]{1,0:T(8,128)(2,1)} %get-tuple-element.39), channel_id=1, source_target_pairs={{1,3},{2,1},{3,2},{5,7},{6,5},{7,6},{9,11},{10,9},{11,10},{13,15},... | collective-permute-start | bytes 196616 | tf_op jit(solution)/shard_map/ppermute | solution.py:467
  138.3 3.4 %copy-start.12 = (f32[256,512]{1,0:T(8,128)S(1)}, f32[256,512]{1,0:T(8,128)}, u32[]{:S(2)}) copy-start(f32[256,512]{1,0:T(8,128)} %get-tuple-element.32.refs_0_) | copy-start | bytes 1572868

commit v3 on v2

--- a/solution.py
+++ b/solution.py
@@ -14,6 +14,7 @@
 CAP = 2
 F32 = jnp.float32
 BF16 = jnp.bfloat16
+TINY = pl.CostEstimate(flops=1, bytes_accessed=1, transcendentals=0)
 
 
 def rotate(values, positions):
@@ -148,6 +149,7 @@
         norm_kernel,
         out_shape=(half, half),
         compiler_params=pltpu.CompilerParams(vmem_limit_bytes=16 << 20),
+        cost_estimate=TINY,
         name="norm_split",
     )(states)
 
@@ -170,22 +172,26 @@
         copy.wait()
 
 
-def cut(sources, plan, shapes, gates=(), near=False):
-    args = [*sources, *jax.tree.leaves(gates)]
+def cut(sources, plan, shapes, gates=(), near=False, limit=58):
+    gates = jax.tree.leaves(gates)
+    args = [*sources, *gates]
     hbm = pl.BlockSpec(memory_space=pltpu.HBM)
     vmem = pl.BlockSpec(memory_space=pltpu.VMEM)
+    anywhere = pl.BlockSpec(memory_space=pl.ANY)
     return pl.pallas_call(
         functools.partial(cut_kernel, plan, len(args)),
-        in_specs=[vmem if near else hbm] * len(args),
+        in_specs=[vmem if near else hbm] * len(sources) + [anywhere] * len(gates),
         out_specs=[hbm if near else vmem] * len(shapes),
         out_shape=[jax.ShapeDtypeStruct(shape, BF16) for shape in shapes],
         scratch_shapes=[pltpu.SemaphoreType.DMA((sum(len(p) for p in plan),))],
-        compiler_params=pltpu.CompilerParams(vmem_limit_bytes=8 << 20),
+        compiler_params=pltpu.CompilerParams(vmem_limit_bytes=limit << 20),
+        cost_estimate=TINY,
         name="cut",
     )(*args)
 
 
-def relay_kernel(own, two, up, down, sems):
+def relay_kernel(own, two, *refs):
+    up, down, sems = refs[-3:]
     me = lax.axis_index("ctx")
 
     def moves(act):
@@ -200,17 +206,18 @@
     moves(lambda c: c.wait())
 
 
-def relay(own, two):
+def relay(own, two, gates):
     hbm = pl.BlockSpec(memory_space=pltpu.HBM)
     out = jax.ShapeDtypeStruct(own.shape, BF16)
     return pl.pallas_call(
         relay_kernel,
-        in_specs=[hbm] * 2,
+        in_specs=[hbm] * 2 + [pl.BlockSpec(memory_space=pl.ANY)] * len(gates),
         out_shape=(out, out),
         scratch_shapes=[pltpu.SemaphoreType.DMA((2,))],
         compiler_params=pltpu.CompilerParams(vmem_limit_bytes=4 << 20),
+        cost_estimate=TINY,
         name="relay",
-    )(own, two)
+    )(own, two, *gates)
 
 
 def sort_kernel(blocks_ref, places_ref, *refs):
@@ -226,14 +233,15 @@
 
 
 def sort_blocks(blocks, places, gates):
-    hbm = pl.BlockSpec(memory_space=pltpu.HBM)
+    anywhere = pl.BlockSpec(memory_space=pl.ANY)
     count, size, _ = blocks.shape
     return pl.pallas_call(
         sort_kernel,
         in_specs=[pl.BlockSpec(memory_space=pltpu.VMEM), pl.BlockSpec(memory_space=pltpu.SMEM)]
-        + [hbm] * len(gates),
+        + [anywhere] * len(gates),
         out_shape=jax.ShapeDtypeStruct((KVH, places.shape[0] * size, 2 * HD), BF16),
         compiler_params=pltpu.CompilerParams(vmem_limit_bytes=4 << 20),
+        cost_estimate=TINY,
         name="sort_blocks",
     )(blocks, places, *gates)
 
@@ -249,102 +257,176 @@
         sib[here, cols] = total[(2 * z + 1) * rows : (2 * z + 2) * rows]
 
 
-def project_kernel(shards, slices, chunks, n_weights, started, n_gates, *refs):
-    a_refs, w_refs = refs[:5], refs[5 : 5 + n_weights]
-    refs = refs[5 + n_weights :]
-    before = refs[0] if started else None
-    outs = refs[started + n_gates : -5]
-    a_buf, w_buf, acc, a_sems, w_sems = refs[-5:]
+def load_rows_kernel(*refs):
+    parts, out_ref, sems = refs[:5], refs[-2], refs[-1]
     me = lax.axis_index("ctx")
-    depth = a_buf.shape[2]
-    rows = a_buf.shape[1] // shards
-
-    def row_copies(index, act):
-        cols = pl.ds(slices[index] * depth, depth)
+    rows = parts[0].shape[0]
+
+    def copies(act):
         for k in range(4):
             start = pl.multiple_of(lax.bitwise_xor(me, k) * rows, rows)
-            target = a_buf.at[index, pl.ds(start, rows)]
-            sem = a_sems.at[index * 4 + k]
+            target = out_ref.at[pl.ds(start, rows)]
             if k < 3:
-                act(pltpu.make_async_copy(a_refs[k].at[:, cols], target, sem))
+                act(pltpu.make_async_copy(parts[k], target, sems.at[k]))
             else:
-                for source, chosen in ((a_refs[3], me >= 2), (a_refs[4], me < 2)):
+                for source, chosen in ((parts[3], me >= 2), (parts[4], me < 2)):
 
                     @pl.when(chosen)
                     def _():
-                        act(pltpu.make_async_copy(source.at[:, cols], target, sem))
-
-    weight_copies = {}
-    count = 0
-    for index in range(len(slices)):
-        row_copies(index, lambda c: c.start())
-        for c, (_, pieces) in enumerate(chunks):
-            if index >= len(pieces):
-                continue
-            here, row_to = [], 0
-            for ref, row, col, size in pieces[index]:
-                here.append(
-                    pltpu.make_async_copy(
-                        w_refs[ref].at[pl.ds(row, size), pl.ds(col, STEP)],
-                        w_buf.at[c, index, pl.ds(row_to, size)],
-                        w_sems.at[count],
-                    )
-                )
-                here[-1].start()
-                row_to += size
-                count += 1
-            weight_copies[c, index] = here
-    for index in range(len(slices)):
-        row_copies(index, lambda c: c.wait())
-        for c, (place, pieces) in enumerate(chunks):
-            if index >= len(pieces):
-                continue
-            for copy in weight_copies[c, index]:
-                copy.wait()
-            part = jnp.dot(a_buf[index], w_buf[c, index], preferred_element_type=F32)
-            if index > 0:
-                part += acc[c]
-            elif started:
-                part += before[:, c * STEP : (c + 1) * STEP]
-            if index < len(pieces) - 1:
-                acc[c] = part
-            elif place[1] is None:
-                outs[place[0]][:, place[2]] = part
-            else:
-                share(part, shards, outs[place[0]], outs[place[1]], place[2])
-
-
-def project(shard_rows, weights, slices, chunks, outs, before=None, gates=()):
-    rows, width = shard_rows[0].shape
-    depth = width // 4
-    shards = 4
-    hbm = pl.BlockSpec(memory_space=pltpu.HBM)
+                        act(pltpu.make_async_copy(source, target, sems.at[k]))
+
+    copies(lambda c: c.start())
+    copies(lambda c: c.wait())
+
+
+def load_rows(parts, gate):
+    rows, width = parts[0].shape
+    return pl.pallas_call(
+        load_rows_kernel,
+        in_specs=[pl.BlockSpec(memory_space=pltpu.HBM)] * 5 + [pl.BlockSpec(memory_space=pl.ANY)],
+        out_shape=jax.ShapeDtypeStruct((4 * rows, width), BF16),
+        scratch_shapes=[pltpu.SemaphoreType.DMA((4,))],
+        compiler_params=pltpu.CompilerParams(vmem_limit_bytes=12 << 20),
+        cost_estimate=TINY,
+        name="load_rows",
+    )(*parts, gate)
+
+
+def load_weights_kernel(kv, q, first_x, first_y, last_x, last_y, out_ref, token, sems):
+    depth = kv.shape[0]
+    copies = []
+    for r, sources in enumerate(((kv, q), (first_x, last_x), (first_y, last_y))):
+        col = 0
+        for source in sources:
+            width = source.shape[1]
+            target = out_ref.at[pl.ds(r * depth, depth), pl.ds(col, width)]
+            copies.append(pltpu.make_async_copy(source, target, sems.at[len(copies)]))
+            col += width
+    for copy in copies:
+        copy.start()
+    token[...] = jnp.zeros(token.shape, F32)
+    for copy in copies:
+        copy.wait()
+
+
+def load_weights(*parts):
+    depth = parts[0].shape[0]
+    cols = parts[0].shape[1] + parts[1].shape[1]
+    return pl.pallas_call(
+        load_weights_kernel,
+        in_specs=[pl.BlockSpec(memory_space=pltpu.HBM)] * 6,
+        out_shape=(
+            jax.ShapeDtypeStruct((3 * depth, cols), BF16),
+            jax.ShapeDtypeStruct((8, HD), F32),
+        ),
+        scratch_shapes=[pltpu.SemaphoreType.DMA((6,))],
+        compiler_params=pltpu.CompilerParams(vmem_limit_bytes=16 << 20),
+        cost_estimate=TINY,
+        name="load_weights",
+    )(*parts)
+
+
+def gather_kernel(asked_ref, store_ref, *refs):
+    out_ref, sems = refs[-2:]
+    count = asked_ref.shape[0]
+    copies = [
+        pltpu.make_async_copy(store_ref.at[asked_ref[i]], out_ref.at[i], sems.at[i])
+        for i in range(count)
+    ]
+    for copy in copies:
+        copy.start()
+    for copy in copies:
+        copy.wait()
+
+
+def gather_blocks(asked, store_kv, gate):
+    return pl.pallas_call(
+        gather_kernel,
+        in_specs=[
+            pl.BlockSpec(memory_space=pltpu.SMEM),
+            pl.BlockSpec(memory_space=pltpu.HBM),
+            pl.BlockSpec(memory_space=pl.ANY),
+        ],
+        out_shape=jax.ShapeDtypeStruct(asked.shape + store_kv.shape[1:], BF16),
+        scratch_shapes=[pltpu.SemaphoreType.DMA(asked.shape)],
+        compiler_params=pltpu.CompilerParams(vmem_limit_bytes=4 << 20),
+        cost_estimate=TINY,
+        name="gather_blocks",
+    )(asked, store_kv, gate)
+
+
+def multiply(a_ref, w_ref, d_x, d_y, col, near):
+    depth = w_ref.shape[0] // 3
+    total = 0.0
+    for r in range(3):
+        total += jnp.dot(
+            a_ref[:, r * depth : (r + 1) * depth],
+            w_ref[r * depth : (r + 1) * depth, col : col + STEP],
+            preferred_element_type=F32,
+        )
+    if d_x is None:
+        return total
+    return total + diagonal_part(a_ref, d_x, d_y, near)
+
+
+def diagonal_part(a_ref, d_x, d_y, near):
+    h = d_x.shape[0]
+    part = jnp.dot(a_ref[:, 6 * h : 7 * h], d_x[:, near : near + STEP], preferred_element_type=F32)
+    return part + jnp.dot(a_ref[:, 7 * h :], d_y[:, near : near + STEP], preferred_element_type=F32)
+
+
+def project_kv_kernel(a_ref, w_ref, d_x, d_y, own, sib):
+    share(multiply(a_ref, w_ref, d_x, d_y, 0, 0), 4, own, sib, slice(0, STEP))
+
+
+def project_q_kernel(kv_cols, a_ref, w_ref, d_x, d_y, *refs):
+    own, sib, rest = refs[-3:]
+    early = own.shape[1]
+    for col in range(0, early, STEP):
+        total = multiply(a_ref, w_ref, d_x, d_y, kv_cols + col, kv_cols + col)
+        share(total, 4, own, sib, slice(col, col + STEP))
+    for col in range(0, rest.shape[1], STEP):
+        rest[:, col : col + STEP] = multiply(a_ref, w_ref, None, None, kv_cols + early + col, 0)
+
+
+def project_last_kernel(a_ref, d_x, d_y, rest, *refs):
+    own, sib = refs[-2:]
+    for col in range(0, rest.shape[1], STEP):
+        total = rest[:, col : col + STEP] + diagonal_part(a_ref, d_x, d_y, col)
+        share(total, 4, own, sib, slice(col, col + STEP))
+
+
+def project(kernel, near, gates, outs, limit, work):
     vmem = pl.BlockSpec(memory_space=pltpu.VMEM)
-    started = before is not None
-    args = [*shard_rows, *weights, *([before] if started else []), *gates]
-    n_weight_copies = sum(len(p) for _, pieces in chunks for p in pieces)
-    work = sum(len(pieces) for _, pieces in chunks)
-    return pl.pallas_call(
-        functools.partial(
-            project_kernel, shards, slices, chunks, len(weights), started, len(gates)
-        ),
-        in_specs=[hbm] * (5 + len(weights)) + [vmem] * started + [hbm] * len(gates),
+    return pl.pallas_call(
+        kernel,
+        in_specs=[vmem] * len(near) + [pl.BlockSpec(memory_space=pl.ANY)] * len(gates),
         out_shape=[jax.ShapeDtypeStruct(shape, F32) for shape in outs],
-        scratch_shapes=[
-            pltpu.VMEM((len(slices), shards * rows, depth), BF16),
-            pltpu.VMEM((len(chunks), len(slices), depth, STEP), BF16),
-            pltpu.VMEM((len(chunks), shards * rows, STEP), F32),
-            pltpu.SemaphoreType.DMA((4 * len(slices),)),
-            pltpu.SemaphoreType.DMA((n_weight_copies,)),
-        ],
-        compiler_params=pltpu.CompilerParams(vmem_limit_bytes=58 << 20),
-        cost_estimate=pl.CostEstimate(
-            flops=2 * shards * rows * depth * STEP * work,
-            bytes_accessed=8 * rows * width,
-            transcendentals=0,
-        ),
+        compiler_params=pltpu.CompilerParams(vmem_limit_bytes=limit << 20),
+        cost_estimate=TINY,
         name="project",
-    )(*args)
+    )(*near, *gates)
+
+
+def fresh_kernel(own, sib, fresh_ref, first_ref, second_ref):
+    me = lax.axis_index("ctx")
+    fresh = own[...] + sib[...]
+    low, high = fresh[:, :HD], fresh[:, HD:]
+    fresh_ref[...] = fresh.astype(BF16)
+    first_ref[...] = jnp.where(me == 0, high, low).astype(BF16)
+    second_ref[...] = jnp.where(me == 3, low, high).astype(BF16)
+
+
+def make_fresh(own, sib):
+    rows = own.shape[0]
+    out = lambda cols: jax.ShapeDtypeStruct((rows, cols), BF16)
+    return pl.pallas_call(
+        fresh_kernel,
+        out_shape=(out(2 * HD), out(HD), out(HD)),
+        compiler_params=pltpu.CompilerParams(vmem_limit_bytes=4 << 20),
+        cost_estimate=TINY,
+        name="fresh",
+    )(own, sib)
 
 
 def turn(values, cosine, sine):
@@ -379,6 +461,7 @@
             jax.ShapeDtypeStruct((HD, context), BF16),
         ),
         compiler_params=pltpu.CompilerParams(vmem_limit_bytes=16 << 20),
+        cost_estimate=TINY,
         name="assemble",
     )(fresh, first, second, cached, cosine, sine, targets)
 
@@ -418,6 +501,7 @@
         out_shape=jax.ShapeDtypeStruct((rec_count, width), BF16),
         input_output_aliases=aliases,
         compiler_params=pltpu.CompilerParams(vmem_limit_bytes=16 << 20),
+        cost_estimate=TINY,
         name="attend",
     )(*args)
 
@@ -444,17 +528,23 @@
     first_cols = kv_cols + early
     half = depth // 2
 
+    asked, places = swap_ids(block_slot[0], block_owner[0], store_count)
     (w_first,) = cut(
         (w_keyval, w_query),
         [[(0, (0, 0), (0, 0), (depth, kv_cols)), (1, (0, 0), (0, kv_cols), (depth, early))]],
         [(depth, first_cols)],
+        (asked,),
     )
     first_x, first_y = by_x(w_first), by_y(w_first)
-    asked, places = swap_ids(block_slot[0], block_owner[0], store_count)
+    gathered = gather_blocks(asked.reshape(-1), store_kv, w_first)
+    arrived = lax.all_to_all(gathered, "store", split_axis=0, concat_axis=0, tiled=True)
     (w_last,) = cut(
-        (w_query,), [[(0, (0, early), (0, 0), (depth, late))]], [(depth, late)], (asked,)
+        (w_query,), [[(0, (0, early), (0, 0), (depth, late))]], [(depth, late)], (arrived, first_x, first_y)
     )
     last_x, last_y = by_x(w_last), by_y(w_last)
+    by_head = sort_blocks(arrived, places, (w_last,))
+    cached = lax.all_to_all(by_head, "ctx", split_axis=0, concat_axis=0, tiled=True)
+    cached = cached.reshape(-1, 2 * HD)
 
     keep, send = norm_split(states[0])
     shard, width = keep.shape
@@ -467,7 +557,7 @@
     along = lambda a, pairs: lax.ppermute(a, "ctx", pairs)
     two = along(both, [(0, 2), (1, 3), (2, 0), (3, 1)])
     one = along(both, [(0, 1), (1, 0), (2, 3), (3, 2)])
-    up, down = relay(both, two)
+    up, down = relay(both, two, (one, cached))
     shard_parts = (
         both,
         one,
@@ -476,25 +566,22 @@
         along(down, [(2, 1), (1, 0)]),
     )
 
-    def diagonal(from_x, from_y):
+    def diagonal(from_x, from_y, gates, limit):
         cols = from_x.shape[1]
-        to_x, to_y = cut(
+        sent = cut(
             (from_y, from_x),
             [[(0, (0, 0), (0, 0), (half, cols))], [(1, (half, 0), (0, 0), (half, cols))]],
             [(half, cols)] * 2,
+            gates,
+            limit=limit,
         )
-        return (by_x(to_x), by_y(to_y)), to_x
-
-    diag_first, _ = diagonal(first_x, first_y)
-    diag_last, sent_last = diagonal(last_x, last_y)
-
-    arrived = lax.all_to_all(store_kv[asked], "store", split_axis=0, concat_axis=0, tiled=True)
+        return (by_x(sent[0]), by_y(sent[1])), sent[0]
+
+    diag_first, _ = diagonal(first_x, first_y, (up, last_x, last_y), 8)
+    weights, loaded = load_weights(w_keyval, w_query, first_x, first_y, last_x, last_y)
+    diag_last, sent_last = diagonal(last_x, last_y, (loaded,), 6)
+
     shard_rows = block_count * piece_rows
-    arrived = arrived.reshape((-1,) + store_kv.shape[1:])
-    by_head = sort_blocks(arrived, places, (up, sent_last))
-    cached = lax.all_to_all(by_head, "ctx", split_axis=0, concat_axis=0, tiled=True)
-    cached = cached.reshape(ctx_count * shard_rows, 2 * HD)
-
     frequency = jnp.exp(
         jnp.arange(HD // 2, dtype=F32) * (-2.0 * math.log(500000.0) / HD)
     )
@@ -516,34 +603,26 @@
         + row_ids % piece_rows
     )
 
-    def pieces(own, own_col, near, col):
-        whole = [[(own, 0, own_col, depth)], [(near, 0, col, depth)], [(near + 1, 0, col, depth)]]
-        return whole, whole + [[(near + 2, 0, col, half), (near + 3, 0, col, half)]]
-
+    rows = load_rows(shard_parts, sent_last)
     kv_own, kv_sib = project(
-        shard_parts,
-        (w_keyval, first_x, first_y, *diag_first),
-        (0, 1, 2, 3),
-        [((0, 1, slice(0, STEP)), pieces(0, 0, 1, 0)[1])],
+        project_kv_kernel,
+        (rows, weights, *diag_first),
+        (),
         [(rec_count, kv_cols)] * 2,
-    )
-    chunks = []
-    for col in range(0, early, STEP):
-        chunks.append(((0, 1, slice(col, col + STEP)), pieces(0, col, 1, kv_cols + col)[1]))
-    for col in range(0, late, STEP):
-        chunks.append(((2, None, slice(col, col + STEP)), pieces(0, early + col, 5, col)[0]))
+        20,
+        2 * rows.size * kv_cols,
+    )
+    fresh, to_first, to_second = make_fresh(kv_own, by_core(kv_sib))
+    first = along(to_first, [(0, 1), (1, 2), (2, 0)])
+    second = along(to_second, [(1, 3), (2, 1), (3, 2)])
     early_own, early_sib, rest = project(
-        shard_parts,
-        (w_query, first_x, first_y, *diag_first, last_x, last_y),
-        (0, 1, 2, 3),
-        chunks,
+        functools.partial(project_q_kernel, kv_cols),
+        (rows, weights, *diag_first),
+        (to_first,),
         [(rec_count, early)] * 2 + [(2 * rec_count, late)],
-        gates=(kv_sib,),
-    )
-    fresh = (kv_own + by_core(kv_sib)).astype(BF16)
-    low, high = fresh[:, :HD], fresh[:, HD:]
-    first = along(jnp.where(my_index == 0, high, low), [(0, 1), (1, 2), (2, 0)])
-    second = along(jnp.where(my_index == 3, low, high), [(1, 3), (2, 1), (3, 2)])
+        22,
+        2 * rows.size * query_cols,
+    )
     key_rows, value_rows = assemble(
         fresh, first, second, cached, cosine, sine, targets.reshape(1, rec_count)
     )
@@ -557,15 +636,12 @@
     )
     result = attend(early_own, by_core(early_sib), shared, query_cols, 0, None)
     own, sib = project(
-        shard_parts,
-        diag_last,
-        (3,),
-        [
-            ((0, 1, slice(col, col + STEP)), [[(0, 0, col, half), (1, 0, col, half)]])
-            for col in range(0, late, STEP)
-        ],
+        project_last_kernel,
+        (rows, *diag_last, rest),
+        (first, second, cached),
         [(rec_count, late)] * 2,
-        before=rest,
+        12,
+        rows.size * late // 2,
     )
     result = attend(own, by_core(sib), shared, query_cols, early, result)
     return result.reshape(1, rec_count, query_cols)

time: 146 us -> 130 us (0.89)
  starting transfers between devices: 33.8 us -> 23.2 us
  Pallas kernels: 37.1 us -> 28.1 us
  waiting for transfers between devices: 27.6 us -> 30.8 us
    all_to_all x0 -> x1, blocking collectives: none -> 23 us  [fast_body(): lax.all_to_all(gathered, 'store', split_axis=0, concat_axis=0, tiled=True)]
    all_to_all x1, blocking collectives: 32.2 us -> 9.73 us  [swap_ids(): lax.all_to_all(wanted, 'store', split_axis=0, concat_axis=0, tiled=True)]
    pallas_call x4 -> x8, Pallas kernels: 24 us -> 12.2 us  [the longest x3 5.9 us: project(): pl.pallas_call(kernel, in_specs=[vmem] * len(near) + [pl.BlockSpec(memory...]
    ppermute x6, waiting for transfers between devices: 11.3 us -> 21 us  [fast_body(): along = lambda a, pairs: lax.ppermute(a, 'ctx', pairs)]
    ppermute x4, waiting for transfers between devices: 6.73 us -> 0.91 us  [fast_body(): by_x = lambda a: lax.ppermute(a, 'store', xf)]
    ppermute x4, waiting for transfers between devices: 5.84 us -> 0.68 us  [fast_body(): by_y = lambda a: lax.ppermute(a, 'store', yf)]
    all_to_all x1, waiting for transfers between devices: 0.01 us -> 4.73 us  [fast_body(): lax.all_to_all(by_head, 'ctx', split_axis=0, concat_axis=0, tiled=True)]
    all_to_all x1 -> x0, waiting for transfers between devices: 3.73 us -> none  [fast_body(): lax.all_to_all(store_kv[asked], 'store', split_axis=0, concat_axis=0, til...]
  transfers between devices with their start and end apart: 20 -> 19, of which waited for: 5 -> 8; matrix products, arithmetic and copies ran while one was open for 3% -> 2% of each run, Pallas kernels for 23% -> 17%
where the time goes in v3:
time: 130 us; the launch traced here: 129 us
  blocking collectives  32.8 us (25%)
  waiting for transfers between devices  30.8 us (24%)
  Pallas kernels  28.1 us (22%)
  starting transfers between devices  23.2 us (18%)
  local copies, waits for them, and re-layouts  10.2 us (8%)
  other arithmetic  3.83 us (3%)
    all_to_all x1, blocking collectives, fast_body(): lax.all_to_all(gathered, 'store', split_axis=0, concat_axis=0, tiled=True)  23 us
    ppermute x6, waiting for transfers between devices, fast_body(): along = lambda a, pairs: lax.ppermute(a, 'ctx', pairs)  21 us
    ppermute x6, starting transfers between devices, fast_body(): along = lambda a, pairs: lax.ppermute(a, 'ctx', pairs)  9.87 us
    all_to_all x1, blocking collectives, swap_ids(): lax.all_to_all(wanted, 'store', split_axis=0, concat_axis=0, tiled=True)  9.73 us
    unnamed x38, local copies, waits for them, and re-layouts  9.56 us
    pallas_call x5, Pallas kernels, cut(): pl.pallas_call(functools.partial(cut_kernel, plan, len(args)), in_specs=[...  8.5 us
    pallas_call x2, Pallas kernels, attend(): pl.pallas_call(functools.partial(attend_kernel, cols // HD), grid=(1,), i...  5.93 us
    pallas_call x3, Pallas kernels, project(): pl.pallas_call(kernel, in_specs=[vmem] * len(near) + [pl.BlockSpec(memory...  5.9 us
  transfers between devices with their start and end apart: 19, of which 8 were waited for; matrix products, arithmetic and copies ran while one was open for 2% of the time, Pallas kernels for 17%

profile of v3, /device:TPU:0, one launch (start us, length us, event | category | flops | bytes accessed | tf_op | source)
XLA Modules:
  0.0 129.3 jit_solution(6417624870698339827)
XLA Ops:
  0.0 0.9 convert_reduce_fusion
  0.9 0.7 iota_compare_fusion.1
  1.6 0.8 select_reduce_fusion
  2.4 0.1 copy.16
  2.5 9.7 %all_to_all.21 = s32[8,1,2]{2,1,0:T(1,128)} all-to-all(s32[8,1,2]{2,1,0:T(1,128)S(1)} %copy.16), channel_id=1, replica_groups=mesh['store'=8,'ctx'=4] {'store'}, dimensions={0} | all-to-all | bytes 128 | tf_op jit(solution)/shard_map/all_to_all | solution.py:51
  12.2 2.7 %cut.6.refs_0_ = bf16[1024,768]{1,0:T(8,128)(2,1)} custom-call(bf16[1024,256]{1,0:T(8,128)(2,1)} %kv.1, bf16[1024,1024]{1,0:T(8,128)(2,1)} %q.1, s32[8,2]{1,0:T(8,128)} %bitcast.13), custom_call_target="tpu_custom_call" | custom-call | flops 1 | bytes 1 | tf_op jit(solution)/shard_map/cut/pallas_call | solution.py:181
  14.9 0.6 collective-permute-start.3
  15.5 0.6 collective-permute-start.4
  16.1 0.4 norm_split.1
  16.5 0.8 copy-done.14
  17.3 1.9 %collective-permute-done.refs_1_ = bf16[64,4096]{1,0:T(8,128)(2,1)S(1)} collective-permute-done((bf16[64,4096]{1,0:T(8,128)(2,1)S(1)}, bf16[64,4096]{1,0:T(8,128)(2,1)S(1)}, u32[]{:S(2)}, u32[]{:S(2)}) %collective-permute-start) | collective-permute-done | bytes 524320 | tf_op jit(solution)/shard_map/ppermute | solution.py:522
  19.2 0.8 copy-done.16
  20.0 2.2 %cut.5.own.refs_0_ = bf16[128,4096]{1,0:T(8,128)(2,1)} custom-call(bf16[64,4096]{1,0:T(8,128)(2,1)} %copy-done.14, bf16[64,4096]{1,0:T(8,128)(2,1)} %copy-done.16), custom_call_target="tpu_custom_call" | custom-call | flops 1 | bytes 1 | tf_op jit(solution)/shard_map/cut/pallas_call | solution.py:181
  22.2 1.6 %collective-permute-start.1 = (bf16[128,4096]{1,0:T(8,128)(2,1)}, bf16[128,4096]{1,0:T(8,128)(2,1)}, u32[]{:S(2)}, u32[]{:S(2)}) collective-permute-start(bf16[128,4096]{1,0:T(8,128)(2,1)} %cut.5.own.refs_0_), channel_id=1, source_target_pairs={{0,1},{1,0},{2,3},{3,2},{4,5},{5,4},{6,7},{7,6},{8,9},{9,8},{10,11... | collective-permute-start | bytes 3145736 | tf_op jit(solution)/shard_map/ppermute | solution.py:557
  23.9 2.6 %collective-permute-start.2 = (bf16[128,4096]{1,0:T(8,128)(2,1)}, bf16[128,4096]{1,0:T(8,128)(2,1)}, u32[]{:S(2)}, u32[]{:S(2)}) collective-permute-start(bf16[128,4096]{1,0:T(8,128)(2,1)} %cut.5.own.refs_0_), channel_id=1, source_target_pairs={{0,2},{1,3},{2,0},{3,1},{4,6},{5,7},{6,4},{7,5},{8,10},{9,11},{10,... | collective-permute-start | bytes 3145736 | tf_op jit(solution)/shard_map/ppermute | solution.py:557
  26.5 0.5 broadcast.250
  27.0 0.7 reduce.3
  27.7 0.1 reshape.203.asked_ref
  27.7 1.4 %copy-done.7 = bf16[1024,768]{1,0:T(8,128)(2,1)S(1)} copy-done((bf16[1024,768]{1,0:T(8,128)(2,1)S(1)}, bf16[1024,768]{1,0:T(8,128)(2,1)}, u32[]{:S(2)}) %copy-start.7) | copy-done | bytes 1572888
  29.1 1.0 copy-done.13
  30.2 1.1 gather_blocks.1
  31.3 23.0 %all_to_all.22.refs_1_.blocks_ref = bf16[16,8,1024]{2,1,0:T(8,128)(2,1)} all-to-all(bf16[16,8,1024]{2,1,0:T(8,128)(2,1)S(1)} %gather_blocks.1), channel_id=1, replica_groups=mesh['store'=8,'ctx'=4] {'store'}, dimensions={0} | all-to-all | bytes 524288 | tf_op jit(solution)/shard_map/all_to_all | solution.py:540
  54.3 1.1 copy-done.1
  55.5 1.2 copy-done.3
  56.7 2.2 %cut.7.refs_0_ = bf16[1024,512]{1,0:T(8,128)(2,1)} custom-call(bf16[1024,1024]{1,0:T(8,128)(2,1)} %q.1, bf16[16,8,1024]{2,1,0:T(8,128)(2,1)} %all_to_all.22.refs_1_.blocks_ref, bf16[1024,768]{1,0:T(8,128)(2,1)} %copy-done.1, bf16[1024,768]{1,0:T(8,128)(2,1)} %copy-done.3), custom_call_target="tpu_custom_call" | custom-call | flops 1 | bytes 1 | tf_op jit(solution)/shard_map/cut/pallas_call | solution.py:181
  58.9 1.2 collective-permute-start.7
  60.1 0.8 collective-permute-start.8
  61.0 1.2 copy-done.8
  62.2 0.6 sort_blocks.1
  62.8 0.7 copy-done.12
  63.5 5.1 %all-to-all-start.2 = ((bf16[4,128,256]{2,1,0:T(8,128)(2,1)}), bf16[4,128,256]{2,1,0:T(8,128)(2,1)S(1)}, u32[]{:S(2)}, u32[]{:S(2)}) async-start(bf16[4,128,256]{2,1,0:T(8,128)(2,1)} %copy-done.12), calls=%async_computation.2 | async-start | bytes 524288 | tf_op jit(solution)/shard_map/all_to_all | solution.py:546
  68.6 1.5 %collective-permute-done.1.refs_0_.refs_1_ = bf16[128,4096]{1,0:T(8,128)(2,1)} collective-permute-done((bf16[128,4096]{1,0:T(8,128)(2,1)}, bf16[128,4096]{1,0:T(8,128)(2,1)}, u32[]{:S(2)}, u32[]{:S(2)}) %collective-permute-start.1) | collective-permute-done | bytes 1048608 | tf_op jit(solution)/shard_map/ppermute | solution.py:557
  70.2 3.2 %collective-permute-done.2.two.refs_2_ = bf16[128,4096]{1,0:T(8,128)(2,1)} collective-permute-done((bf16[128,4096]{1,0:T(8,128)(2,1)}, bf16[128,4096]{1,0:T(8,128)(2,1)}, u32[]{:S(2)}, u32[]{:S(2)}) %collective-permute-start.2) | collective-permute-done | bytes 1048608 | tf_op jit(solution)/shard_map/ppermute | solution.py:557
  73.3 4.7 %all-to-all-done.2 = bf16[4,128,256]{2,1,0:T(8,128)(2,1)S(1)} async-done(((bf16[4,128,256]{2,1,0:T(8,128)(2,1)}), bf16[4,128,256]{2,1,0:T(8,128)(2,1)S(1)}, u32[]{:S(2)}, u32[]{:S(2)}) %all-to-all-start.2) | async-done | bytes 262176 | tf_op jit(solution)/shard_map/all_to_all | solution.py:546
  78.1 1.2 copy-done.5
  79.3 1.6 %relay.1 = (bf16[128,4096]{1,0:T(8,128)(2,1)S(1)}, bf16[128,4096]{1,0:T(8,128)(2,1)S(1)}) custom-call(bf16[128,4096]{1,0:T(8,128)(2,1)S(1)} %copy-done.5, bf16[128,4096]{1,0:T(8,128)(2,1)} %collective-permute-done.2.two.refs_2_, bf16[128,4096]{1,0:T(8,128)(2,1)} %collective-permute-done.1.refs_0_.refs_1_, bf16[512,256]{1,0:T(8,128)(2,1)S(1)} %bitcast.9), custom_call_target="tpu_custom_call" | custom-call | flops 1 | bytes 1 | tf_op jit(solution)/shard_map/relay/pallas_call | solution.py:212
  80.9 0.7 collective-permute-start.5
  81.6 1.4 %collective-permute-start.6 = (bf16[128,4096]{1,0:T(8,128)(2,1)S(1)}, bf16[128,4096]{1,0:T(8,128)(2,1)S(1)}, u32[]{:S(2)}, u32[]{:S(2)}) collective-permute-start(bf16[128,4096]{1,0:T(8,128)(2,1)S(1)} %get-tuple-element.30), channel_id=1, source_target_pairs={{2,1},{1,0},{6,5},{5,4},{10,9},{9,8},{14,13},{13,12},{18,17},{17,1... | collective-permute-start | bytes 3145736 | tf_op jit(solution)/shard_map/ppermute | solution.py:557
  83.1 0.7 collective-permute-done.7.last_y.refs_0_.refs_4_
  83.7 0.9 collective-permute-done.8.last_x.refs_1_.refs_3_
  84.6 0.1 cut.9
  84.8 1.3 collective-permute-start.11
  86.0 1.5 %collective-permute-start.12 = (bf16[512,768]{1,0:T(8,128)(2,1)S(1)}, bf16[512,768]{1,0:T(8,128)(2,1)S(1)}, u32[]{:S(2)}, u32[]{:S(2)}) collective-permute-start(bf16[512,768]{1,0:T(8,128)(2,1)S(1)} %get-tuple-element.36), channel_id=1, source_target_pairs={{0,16},{4,20},{8,24},{12,28},{16,0},{20,4},{24,8},{28,12},{1,17},{... | collective-permute-start | bytes 2359304 | tf_op jit(solution)/shard_map/ppermute | solution.py:521
  87.5 2.0 %load_weights.1 = (bf16[3072,1280]{1,0:T(8,128)(2,1)S(1)}, f32[8,128]{1,0:T(8,128)S(1)}) custom-call(bf16[1024,256]{1,0:T(8,128)(2,1)S(1)} %copy-done.10, bf16[1024,1024]{1,0:T(8,128)(2,1)S(1)} %copy-done, bf16[1024,768]{1,0:T(8,128)(2,1)S(1)} %copy-done.2, bf16[1024,768]{1,0:T(8,128)(2,1)S(1)} %copy-done.4, ...), custom_call_target="tpu_custom_call" | custom-call | flops 1 | bytes 1 | tf_op jit(solution)/shard_map/load_weights/pallas_call | solution.py:315
  89.5 1.3 %cut.8 = (bf16[512,512]{1,0:T(8,128)(2,1)S(1)}, bf16[512,512]{1,0:T(8,128)(2,1)S(1)}) custom-call(bf16[1024,512]{1,0:T(8,128)(2,1)} %collective-permute-done.7.last_y.refs_0_.refs_4_, bf16[1024,512]{1,0:T(8,128)(2,1)} %collective-permute-done.8.last_x.refs_1_.refs_3_, f32[8,128]{1,0:T(8,128)S(1)} %get-tuple-element.31.refs_2_), custom_call_target="tpu_custom_call" | custom-call | flops 1 | bytes 1 | tf_op jit(solution)/shard_map/cut/pallas_call | solution.py:181
  90.9 0.6 collective-permute-start.10
  91.5 0.8 collective-permute-start.9
  92.3 16.3 %collective-permute-done.6.refs_4_ = bf16[128,4096]{1,0:T(8,128)(2,1)S(1)} collective-permute-done((bf16[128,4096]{1,0:T(8,128)(2,1)S(1)}, bf16[128,4096]{1,0:T(8,128)(2,1)S(1)}, u32[]{:S(2)}, u32[]{:S(2)}) %collective-permute-start.6) | collective-permute-done | bytes 1048608 | tf_op jit(solution)/shard_map/ppermute | solution.py:557
  108.7 1.6 %load_rows.1.a_ref = bf16[512,4096]{1,0:T(8,128)(2,1)S(1)} custom-call(bf16[128,4096]{1,0:T(8,128)(2,1)S(1)} %copy-done.6, bf16[128,4096]{1,0:T(8,128)(2,1)} %collective-permute-done.1.refs_0_.refs_1_, bf16[128,4096]{1,0:T(8,128)(2,1)} %collective-permute-done.2.two.refs_2_, bf16[128,4096]{1,0:T(8,128)(2,1)S(1)} %collective-permute-done.5.refs_3_, ...), custom_call_target="tpu_custom_call" | custom-call | flops 1 | bytes 1 | tf_op jit(solution)/shard_map/load_rows/pallas_call | solution.py:284
  110.3 1.2 project.3
  111.6 0.1 collective-permute-start.13
  111.7 1.5 %collective-permute-done.13.sib = f32[256,256]{1,0:T(8,128)S(1)} collective-permute-done((f32[256,256]{1,0:T(8,128)S(1)}, f32[256,256]{1,0:T(8,128)S(1)}, u32[]{:S(2)}, u32[]{:S(2)}) %collective-permute-start.13) | collective-permute-done | bytes 262176 | tf_op jit(solution)/shard_map/ppermute | solution.py:522
  113.2 2.8 %collective-permute-start.14 = (bf16[256,128]{1,0:T(8,128)(2,1)S(1)}, bf16[256,128]{1,0:T(8,128)(2,1)S(1)}, u32[]{:S(2)}, u32[]{:S(2)}) collective-permute-start(bf16[256,128]{1,0:T(8,128)(2,1)S(1)} %get-tuple-element.39.refs_0_), channel_id=1, source_target_pairs={{0,1},{1,2},{2,0},{4,5},{5,6},{6,4},{8,9},{9,10},{10,8},{12,13},{1... | collective-permute-start | bytes 196616 | tf_op jit(solution)/shard_map/ppermute | solution.py:557
  116.1 0.7 collective-permute-start.15
  116.8 3.9 %project.4 = (f32[256,512]{1,0:T(8,128)S(1)}, f32[256,512]{1,0:T(8,128)S(1)}, f32[512,512]{1,0:T(8,128)S(1)}) custom-call(bf16[512,4096]{1,0:T(8,128)(2,1)S(1)} %load_rows.1.a_ref, bf16[3072,1280]{1,0:T(8,128)(2,1)S(1)} %get-tuple-element.34.w_ref, bf16[512,768]{1,0:T(8,128)(2,1)S(1)} %collective-permute-done.11.d_x, ...), custom_call_target="tpu_custom_call" | custom-call | flops 1 | bytes 1 | tf_op jit(solution)/shard_map/project/pallas_call | solution.py:401
  120.7 0.1 collective-permute-start.17
  120.9 0.7 project.5
  121.6 0.5 collective-permute-start.16
  122.1 0.1 fusion.13.refs_7_
  122.2 0.5 fusion.21
  122.8 0.1 pad_maximum_fusion
  122.9 0.4 assemble.1
  123.3 3.0 %attend.2.refs_8_ = bf16[256,1024]{1,0:T(8,128)(2,1)} custom-call(f32[256,512]{1,0:T(8,128)S(1)} %get-tuple-element.47.refs_0_, f32[256,512]{1,0:T(8,128)S(1)} %collective-permute-done.17.refs_1_, bf16[512,128]{1,0:T(8,128)(2,1)S(1)} %get-tuple-element.45.refs_2_, bf16[128,512]{1,0:T(8,128)(2,1)S(1)} %get-tuple-element.46.refs_3_, ...), custom_call_target="tpu_custom_call" | custom-call | flops 1 | bytes 1 | tf_op jit(solution)/shard_map/attend/pallas_call | solution.py:496
  126.3 3.0 %attend.3 = bf16[256,1024]{1,0:T(8,128)(2,1)} custom-call(f32[256,512]{1,0:T(8,128)S(1)} %get-tuple-element.42.refs_0_, f32[256,512]{1,0:T(8,128)S(1)} %collective-permute-done.16.refs_1_, bf16[512,128]{1,0:T(8,128)(2,1)S(1)} %get-tuple-element.45.refs_2_, bf16[128,512]{1,0:T(8,128)(2,1)S(1)} %get-tuple-element.46.refs_3_, ...), custom_call_target="tpu_custom_call", output_to_operand_aliasing={{}: (8, {})} | custom-call | flops 1 | bytes 1 | tf_op jit(solution)/shard_map/attend/pallas_call | solution.py:496
  (46 shorter events, 0.2 us)
Async XLA Ops:
  12.2 3.9 %copy-start.11 = (bf16[1,64,8192]{2,1,0:T(8,128)(2,1)S(1)}, bf16[1,64,8192]{2,1,0:T(8,128)(2,1)}, u32[]{:S(2)}) copy-start(bf16[1,64,8192]{2,1,0:T(8,128)(2,1)} %param.11) | copy-start | bytes 3145732
  14.9 12.1 %copy-start.17 = (s32[8,1,2]{2,1,0:T(1,128)S(1)}, s32[8,1,2]{2,1,0:T(1,128)}, u32[]{:S(2)}) copy-start(s32[8,1,2]{2,1,0:T(1,128)} %all_to_all.21) | copy-start | bytes 196
  14.9 39.4 %collective-permute-start.3 = (bf16[1024,768]{1,0:T(8,128)(2,1)}, bf16[1024,768]{1,0:T(8,128)(2,1)S(1)}, u32[]{:S(2)}, u32[]{:S(2)}) collective-permute-start(bf16[1024,768]{1,0:T(8,128)(2,1)} %cut.6.refs_0_), channel_id=1, source_target_pairs={{0,8},{4,12},{8,0},{12,4},{16,24},{20,28},{24,16},{28,20},{1,9},{5... | collective-permute-start | bytes 4718600 | tf_op jit(solution)/shard_map/ppermute | solution.py:520
  15.5 38.8 %collective-permute-start.4 = (bf16[1024,768]{1,0:T(8,128)(2,1)}, bf16[1024,768]{1,0:T(8,128)(2,1)S(1)}, u32[]{:S(2)}, u32[]{:S(2)}) collective-permute-start(bf16[1024,768]{1,0:T(8,128)(2,1)} %cut.6.refs_0_), channel_id=1, source_target_pairs={{0,16},{4,20},{8,24},{12,28},{16,0},{20,4},{24,8},{28,12},{1,17},{... | collective-permute-start | bytes 4718600 | tf_op jit(solution)/shard_map/ppermute | solution.py:521
  16.5 0.8 copy-start.14
  17.3 1.9 %collective-permute-start = (bf16[64,4096]{1,0:T(8,128)(2,1)S(1)}, bf16[64,4096]{1,0:T(8,128)(2,1)S(1)}, u32[]{:S(2)}, u32[]{:S(2)}) collective-permute-start(bf16[64,4096]{1,0:T(8,128)(2,1)S(1)} %get-tuple-element.28), channel_id=1, source_target_pairs={{0,4},{4,0},{8,12},{12,8},{16,20},{20,16},{24,28},{28,24},{1,5},{5... | collective-permute-start | bytes 1572872 | tf_op jit(solution)/shard_map/ppermute | solution.py:522
  19.2 0.8 copy-start.16
  22.2 47.9 %collective-permute-start.1 = (bf16[128,4096]{1,0:T(8,128)(2,1)}, bf16[128,4096]{1,0:T(8,128)(2,1)}, u32[]{:S(2)}, u32[]{:S(2)}) collective-permute-start(bf16[128,4096]{1,0:T(8,128)(2,1)} %cut.5.own.refs_0_), channel_id=1, source_target_pairs={{0,1},{1,0},{2,3},{3,2},{4,5},{5,4},{6,7},{7,6},{8,9},{9,8},{10,11... | collective-permute-start | bytes 3145736 | tf_op jit(solution)/shard_map/ppermute | solution.py:557
  23.9 49.4 %collective-permute-start.2 = (bf16[128,4096]{1,0:T(8,128)(2,1)}, bf16[128,4096]{1,0:T(8,128)(2,1)}, u32[]{:S(2)}, u32[]{:S(2)}) collective-permute-start(bf16[128,4096]{1,0:T(8,128)(2,1)} %cut.5.own.refs_0_), channel_id=1, source_target_pairs={{0,2},{1,3},{2,0},{3,1},{4,6},{5,7},{6,4},{7,5},{8,10},{9,11},{10,... | collective-permute-start | bytes 3145736 | tf_op jit(solution)/shard_map/ppermute | solution.py:557
  27.7 1.4 %copy-start.7 = (bf16[1024,768]{1,0:T(8,128)(2,1)S(1)}, bf16[1024,768]{1,0:T(8,128)(2,1)}, u32[]{:S(2)}) copy-start(bf16[1024,768]{1,0:T(8,128)(2,1)} %cut.6.refs_0_) | copy-start | bytes 4718596
  29.1 1.0 copy-start.13
  54.3 6.6 %copy-start.18 = (s32[1,16]{1,0:T(1,128)S(1)}, s32[1,16]{1,0:T(1,128)}, u32[]{:S(2)}) copy-start(s32[1,16]{1,0:T(1,128)} %param.9) | copy-start | bytes 196
  54.3 6.7 %copy-start.9 = (bf16[16,8,1024]{2,1,0:T(8,128)(2,1)S(1)}, bf16[16,8,1024]{2,1,0:T(8,128)(2,1)}, u32[]{:S(2)}) copy-start(bf16[16,8,1024]{2,1,0:T(8,128)(2,1)} %all_to_all.22.refs_1_.blocks_ref) | copy-start | bytes 786436
  54.3 1.2 copy-start.1
  55.5 1.2 copy-start.3
  58.9 24.9 %collective-permute-start.7 = (bf16[1024,512]{1,0:T(8,128)(2,1)}, bf16[1024,512]{1,0:T(8,128)(2,1)}, u32[]{:S(2)}, u32[]{:S(2)}) collective-permute-start(bf16[1024,512]{1,0:T(8,128)(2,1)} %cut.7.refs_0_), channel_id=1, source_target_pairs={{0,16},{4,20},{8,24},{12,28},{16,0},{20,4},{24,8},{28,12},{1,17},{... | collective-permute-start | bytes 3145736 | tf_op jit(solution)/shard_map/ppermute | solution.py:521
  60.1 24.5 %collective-permute-start.8 = (bf16[1024,512]{1,0:T(8,128)(2,1)}, bf16[1024,512]{1,0:T(8,128)(2,1)}, u32[]{:S(2)}, u32[]{:S(2)}) collective-permute-start(bf16[1024,512]{1,0:T(8,128)(2,1)} %cut.7.refs_0_), channel_id=1, source_target_pairs={{0,8},{4,12},{8,0},{12,4},{16,24},{20,28},{24,16},{28,20},{1,9},{5... | collective-permute-start | bytes 3145736 | tf_op jit(solution)/shard_map/ppermute | solution.py:520
  61.0 1.2 copy-start.8
  62.8 0.7 copy-start.12
  63.5 21.1 %copy-start.2 = (bf16[1024,768]{1,0:T(8,128)(2,1)S(1)}, bf16[1024,768]{1,0:T(8,128)(2,1)}, u32[]{:S(2)}) copy-start(bf16[1024,768]{1,0:T(8,128)(2,1)} %copy-done.1) | copy-start | bytes 4718596
  63.5 21.1 %copy-start.4 = (bf16[1024,768]{1,0:T(8,128)(2,1)S(1)}, bf16[1024,768]{1,0:T(8,128)(2,1)}, u32[]{:S(2)}) copy-start(bf16[1024,768]{1,0:T(8,128)(2,1)} %copy-done.3) | copy-start | bytes 4718596
  63.5 14.6 %all-to-all-start.2 = ((bf16[4,128,256]{2,1,0:T(8,128)(2,1)}), bf16[4,128,256]{2,1,0:T(8,128)(2,1)S(1)}, u32[]{:S(2)}, u32[]{:S(2)}) async-start(bf16[4,128,256]{2,1,0:T(8,128)(2,1)} %copy-done.12), calls=%async_computation.2 | async-start | bytes 524288 | tf_op jit(solution)/shard_map/all_to_all | solution.py:546
  78.1 1.2 copy-start.5
  80.9 10.6 %collective-permute-start.5 = (bf16[128,4096]{1,0:T(8,128)(2,1)S(1)}, bf16[128,4096]{1,0:T(8,128)(2,1)S(1)}, u32[]{:S(2)}, u32[]{:S(2)}) collective-permute-start(bf16[128,4096]{1,0:T(8,128)(2,1)S(1)} %get-tuple-element.29.refs_2_), channel_id=1, source_target_pairs={{1,2},{2,3},{5,6},{6,7},{9,10},{10,11},{13,14},{14,15},{17,18},{18... | collective-permute-start | bytes 3145736 | tf_op jit(solution)/shard_map/ppermute | solution.py:557
  81.6 5.9 %copy-start = (bf16[1024,1024]{1,0:T(8,128)(2,1)S(1)}, bf16[1024,1024]{1,0:T(8,128)(2,1)}, u32[]{:S(2)}) copy-start(bf16[1024,1024]{1,0:T(8,128)(2,1)} %q.1) | copy-start | bytes 6291460
  81.6 5.9 %copy-start.10 = (bf16[1024,256]{1,0:T(8,128)(2,1)S(1)}, bf16[1024,256]{1,0:T(8,128)(2,1)}, u32[]{:S(2)}) copy-start(bf16[1024,256]{1,0:T(8,128)(2,1)} %kv.1) | copy-start | bytes 1572868
  81.6 27.0 %collective-permute-start.6 = (bf16[128,4096]{1,0:T(8,128)(2,1)S(1)}, bf16[128,4096]{1,0:T(8,128)(2,1)S(1)}, u32[]{:S(2)}, u32[]{:S(2)}) collective-permute-start(bf16[128,4096]{1,0:T(8,128)(2,1)S(1)} %get-tuple-element.30), channel_id=1, source_target_pairs={{2,1},{1,0},{6,5},{5,4},{10,9},{9,8},{14,13},{13,12},{18,17},{17,1... | collective-permute-start | bytes 3145736 | tf_op jit(solution)/shard_map/ppermute | solution.py:557
  84.8 25.6 %collective-permute-start.11 = (bf16[512,768]{1,0:T(8,128)(2,1)S(1)}, bf16[512,768]{1,0:T(8,128)(2,1)S(1)}, u32[]{:S(2)}, u32[]{:S(2)}) collective-permute-start(bf16[512,768]{1,0:T(8,128)(2,1)S(1)} %get-tuple-element.35), channel_id=1, source_target_pairs={{0,8},{4,12},{8,0},{12,4},{16,24},{20,28},{24,16},{28,20},{1,9},{5... | collective-permute-start | bytes 2359304 | tf_op jit(solution)/shard_map/ppermute | solution.py:520
  86.0 24.3 %collective-permute-start.12 = (bf16[512,768]{1,0:T(8,128)(2,1)S(1)}, bf16[512,768]{1,0:T(8,128)(2,1)S(1)}, u32[]{:S(2)}, u32[]{:S(2)}) collective-permute-start(bf16[512,768]{1,0:T(8,128)(2,1)S(1)} %get-tuple-element.36), channel_id=1, source_target_pairs={{0,16},{4,20},{8,24},{12,28},{16,0},{20,4},{24,8},{28,12},{1,17},{... | collective-permute-start | bytes 2359304 | tf_op jit(solution)/shard_map/ppermute | solution.py:521
  89.5 19.1 %copy-start.6 = (bf16[128,4096]{1,0:T(8,128)(2,1)S(1)}, bf16[128,4096]{1,0:T(8,128)(2,1)}, u32[]{:S(2)}) copy-start(bf16[128,4096]{1,0:T(8,128)(2,1)} %cut.5.own.refs_0_) | copy-start | bytes 3145732
  90.9 30.0 %collective-permute-start.10 = (bf16[512,512]{1,0:T(8,128)(2,1)S(1)}, bf16[512,512]{1,0:T(8,128)(2,1)S(1)}, u32[]{:S(2)}, u32[]{:S(2)}) collective-permute-start(bf16[512,512]{1,0:T(8,128)(2,1)S(1)} %get-tuple-element.33), channel_id=1, source_target_pairs={{0,16},{4,20},{8,24},{12,28},{16,0},{20,4},{24,8},{28,12},{1,17},{... | collective-permute-start | bytes 1572872 | tf_op jit(solution)/shard_map/ppermute | solution.py:521
  91.5 29.3 %collective-permute-start.9 = (bf16[512,512]{1,0:T(8,128)(2,1)S(1)}, bf16[512,512]{1,0:T(8,128)(2,1)S(1)}, u32[]{:S(2)}, u32[]{:S(2)}) collective-permute-start(bf16[512,512]{1,0:T(8,128)(2,1)S(1)} %get-tuple-element.32.refs_5_), channel_id=1, source_target_pairs={{0,8},{4,12},{8,0},{12,4},{16,24},{20,28},{24,16},{28,20},{1,9},{5... | collective-permute-start | bytes 1572872 | tf_op jit(solution)/shard_map/ppermute | solution.py:520
  110.3 6.4 %copy-start.15 = (s32[1,256]{1,0:T(1,128)S(1)}, s32[1,256]{1,0:T(1,128)}, u32[]{:S(2)}) copy-start(s32[1,256]{1,0:T(1,128)} %refs_6_.3) | copy-start | bytes 3076
  111.6 1.6 %collective-permute-start.13 = (f32[256,256]{1,0:T(8,128)S(1)}, f32[256,256]{1,0:T(8,128)S(1)}, u32[]{:S(2)}, u32[]{:S(2)}) collective-permute-start(f32[256,256]{1,0:T(8,128)S(1)} %get-tuple-element.38), channel_id=1, source_target_pairs={{0,4},{4,0},{8,12},{12,8},{16,20},{20,16},{24,28},{28,24},{1,5},{5... | collective-permute-start | bytes 786440 | tf_op jit(solution)/shard_map/ppermute | solution.py:522
  113.2 7.6 %collective-permute-start.14 = (bf16[256,128]{1,0:T(8,128)(2,1)S(1)}, bf16[256,128]{1,0:T(8,128)(2,1)S(1)}, u32[]{:S(2)}, u32[]{:S(2)}) collective-permute-start(bf16[256,128]{1,0:T(8,128)(2,1)S(1)} %get-tuple-element.39.refs_0_), channel_id=1, source_target_pairs={{0,1},{1,2},{2,0},{4,5},{5,6},{6,4},{8,9},{9,10},{10,8},{12,13},{1... | collective-permute-start | bytes 196616 | tf_op jit(solution)/shard_map/ppermute | solution.py:557
  116.1 4.8 %collective-permute-start.15 = (bf16[256,128]{1,0:T(8,128)(2,1)S(1)}, bf16[256,128]{1,0:T(8,128)(2,1)S(1)}, u32[]{:S(2)}, u32[]{:S(2)}) collective-permute-start(bf16[256,128]{1,0:T(8,128)(2,1)S(1)} %get-tuple-element.41), channel_id=1, source_target_pairs={{1,3},{2,1},{3,2},{5,7},{6,5},{7,6},{9,11},{10,9},{11,10},{13,15},... | collective-permute-start | bytes 196616 | tf_op jit(solution)/shard_map/ppermute | solution.py:557
  120.7 2.6 %collective-permute-start.17 = (f32[256,512]{1,0:T(8,128)S(1)}, f32[256,512]{1,0:T(8,128)S(1)}, u32[]{:S(2)}, u32[]{:S(2)}) collective-permute-start(f32[256,512]{1,0:T(8,128)S(1)} %get-tuple-element.48), channel_id=1, source_target_pairs={{0,4},{4,0},{8,12},{12,8},{16,20},{20,16},{24,28},{28,24},{1,5},{5... | collective-permute-start | bytes 1572872 | tf_op jit(solution)/shard_map/ppermute | solution.py:522
  121.6 4.7 %collective-permute-start.16 = (f32[256,512]{1,0:T(8,128)S(1)}, f32[256,512]{1,0:T(8,128)S(1)}, u32[]{:S(2)}, u32[]{:S(2)}) collective-permute-start(f32[256,512]{1,0:T(8,128)S(1)} %get-tuple-element.43), channel_id=1, source_target_pairs={{0,4},{4,0},{8,12},{12,8},{16,20},{20,16},{24,28},{28,24},{1,5},{5... | collective-permute-start | bytes 1572872 | tf_op jit(solution)/shard_map/ppermute | solution.py:522

commit v4 on v3

--- a/solution.py
+++ b/solution.py
@@ -328,10 +328,13 @@
 
 def gather_kernel(asked_ref, store_ref, *refs):
     out_ref, sems = refs[-2:]
-    count = asked_ref.shape[0]
+    owners, cap = asked_ref.shape
     copies = [
-        pltpu.make_async_copy(store_ref.at[asked_ref[i]], out_ref.at[i], sems.at[i])
-        for i in range(count)
+        pltpu.make_async_copy(
+            store_ref.at[asked_ref[i, j]], out_ref.at[i * cap + j], sems.at[i * cap + j]
+        )
+        for i in range(owners)
+        for j in range(cap)
     ]
     for copy in copies:
         copy.start()
@@ -347,46 +350,42 @@
             pl.BlockSpec(memory_space=pltpu.HBM),
             pl.BlockSpec(memory_space=pl.ANY),
         ],
-        out_shape=jax.ShapeDtypeStruct(asked.shape + store_kv.shape[1:], BF16),
-        scratch_shapes=[pltpu.SemaphoreType.DMA(asked.shape)],
+        out_shape=jax.ShapeDtypeStruct((asked.size,) + store_kv.shape[1:], BF16),
+        scratch_shapes=[pltpu.SemaphoreType.DMA((asked.size,))],
         compiler_params=pltpu.CompilerParams(vmem_limit_bytes=4 << 20),
         cost_estimate=TINY,
         name="gather_blocks",
     )(asked, store_kv, gate)
 
 
-def multiply(a_ref, w_ref, d_x, d_y, col, near):
+def diagonal_part(a_ref, d_x, d_y, col):
+    h = d_x.shape[0]
+    part = jnp.dot(a_ref[:, 6 * h : 7 * h], d_x[:, col : col + STEP], preferred_element_type=F32)
+    return part + jnp.dot(a_ref[:, 7 * h :], d_y[:, col : col + STEP], preferred_element_type=F32)
+
+
+def project_near_kernel(a_ref, w_ref, first, last):
     depth = w_ref.shape[0] // 3
-    total = 0.0
-    for r in range(3):
-        total += jnp.dot(
-            a_ref[:, r * depth : (r + 1) * depth],
-            w_ref[r * depth : (r + 1) * depth, col : col + STEP],
-            preferred_element_type=F32,
-        )
-    if d_x is None:
-        return total
-    return total + diagonal_part(a_ref, d_x, d_y, near)
-
-
-def diagonal_part(a_ref, d_x, d_y, near):
-    h = d_x.shape[0]
-    part = jnp.dot(a_ref[:, 6 * h : 7 * h], d_x[:, near : near + STEP], preferred_element_type=F32)
-    return part + jnp.dot(a_ref[:, 7 * h :], d_y[:, near : near + STEP], preferred_element_type=F32)
-
-
-def project_kv_kernel(a_ref, w_ref, d_x, d_y, own, sib):
-    share(multiply(a_ref, w_ref, d_x, d_y, 0, 0), 4, own, sib, slice(0, STEP))
-
-
-def project_q_kernel(kv_cols, a_ref, w_ref, d_x, d_y, *refs):
-    own, sib, rest = refs[-3:]
-    early = own.shape[1]
-    for col in range(0, early, STEP):
-        total = multiply(a_ref, w_ref, d_x, d_y, kv_cols + col, kv_cols + col)
-        share(total, 4, own, sib, slice(col, col + STEP))
+    col = 0
+    for out in (first, last):
+        for here in range(0, out.shape[1], STEP):
+            total = 0.0
+            for r in range(3):
+                part = slice(r * depth, (r + 1) * depth)
+                total += jnp.dot(
+                    a_ref[:, part], w_ref[part, col : col + STEP], preferred_element_type=F32
+                )
+            out[:, here : here + STEP] = total
+            col += STEP
+
+
+def project_first_kernel(a_ref, d_x, d_y, rest, kv_own, kv_sib, own, sib):
     for col in range(0, rest.shape[1], STEP):
-        rest[:, col : col + STEP] = multiply(a_ref, w_ref, None, None, kv_cols + early + col, 0)
+        total = rest[:, col : col + STEP] + diagonal_part(a_ref, d_x, d_y, col)
+        if col == 0:
+            share(total, 4, kv_own, kv_sib, slice(0, STEP))
+        else:
+            share(total, 4, own, sib, slice(col - STEP, col))
 
 
 def project_last_kernel(a_ref, d_x, d_y, rest, *refs):
@@ -396,7 +395,7 @@
         share(total, 4, own, sib, slice(col, col + STEP))
 
 
-def project(kernel, near, gates, outs, limit, work):
+def project(kernel, near, gates, outs, limit):
     vmem = pl.BlockSpec(memory_space=pltpu.VMEM)
     return pl.pallas_call(
         kernel,
@@ -533,13 +532,12 @@
         (w_keyval, w_query),
         [[(0, (0, 0), (0, 0), (depth, kv_cols)), (1, (0, 0), (0, kv_cols), (depth, early))]],
         [(depth, first_cols)],
-        (asked,),
     )
     first_x, first_y = by_x(w_first), by_y(w_first)
-    gathered = gather_blocks(asked.reshape(-1), store_kv, w_first)
+    gathered = gather_blocks(asked, store_kv, asked)
     arrived = lax.all_to_all(gathered, "store", split_axis=0, concat_axis=0, tiled=True)
     (w_last,) = cut(
-        (w_query,), [[(0, (0, early), (0, 0), (depth, late))]], [(depth, late)], (arrived, first_x, first_y)
+        (w_query,), [[(0, (0, early), (0, 0), (depth, late))]], [(depth, late)], (arrived, first_x, first_y), limit=8
     )
     last_x, last_y = by_x(w_last), by_y(w_last)
     by_head = sort_blocks(arrived, places, (w_last,))
@@ -553,11 +551,12 @@
         [[(0, (0, 0), (0, 0), (shard, width)), (1, (0, 0), (shard, 0), (shard, width))]],
         [(2 * shard, width)],
         near=True,
+        limit=4,
     )
     along = lambda a, pairs: lax.ppermute(a, "ctx", pairs)
     two = along(both, [(0, 2), (1, 3), (2, 0), (3, 1)])
     one = along(both, [(0, 1), (1, 0), (2, 3), (3, 2)])
-    up, down = relay(both, two, (one, cached))
+    up, down = relay(both, two, (one,))
     shard_parts = (
         both,
         one,
@@ -577,7 +576,7 @@
         )
         return (by_x(sent[0]), by_y(sent[1])), sent[0]
 
-    diag_first, _ = diagonal(first_x, first_y, (up, last_x, last_y), 8)
+    diag_first, _ = diagonal(first_x, first_y, (up, last_x, last_y, cached), 8)
     weights, loaded = load_weights(w_keyval, w_query, first_x, first_y, last_x, last_y)
     diag_last, sent_last = diagonal(last_x, last_y, (loaded,), 6)
 
@@ -604,25 +603,23 @@
     )
 
     rows = load_rows(shard_parts, sent_last)
-    kv_own, kv_sib = project(
-        project_kv_kernel,
-        (rows, weights, *diag_first),
+    first_part, last_part = project(
+        project_near_kernel,
+        (rows, weights),
         (),
-        [(rec_count, kv_cols)] * 2,
+        [(2 * rec_count, first_cols), (2 * rec_count, late)],
         20,
-        2 * rows.size * kv_cols,
+    )
+    kv_own, kv_sib, early_own, early_sib = project(
+        project_first_kernel,
+        (rows, *diag_first, first_part),
+        (),
+        [(rec_count, kv_cols)] * 2 + [(rec_count, early)] * 2,
+        14,
     )
     fresh, to_first, to_second = make_fresh(kv_own, by_core(kv_sib))
     first = along(to_first, [(0, 1), (1, 2), (2, 0)])
     second = along(to_second, [(1, 3), (2, 1), (3, 2)])
-    early_own, early_sib, rest = project(
-        functools.partial(project_q_kernel, kv_cols),
-        (rows, weights, *diag_first),
-        (to_first,),
-        [(rec_count, early)] * 2 + [(2 * rec_count, late)],
-        22,
-        2 * rows.size * query_cols,
-    )
     key_rows, value_rows = assemble(
         fresh, first, second, cached, cosine, sine, targets.reshape(1, rec_count)
     )
@@ -637,11 +634,10 @@
     result = attend(early_own, by_core(early_sib), shared, query_cols, 0, None)
     own, sib = project(
         project_last_kernel,
-        (rows, *diag_last, rest),
+        (rows, *diag_last, last_part),
         (first, second, cached),
         [(rec_count, late)] * 2,
         12,
-        rows.size * late // 2,
     )
     result = attend(own, by_core(sib), shared, query_cols, early, result)
     return result.reshape(1, rec_count, query_cols)

time: 130 us -> 124 us (0.954); the launches traced: 129 us -> 122 us
  local copies, waits for them, and re-layouts: 10.2 us -> 1.85 us
  blocking collectives: 32.8 us -> 38 us
  waiting for transfers between devices: 30.8 us -> 25.6 us
  starting transfers between devices: 23.2 us -> 26 us
  other arithmetic: 3.83 us -> 1.13 us
    all_to_all x1, blocking collectives: 9.73 us -> 27.7 us  [swap_ids(): lax.all_to_all(wanted, 'store', split_axis=0, concat_axis=0, tiled=True)]
    ppermute x6, waiting for transfers between devices: 21 us -> 4.25 us  [fast_body(): along = lambda a, pairs: lax.ppermute(a, 'ctx', pairs)]
    all_to_all x1, blocking collectives: 23 us -> 10.3 us  [fast_body(): lax.all_to_all(gathered, 'store', split_axis=0, concat_axis=0, tiled=True)]
    ppermute x4, waiting for transfers between devices: 0.91 us -> 11.8 us  [fast_body(): by_x = lambda a: lax.ppermute(a, 'store', xf)]
    unnamed x38 -> x16, local copies, waits for them, and re-layouts: 9.56 us -> 1.76 us
    ppermute x4, waiting for transfers between devices: 0.68 us -> 3.61 us  [fast_body(): by_y = lambda a: lax.ppermute(a, 'store', yf)]
    all_to_all x1, waiting for transfers between devices: 4.73 us -> 2.72 us  [fast_body(): lax.all_to_all(by_head, 'ctx', split_axis=0, concat_axis=0, tiled=True)]
    pallas_call x5, Pallas kernels: 8.5 us -> 6.58 us  [cut(): pl.pallas_call(functools.partial(cut_kernel, plan, len(args)), in_specs=[...]
  transfers between devices with their start and end apart: 19 -> 19, of which waited for: 8 -> 10; matrix products, arithmetic and copies ran while one was open for 2% -> 1% of each run, Pallas kernels for 17% -> 19%
where the time goes in v4:
time: 124 us; the launch traced here: 122 us
  blocking collectives  38 us (31%)
  Pallas kernels  28.9 us (23%)
  starting transfers between devices  26 us (21%)
  waiting for transfers between devices  25.6 us (21%)
  local copies, waits for them, and re-layouts  1.85 us (1%)
    all_to_all x1, blocking collectives, swap_ids(): lax.all_to_all(wanted, 'store', split_axis=0, concat_axis=0, tiled=True)  27.7 us
    ppermute x4, waiting for transfers between devices, fast_body(): by_x = lambda a: lax.ppermute(a, 'store', xf)  11.8 us
    ppermute x6, starting transfers between devices, fast_body(): along = lambda a, pairs: lax.ppermute(a, 'ctx', pairs)  11.2 us
    all_to_all x1, blocking collectives, fast_body(): lax.all_to_all(gathered, 'store', split_axis=0, concat_axis=0, tiled=True)  10.3 us
    pallas_call x5, Pallas kernels, cut(): pl.pallas_call(functools.partial(cut_kernel, plan, len(args)), in_specs=[...  6.58 us
    pallas_call x2, Pallas kernels, attend(): pl.pallas_call(functools.partial(attend_kernel, cols // HD), grid=(1,), i...  5.97 us
    pallas_call x3, Pallas kernels, project(): pl.pallas_call(kernel, in_specs=[vmem] * len(near) + [pl.BlockSpec(memory...  5.9 us
    ppermute x4, starting transfers between devices, fast_body(): by_y = lambda a: lax.ppermute(a, 'store', yf)  5.68 us
  transfers between devices with their start and end apart: 19, of which 10 were waited for; matrix products, arithmetic and copies ran while one was open for 1% of the time, Pallas kernels for 19%

profile of v4, /device:TPU:0, one launch (start us, length us, event | category | flops | bytes accessed | tf_op | source)
XLA Modules:
  0.0 121.7 jit_solution(11691929093641015734)
XLA Ops:
  0.0 2.7 %cut.6 = bf16[1024,768]{1,0:T(8,128)(2,1)} custom-call(bf16[1024,256]{1,0:T(8,128)(2,1)} %kv.1, bf16[1024,1024]{1,0:T(8,128)(2,1)} %q.1), custom_call_target="tpu_custom_call" | custom-call | flops 1 | bytes 1 | tf_op jit(solution)/shard_map/cut/pallas_call | solution.py:181
  2.7 3.0 %collective-permute-start.6 = (bf16[1024,768]{1,0:T(8,128)(2,1)}, bf16[1024,768]{1,0:T(8,128)(2,1)}, u32[]{:S(2)}, u32[]{:S(2)}) collective-permute-start(bf16[1024,768]{1,0:T(8,128)(2,1)} %cut.6), channel_id=1, source_target_pairs={{0,16},{4,20},{8,24},{12,28},{16,0},{20,4},{24,8},{28,12},{1,17},{... | collective-permute-start | bytes 4718600 | tf_op jit(solution)/shard_map/ppermute | solution.py:520
  5.7 1.5 %collective-permute-start.5 = (bf16[1024,768]{1,0:T(8,128)(2,1)}, bf16[1024,768]{1,0:T(8,128)(2,1)}, u32[]{:S(2)}, u32[]{:S(2)}) collective-permute-start(bf16[1024,768]{1,0:T(8,128)(2,1)} %cut.6), channel_id=1, source_target_pairs={{0,8},{4,12},{8,0},{12,4},{16,24},{20,28},{24,16},{28,20},{1,9},{5... | collective-permute-start | bytes 4718600 | tf_op jit(solution)/shard_map/ppermute | solution.py:519
  7.2 0.4 norm_split.1
  7.7 0.1 collective-permute-start
  7.8 0.2 convert_reduce_fusion
  8.0 1.7 %collective-permute-done.refs_1_ = bf16[64,4096]{1,0:T(8,128)(2,1)S(1)} collective-permute-done((bf16[64,4096]{1,0:T(8,128)(2,1)S(1)}, bf16[64,4096]{1,0:T(8,128)(2,1)S(1)}, u32[]{:S(2)}, u32[]{:S(2)}) %collective-permute-start) | collective-permute-done | bytes 524320 | tf_op jit(solution)/shard_map/ppermute | solution.py:521
  9.6 0.1 cut.5.own.refs_0_
  9.7 2.7 %collective-permute-start.2 = (bf16[128,4096]{1,0:T(8,128)(2,1)S(1)}, bf16[128,4096]{1,0:T(8,128)(2,1)}, u32[]{:S(2)}, u32[]{:S(2)}) collective-permute-start(bf16[128,4096]{1,0:T(8,128)(2,1)S(1)} %cut.5.own.refs_0_), channel_id=1, source_target_pairs={{0,2},{1,3},{2,0},{3,1},{4,6},{5,7},{6,4},{7,5},{8,10},{9,11},{10,... | collective-permute-start | bytes 3145736 | tf_op jit(solution)/shard_map/ppermute | solution.py:556
  12.4 1.6 %collective-permute-start.1 = (bf16[128,4096]{1,0:T(8,128)(2,1)S(1)}, bf16[128,4096]{1,0:T(8,128)(2,1)}, u32[]{:S(2)}, u32[]{:S(2)}) collective-permute-start(bf16[128,4096]{1,0:T(8,128)(2,1)S(1)} %cut.5.own.refs_0_), channel_id=1, source_target_pairs={{0,1},{1,0},{2,3},{3,2},{4,5},{5,4},{6,7},{7,6},{8,9},{9,8},{10,11... | collective-permute-start | bytes 3145736 | tf_op jit(solution)/shard_map/ppermute | solution.py:556
  14.0 0.1 select_reduce_fusion
  14.1 0.1 copy.15
  14.2 27.7 %all_to_all.21 = s32[8,1,2]{2,1,0:T(1,128)S(1)} all-to-all(s32[8,1,2]{2,1,0:T(1,128)S(1)} %copy.15), channel_id=1, replica_groups=mesh['store'=8,'ctx'=4] {'store'}, dimensions={0} | all-to-all | bytes 128 | tf_op jit(solution)/shard_map/all_to_all | solution.py:51
  41.9 1.0 copy-done.4
  43.0 1.1 gather_blocks.1
  44.1 10.3 %all_to_all.22.refs_1_.blocks_ref = bf16[16,8,1024]{2,1,0:T(8,128)(2,1)S(1)} all-to-all(bf16[16,8,1024]{2,1,0:T(8,128)(2,1)S(1)} %gather_blocks.1), channel_id=1, replica_groups=mesh['store'=8,'ctx'=4] {'store'}, dimensions={0} | all-to-all | bytes 524288 | tf_op jit(solution)/shard_map/all_to_all | solution.py:538
  54.4 0.0 collective-permute-done.6.refs_3_.first_y.refs_0_
  54.4 0.0 collective-permute-done.5.refs_2_.first_x.refs_1_
  54.4 1.2 cut.7.refs_0_
  55.6 0.6 collective-permute-start.8
  56.2 0.6 collective-permute-start.7
  56.7 0.6 sort_blocks.1
  57.3 0.0 copy-start.3
  57.3 0.7 copy-done.3
  58.0 4.9 %all-to-all-start.2 = ((bf16[4,128,256]{2,1,0:T(8,128)(2,1)}), bf16[4,128,256]{2,1,0:T(8,128)(2,1)S(1)}, u32[]{:S(2)}, u32[]{:S(2)}) async-start(bf16[4,128,256]{2,1,0:T(8,128)(2,1)} %copy-done.3), calls=%async_computation.2 | async-start | bytes 524288 | tf_op jit(solution)/shard_map/all_to_all | solution.py:544
  62.9 0.0 collective-permute-done.2.two.refs_2_
  62.9 0.0 collective-permute-done.1.refs_0_.refs_1_
  62.9 3.0 %relay.1 = (bf16[128,4096]{1,0:T(8,128)(2,1)}, bf16[128,4096]{1,0:T(8,128)(2,1)}) custom-call(bf16[128,4096]{1,0:T(8,128)(2,1)S(1)} %cut.5.own.refs_0_, bf16[128,4096]{1,0:T(8,128)(2,1)} %collective-permute-done.2.two.refs_2_, bf16[128,4096]{1,0:T(8,128)(2,1)} %collective-permute-done.1.refs_0_.refs_1_), custom_call_target="tpu_custom_call" | custom-call | flops 1 | bytes 1 | tf_op jit(solution)/shard_map/relay/pallas_call | solution.py:212
  65.9 1.3 %collective-permute-start.4 = (bf16[128,4096]{1,0:T(8,128)(2,1)}, bf16[128,4096]{1,0:T(8,128)(2,1)}, u32[]{:S(2)}, u32[]{:S(2)}) collective-permute-start(bf16[128,4096]{1,0:T(8,128)(2,1)} %get-tuple-element.31), channel_id=1, source_target_pairs={{2,1},{1,0},{6,5},{5,4},{10,9},{9,8},{14,13},{13,12},{18,17},{17,1... | collective-permute-start | bytes 3145736 | tf_op jit(solution)/shard_map/ppermute | solution.py:556
  67.2 1.7 %collective-permute-start.3 = (bf16[128,4096]{1,0:T(8,128)(2,1)}, bf16[128,4096]{1,0:T(8,128)(2,1)}, u32[]{:S(2)}, u32[]{:S(2)}) collective-permute-start(bf16[128,4096]{1,0:T(8,128)(2,1)} %get-tuple-element.30.refs_2_), channel_id=1, source_target_pairs={{1,2},{2,3},{5,6},{6,7},{9,10},{10,11},{13,14},{14,15},{17,18},{18... | collective-permute-start | bytes 3145736 | tf_op jit(solution)/shard_map/ppermute | solution.py:556
  68.9 2.7 %all-to-all-done.2 = bf16[4,128,256]{2,1,0:T(8,128)(2,1)S(1)} async-done(((bf16[4,128,256]{2,1,0:T(8,128)(2,1)}), bf16[4,128,256]{2,1,0:T(8,128)(2,1)S(1)}, u32[]{:S(2)}, u32[]{:S(2)}) %all-to-all-start.2) | async-done | bytes 262176 | tf_op jit(solution)/shard_map/all_to_all | solution.py:544
  71.6 8.7 %collective-permute-done.8.last_x.refs_1_.refs_3_ = bf16[1024,512]{1,0:T(8,128)(2,1)} collective-permute-done((bf16[1024,512]{1,0:T(8,128)(2,1)}, bf16[1024,512]{1,0:T(8,128)(2,1)}, u32[]{:S(2)}, u32[]{:S(2)}) %collective-permute-start.8) | collective-permute-done | bytes 1048608 | tf_op jit(solution)/shard_map/ppermute | solution.py:519
  80.3 1.0 collective-permute-done.7.last_y.refs_0_.refs_4_
  81.3 1.4 %cut.9 = (bf16[512,768]{1,0:T(8,128)(2,1)S(1)}, bf16[512,768]{1,0:T(8,128)(2,1)S(1)}) custom-call(bf16[1024,768]{1,0:T(8,128)(2,1)} %collective-permute-done.6.refs_3_.first_y.refs_0_, bf16[1024,768]{1,0:T(8,128)(2,1)} %collective-permute-done.5.refs_2_.first_x.refs_1_, bf16[128,4096]{1,0:T(8,128)(2,1)} %get-tuple-element.30.refs_2_, ...), custom_call_target="tpu_custom_call" | custom-call | flops 1 | bytes 1 | tf_op jit(solution)/shard_map/cut/pallas_call | solution.py:181
  82.8 0.8 collective-permute-start.11
  83.6 0.6 collective-permute-start.12
  84.1 2.9 %load_weights.1 = (bf16[3072,1280]{1,0:T(8,128)(2,1)S(1)}, f32[8,128]{1,0:T(8,128)S(1)}) custom-call(bf16[1024,256]{1,0:T(8,128)(2,1)S(1)} %copy-done.1, bf16[1024,1024]{1,0:T(8,128)(2,1)S(1)} %copy-done, bf16[1024,768]{1,0:T(8,128)(2,1)} %collective-permute-done.5.refs_2_.first_x.refs_1_, bf16[1024,768]{1,0:T(8,128)(2,1)} %collective-permute-done.6.refs_3_.first_y.refs_0_, ...), custom_call_target="tpu_custom_call" | custom-call | flops 1 | bytes 1 | tf_op jit(solution)/shard_map/load_weights/pallas_call | solution.py:315
  87.0 1.2 %cut.8 = (bf16[512,512]{1,0:T(8,128)(2,1)S(1)}, bf16[512,512]{1,0:T(8,128)(2,1)S(1)}) custom-call(bf16[1024,512]{1,0:T(8,128)(2,1)} %collective-permute-done.7.last_y.refs_0_.refs_4_, bf16[1024,512]{1,0:T(8,128)(2,1)} %collective-permute-done.8.last_x.refs_1_.refs_3_, f32[8,128]{1,0:T(8,128)S(1)} %get-tuple-element.32.refs_2_), custom_call_target="tpu_custom_call" | custom-call | flops 1 | bytes 1 | tf_op jit(solution)/shard_map/cut/pallas_call | solution.py:181
  88.2 1.5 %collective-permute-start.10 = (bf16[512,512]{1,0:T(8,128)(2,1)S(1)}, bf16[512,512]{1,0:T(8,128)(2,1)S(1)}, u32[]{:S(2)}, u32[]{:S(2)}) collective-permute-start(bf16[512,512]{1,0:T(8,128)(2,1)S(1)} %get-tuple-element.34), channel_id=1, source_target_pairs={{0,16},{4,20},{8,24},{12,28},{16,0},{20,4},{24,8},{28,12},{1,17},{... | collective-permute-start | bytes 1572872 | tf_op jit(solution)/shard_map/ppermute | solution.py:520
  89.7 3.2 %collective-permute-done.4.refs_4_ = bf16[128,4096]{1,0:T(8,128)(2,1)} collective-permute-done((bf16[128,4096]{1,0:T(8,128)(2,1)}, bf16[128,4096]{1,0:T(8,128)(2,1)}, u32[]{:S(2)}, u32[]{:S(2)}) %collective-permute-start.4) | collective-permute-done | bytes 1048608 | tf_op jit(solution)/shard_map/ppermute | solution.py:556
  93.0 1.0 collective-permute-start.9
  94.0 0.0 collective-permute-done.3.refs_3_
  94.0 2.0 %load_rows.1.a_ref = bf16[512,4096]{1,0:T(8,128)(2,1)S(1)} custom-call(bf16[128,4096]{1,0:T(8,128)(2,1)S(1)} %cut.5.own.refs_0_, bf16[128,4096]{1,0:T(8,128)(2,1)} %collective-permute-done.1.refs_0_.refs_1_, bf16[128,4096]{1,0:T(8,128)(2,1)} %collective-permute-done.2.two.refs_2_, bf16[128,4096]{1,0:T(8,128)(2,1)} %collective-permute-done.3.refs_3_, ...), custom_call_target="tpu_custom_call" | custom-call | flops 1 | bytes 1 | tf_op jit(solution)/shard_map/load_rows/pallas_call | solution.py:284
  95.9 4.2 %project.3 = (f32[512,768]{1,0:T(8,128)S(1)}, f32[512,512]{1,0:T(8,128)S(1)}) custom-call(bf16[512,4096]{1,0:T(8,128)(2,1)S(1)} %load_rows.1.a_ref, bf16[3072,1280]{1,0:T(8,128)(2,1)S(1)} %get-tuple-element.35.w_ref), custom_call_target="tpu_custom_call" | custom-call | flops 1 | bytes 1 | tf_op jit(solution)/shard_map/project/pallas_call | solution.py:400
  100.2 3.1 %collective-permute-done.11.d_x = bf16[512,768]{1,0:T(8,128)(2,1)S(1)} collective-permute-done((bf16[512,768]{1,0:T(8,128)(2,1)S(1)}, bf16[512,768]{1,0:T(8,128)(2,1)S(1)}, u32[]{:S(2)}, u32[]{:S(2)}) %collective-permute-start.11) | collective-permute-done | bytes 786464 | tf_op jit(solution)/shard_map/ppermute | solution.py:519
  103.3 0.7 collective-permute-done.12.d_y
  104.0 1.0 project.4
  105.0 0.1 collective-permute-start.13
  105.1 1.5 %collective-permute-done.13.sib = f32[256,256]{1,0:T(8,128)S(1)} collective-permute-done((f32[256,256]{1,0:T(8,128)S(1)}, f32[256,256]{1,0:T(8,128)S(1)}, u32[]{:S(2)}, u32[]{:S(2)}) %collective-permute-start.13) | collective-permute-done | bytes 262176 | tf_op jit(solution)/shard_map/ppermute | solution.py:521
  106.7 3.4 %collective-permute-start.14 = (bf16[256,128]{1,0:T(8,128)(2,1)S(1)}, bf16[256,128]{1,0:T(8,128)(2,1)S(1)}, u32[]{:S(2)}, u32[]{:S(2)}) collective-permute-start(bf16[256,128]{1,0:T(8,128)(2,1)S(1)} %get-tuple-element.42), channel_id=1, source_target_pairs={{0,1},{1,2},{2,0},{4,5},{5,6},{6,4},{8,9},{9,10},{10,8},{12,13},{1... | collective-permute-start | bytes 196616 | tf_op jit(solution)/shard_map/ppermute | solution.py:556
  110.0 0.7 collective-permute-start.15
  110.8 0.1 collective-permute-start.17
  110.8 1.9 %collective-permute-done.10.d_y = bf16[512,512]{1,0:T(8,128)(2,1)S(1)} collective-permute-done((bf16[512,512]{1,0:T(8,128)(2,1)S(1)}, bf16[512,512]{1,0:T(8,128)(2,1)S(1)}, u32[]{:S(2)}, u32[]{:S(2)}) %collective-permute-start.10) | collective-permute-done | bytes 524320 | tf_op jit(solution)/shard_map/ppermute | solution.py:520
  112.7 0.0 collective-permute-done.9.d_x
  112.7 1.0 collective-permute-done.14.refs_0_.first_ref
  113.7 0.7 project.5
  114.4 0.1 collective-permute-start.16
  114.5 0.1 fusion.13.refs_7_
  114.6 0.5 fusion.21
  115.2 0.1 pad_maximum_fusion
  115.3 0.4 assemble.1
  115.7 0.0 collective-permute-done.17.refs_1_
  115.7 3.0 %attend.2.refs_8_ = bf16[256,1024]{1,0:T(8,128)(2,1)} custom-call(f32[256,512]{1,0:T(8,128)S(1)} %get-tuple-element.49.refs_0_, f32[256,512]{1,0:T(8,128)S(1)} %collective-permute-done.17.refs_1_, bf16[512,128]{1,0:T(8,128)(2,1)S(1)} %get-tuple-element.47.refs_2_, bf16[128,512]{1,0:T(8,128)(2,1)S(1)} %get-tuple-element.48.refs_3_, ...), custom_call_target="tpu_custom_call" | custom-call | flops 1 | bytes 1 | tf_op jit(solution)/shard_map/attend/pallas_call | solution.py:495
  118.7 3.0 %attend.3 = bf16[256,1024]{1,0:T(8,128)(2,1)} custom-call(f32[256,512]{1,0:T(8,128)S(1)} %get-tuple-element.44.refs_0_, f32[256,512]{1,0:T(8,128)S(1)} %collective-permute-done.16.refs_1_, bf16[512,128]{1,0:T(8,128)(2,1)S(1)} %get-tuple-element.47.refs_2_, bf16[128,512]{1,0:T(8,128)(2,1)S(1)} %get-tuple-element.48.refs_3_, ...), custom_call_target="tpu_custom_call", output_to_operand_aliasing={{}: (8, {})} | custom-call | flops 1 | bytes 1 | tf_op jit(solution)/shard_map/attend/pallas_call | solution.py:495
  (21 shorter events, 0.1 us)
Async XLA Ops:
  0.0 7.2 %copy-start.2 = (bf16[1,64,8192]{2,1,0:T(8,128)(2,1)S(1)}, bf16[1,64,8192]{2,1,0:T(8,128)(2,1)}, u32[]{:S(2)}) copy-start(bf16[1,64,8192]{2,1,0:T(8,128)(2,1)} %param.11) | copy-start | bytes 3145732
  0.0 7.7 %copy-start.7 = (s32[1,16]{1,0:T(1,128)S(1)}, s32[1,16]{1,0:T(1,128)}, u32[]{:S(2)}) copy-start(s32[1,16]{1,0:T(1,128)} %param.9) | copy-start | bytes 196
  2.7 51.7 %collective-permute-start.6 = (bf16[1024,768]{1,0:T(8,128)(2,1)}, bf16[1024,768]{1,0:T(8,128)(2,1)}, u32[]{:S(2)}, u32[]{:S(2)}) collective-permute-start(bf16[1024,768]{1,0:T(8,128)(2,1)} %cut.6), channel_id=1, source_target_pairs={{0,16},{4,20},{8,24},{12,28},{16,0},{20,4},{24,8},{28,12},{1,17},{... | collective-permute-start | bytes 4718600 | tf_op jit(solution)/shard_map/ppermute | solution.py:520
  5.7 48.7 %collective-permute-start.5 = (bf16[1024,768]{1,0:T(8,128)(2,1)}, bf16[1024,768]{1,0:T(8,128)(2,1)}, u32[]{:S(2)}, u32[]{:S(2)}) collective-permute-start(bf16[1024,768]{1,0:T(8,128)(2,1)} %cut.6), channel_id=1, source_target_pairs={{0,8},{4,12},{8,0},{12,4},{16,24},{20,28},{24,16},{28,20},{1,9},{5... | collective-permute-start | bytes 4718600 | tf_op jit(solution)/shard_map/ppermute | solution.py:519
  7.2 6.8 %copy-start.6 = (s32[1,16]{1,0:T(1,128)S(1)}, s32[1,16]{1,0:T(1,128)}, u32[]{:S(2)}) copy-start(s32[1,16]{1,0:T(1,128)} %param.8) | copy-start | bytes 196
  7.7 2.0 %collective-permute-start = (bf16[64,4096]{1,0:T(8,128)(2,1)S(1)}, bf16[64,4096]{1,0:T(8,128)(2,1)S(1)}, u32[]{:S(2)}, u32[]{:S(2)}) collective-permute-start(bf16[64,4096]{1,0:T(8,128)(2,1)S(1)} %get-tuple-element.29), channel_id=1, source_target_pairs={{0,4},{4,0},{8,12},{12,8},{16,20},{20,16},{24,28},{28,24},{1,5},{5... | collective-permute-start | bytes 1572872 | tf_op jit(solution)/shard_map/ppermute | solution.py:521
  9.6 44.7 %copy-start = (bf16[1024,1024]{1,0:T(8,128)(2,1)S(1)}, bf16[1024,1024]{1,0:T(8,128)(2,1)}, u32[]{:S(2)}) copy-start(bf16[1024,1024]{1,0:T(8,128)(2,1)} %q.1) | copy-start | bytes 6291460
  9.7 53.2 %collective-permute-start.2 = (bf16[128,4096]{1,0:T(8,128)(2,1)S(1)}, bf16[128,4096]{1,0:T(8,128)(2,1)}, u32[]{:S(2)}, u32[]{:S(2)}) collective-permute-start(bf16[128,4096]{1,0:T(8,128)(2,1)S(1)} %cut.5.own.refs_0_), channel_id=1, source_target_pairs={{0,2},{1,3},{2,0},{3,1},{4,6},{5,7},{6,4},{7,5},{8,10},{9,11},{10,... | collective-permute-start | bytes 3145736 | tf_op jit(solution)/shard_map/ppermute | solution.py:556
  12.4 50.5 %collective-permute-start.1 = (bf16[128,4096]{1,0:T(8,128)(2,1)S(1)}, bf16[128,4096]{1,0:T(8,128)(2,1)}, u32[]{:S(2)}, u32[]{:S(2)}) collective-permute-start(bf16[128,4096]{1,0:T(8,128)(2,1)S(1)} %cut.5.own.refs_0_), channel_id=1, source_target_pairs={{0,1},{1,0},{2,3},{3,2},{4,5},{5,4},{6,7},{7,6},{8,9},{9,8},{10,11... | collective-permute-start | bytes 3145736 | tf_op jit(solution)/shard_map/ppermute | solution.py:556
  41.9 1.0 copy-start.4
  55.6 24.7 %collective-permute-start.8 = (bf16[1024,512]{1,0:T(8,128)(2,1)}, bf16[1024,512]{1,0:T(8,128)(2,1)}, u32[]{:S(2)}, u32[]{:S(2)}) collective-permute-start(bf16[1024,512]{1,0:T(8,128)(2,1)} %cut.7.refs_0_), channel_id=1, source_target_pairs={{0,8},{4,12},{8,0},{12,4},{16,24},{20,28},{24,16},{28,20},{1,9},{5... | collective-permute-start | bytes 3145736 | tf_op jit(solution)/shard_map/ppermute | solution.py:519
  56.2 25.1 %collective-permute-start.7 = (bf16[1024,512]{1,0:T(8,128)(2,1)}, bf16[1024,512]{1,0:T(8,128)(2,1)}, u32[]{:S(2)}, u32[]{:S(2)}) collective-permute-start(bf16[1024,512]{1,0:T(8,128)(2,1)} %cut.7.refs_0_), channel_id=1, source_target_pairs={{0,16},{4,20},{8,24},{12,28},{16,0},{20,4},{24,8},{28,12},{1,17},{... | collective-permute-start | bytes 3145736 | tf_op jit(solution)/shard_map/ppermute | solution.py:520
  57.3 0.7 copy-start.3
  58.0 13.6 %all-to-all-start.2 = ((bf16[4,128,256]{2,1,0:T(8,128)(2,1)}), bf16[4,128,256]{2,1,0:T(8,128)(2,1)S(1)}, u32[]{:S(2)}, u32[]{:S(2)}) async-start(bf16[4,128,256]{2,1,0:T(8,128)(2,1)} %copy-done.3), calls=%async_computation.2 | async-start | bytes 524288 | tf_op jit(solution)/shard_map/all_to_all | solution.py:544
  65.9 27.0 %collective-permute-start.4 = (bf16[128,4096]{1,0:T(8,128)(2,1)}, bf16[128,4096]{1,0:T(8,128)(2,1)}, u32[]{:S(2)}, u32[]{:S(2)}) collective-permute-start(bf16[128,4096]{1,0:T(8,128)(2,1)} %get-tuple-element.31), channel_id=1, source_target_pairs={{2,1},{1,0},{6,5},{5,4},{10,9},{9,8},{14,13},{13,12},{18,17},{17,1... | collective-permute-start | bytes 3145736 | tf_op jit(solution)/shard_map/ppermute | solution.py:556
  67.2 26.8 %collective-permute-start.3 = (bf16[128,4096]{1,0:T(8,128)(2,1)}, bf16[128,4096]{1,0:T(8,128)(2,1)}, u32[]{:S(2)}, u32[]{:S(2)}) collective-permute-start(bf16[128,4096]{1,0:T(8,128)(2,1)} %get-tuple-element.30.refs_2_), channel_id=1, source_target_pairs={{1,2},{2,3},{5,6},{6,7},{9,10},{10,11},{13,14},{14,15},{17,18},{18... | collective-permute-start | bytes 3145736 | tf_op jit(solution)/shard_map/ppermute | solution.py:556
  81.3 2.8 %copy-start.1 = (bf16[1024,256]{1,0:T(8,128)(2,1)S(1)}, bf16[1024,256]{1,0:T(8,128)(2,1)}, u32[]{:S(2)}) copy-start(bf16[1024,256]{1,0:T(8,128)(2,1)} %kv.1) | copy-start | bytes 1572868
  82.8 20.5 %collective-permute-start.11 = (bf16[512,768]{1,0:T(8,128)(2,1)S(1)}, bf16[512,768]{1,0:T(8,128)(2,1)S(1)}, u32[]{:S(2)}, u32[]{:S(2)}) collective-permute-start(bf16[512,768]{1,0:T(8,128)(2,1)S(1)} %get-tuple-element.37), channel_id=1, source_target_pairs={{0,8},{4,12},{8,0},{12,4},{16,24},{20,28},{24,16},{28,20},{1,9},{5... | collective-permute-start | bytes 2359304 | tf_op jit(solution)/shard_map/ppermute | solution.py:519
  83.6 20.5 %collective-permute-start.12 = (bf16[512,768]{1,0:T(8,128)(2,1)S(1)}, bf16[512,768]{1,0:T(8,128)(2,1)S(1)}, u32[]{:S(2)}, u32[]{:S(2)}) collective-permute-start(bf16[512,768]{1,0:T(8,128)(2,1)S(1)} %get-tuple-element.38), channel_id=1, source_target_pairs={{0,16},{4,20},{8,24},{12,28},{16,0},{20,4},{24,8},{28,12},{1,17},{... | collective-permute-start | bytes 2359304 | tf_op jit(solution)/shard_map/ppermute | solution.py:520
  88.2 24.5 %collective-permute-start.10 = (bf16[512,512]{1,0:T(8,128)(2,1)S(1)}, bf16[512,512]{1,0:T(8,128)(2,1)S(1)}, u32[]{:S(2)}, u32[]{:S(2)}) collective-permute-start(bf16[512,512]{1,0:T(8,128)(2,1)S(1)} %get-tuple-element.34), channel_id=1, source_target_pairs={{0,16},{4,20},{8,24},{12,28},{16,0},{20,4},{24,8},{28,12},{1,17},{... | collective-permute-start | bytes 1572872 | tf_op jit(solution)/shard_map/ppermute | solution.py:520
  93.0 19.7 %collective-permute-start.9 = (bf16[512,512]{1,0:T(8,128)(2,1)S(1)}, bf16[512,512]{1,0:T(8,128)(2,1)S(1)}, u32[]{:S(2)}, u32[]{:S(2)}) collective-permute-start(bf16[512,512]{1,0:T(8,128)(2,1)S(1)} %get-tuple-element.33.refs_5_), channel_id=1, source_target_pairs={{0,8},{4,12},{8,0},{12,4},{16,24},{20,28},{24,16},{28,20},{1,9},{5... | collective-permute-start | bytes 1572872 | tf_op jit(solution)/shard_map/ppermute | solution.py:519
  104.0 6.7 %copy-start.5 = (s32[1,256]{1,0:T(1,128)S(1)}, s32[1,256]{1,0:T(1,128)}, u32[]{:S(2)}) copy-start(s32[1,256]{1,0:T(1,128)} %refs_6_.3) | copy-start | bytes 3076
  105.0 1.6 %collective-permute-start.13 = (f32[256,256]{1,0:T(8,128)S(1)}, f32[256,256]{1,0:T(8,128)S(1)}, u32[]{:S(2)}, u32[]{:S(2)}) collective-permute-start(f32[256,256]{1,0:T(8,128)S(1)} %get-tuple-element.41), channel_id=1, source_target_pairs={{0,4},{4,0},{8,12},{12,8},{16,20},{20,16},{24,28},{28,24},{1,5},{5... | collective-permute-start | bytes 786440 | tf_op jit(solution)/shard_map/ppermute | solution.py:521
  106.7 7.1 %collective-permute-start.14 = (bf16[256,128]{1,0:T(8,128)(2,1)S(1)}, bf16[256,128]{1,0:T(8,128)(2,1)S(1)}, u32[]{:S(2)}, u32[]{:S(2)}) collective-permute-start(bf16[256,128]{1,0:T(8,128)(2,1)S(1)} %get-tuple-element.42), channel_id=1, source_target_pairs={{0,1},{1,2},{2,0},{4,5},{5,6},{6,4},{8,9},{9,10},{10,8},{12,13},{1... | collective-permute-start | bytes 196616 | tf_op jit(solution)/shard_map/ppermute | solution.py:556
  110.0 3.7 %collective-permute-start.15 = (bf16[256,128]{1,0:T(8,128)(2,1)S(1)}, bf16[256,128]{1,0:T(8,128)(2,1)S(1)}, u32[]{:S(2)}, u32[]{:S(2)}) collective-permute-start(bf16[256,128]{1,0:T(8,128)(2,1)S(1)} %get-tuple-element.43), channel_id=1, source_target_pairs={{1,3},{2,1},{3,2},{5,7},{6,5},{7,6},{9,11},{10,9},{11,10},{13,15},... | collective-permute-start | bytes 196616 | tf_op jit(solution)/shard_map/ppermute | solution.py:556
  110.8 5.0 %collective-permute-start.17 = (f32[256,512]{1,0:T(8,128)S(1)}, f32[256,512]{1,0:T(8,128)S(1)}, u32[]{:S(2)}, u32[]{:S(2)}) collective-permute-start(f32[256,512]{1,0:T(8,128)S(1)} %get-tuple-element.50), channel_id=1, source_target_pairs={{0,4},{4,0},{8,12},{12,8},{16,20},{20,16},{24,28},{28,24},{1,5},{5... | collective-permute-start | bytes 1572872 | tf_op jit(solution)/shard_map/ppermute | solution.py:521
  114.4 4.3 %collective-permute-start.16 = (f32[256,512]{1,0:T(8,128)S(1)}, f32[256,512]{1,0:T(8,128)S(1)}, u32[]{:S(2)}, u32[]{:S(2)}) collective-permute-start(f32[256,512]{1,0:T(8,128)S(1)} %get-tuple-element.45), channel_id=1, source_target_pairs={{0,4},{4,0},{8,12},{12,8},{16,20},{20,16},{24,28},{28,24},{1,5},{5... | collective-permute-start | bytes 1572872 | tf_op jit(solution)/shard_map/ppermute | solution.py:521

commit v5 on v4

--- a/solution.py
+++ b/solution.py
@@ -255,6 +255,24 @@
         here = slice(z * rows, (z + 1) * rows)
         own[here, cols] = total[2 * z * rows : (2 * z + 1) * rows]
         sib[here, cols] = total[(2 * z + 1) * rows : (2 * z + 2) * rows]
+
+
+def hold_kernel(*refs):
+    pass
+
+
+def hold(first, second, gates):
+    anywhere = pl.BlockSpec(memory_space=pl.ANY)
+    return pl.pallas_call(
+        hold_kernel,
+        in_specs=[anywhere] * (2 + len(gates)),
+        out_specs=[anywhere] * 2,
+        out_shape=[jax.ShapeDtypeStruct(first.shape, BF16)] * 2,
+        input_output_aliases={0: 0, 1: 1},
+        compiler_params=pltpu.CompilerParams(vmem_limit_bytes=2 << 20),
+        cost_estimate=TINY,
+        name="hold",
+    )(first, second, *gates)
 
 
 def load_rows_kernel(*refs):
@@ -565,7 +583,7 @@
         along(down, [(2, 1), (1, 0)]),
     )
 
-    def diagonal(from_x, from_y, gates, limit):
+    def diagonal(from_x, from_y, gates, limit, late_gates=()):
         cols = from_x.shape[1]
         sent = cut(
             (from_y, from_x),
@@ -574,9 +592,11 @@
             gates,
             limit=limit,
         )
+        if late_gates:
+            sent = hold(*sent, late_gates)
         return (by_x(sent[0]), by_y(sent[1])), sent[0]
 
-    diag_first, _ = diagonal(first_x, first_y, (up, last_x, last_y, cached), 8)
+    diag_first, _ = diagonal(first_x, first_y, (up, cached), 8, (last_x, last_y))
     weights, loaded = load_weights(w_keyval, w_query, first_x, first_y, last_x, last_y)
     diag_last, sent_last = diagonal(last_x, last_y, (loaded,), 6)
 

time: 124 us -> 122 us (0.984)
  waiting for transfers between devices: 25.6 us -> 23.4 us
    ppermute x4, waiting for transfers between devices: 11.8 us -> 0.69 us  [fast_body(): by_x = lambda a: lax.ppermute(a, 'store', xf)]
    ppermute x4, waiting for transfers between devices: 3.61 us -> 9.07 us  [fast_body(): by_y = lambda a: lax.ppermute(a, 'store', yf)]
    ppermute x6, waiting for transfers between devices: 4.25 us -> 8 us  [fast_body(): along = lambda a, pairs: lax.ppermute(a, 'ctx', pairs)]
    ppermute x4, starting transfers between devices: 3.93 us -> 5.53 us  [fast_body(): by_x = lambda a: lax.ppermute(a, 'store', xf)]
    ppermute x4, starting transfers between devices: 5.68 us -> 4.3 us  [fast_body(): by_y = lambda a: lax.ppermute(a, 'store', yf)]
  transfers between devices with their start and end apart: 19 -> 19, of which waited for: 10 -> 9; matrix products, arithmetic and copies ran while one was open for 1% -> 1% of each run, Pallas kernels for 19% -> 19%
where the time goes in v5:
time: 122 us; the launch traced here: 119 us
  blocking collectives  37.2 us (30%)
  Pallas kernels  28.8 us (24%)
  starting transfers between devices  26.5 us (22%)
  waiting for transfers between devices  23.4 us (19%)
  local copies, waits for them, and re-layouts  1.85 us (2%)
    all_to_all x1, blocking collectives, swap_ids(): lax.all_to_all(wanted, 'store', split_axis=0, concat_axis=0, tiled=True)  27.7 us
    ppermute x6, starting transfers between devices, fast_body(): along = lambda a, pairs: lax.ppermute(a, 'ctx', pairs)  11.5 us
    all_to_all x1, blocking collectives, fast_body(): lax.all_to_all(gathered, 'store', split_axis=0, concat_axis=0, tiled=True)  9.53 us
    ppermute x4, waiting for transfers between devices, fast_body(): by_y = lambda a: lax.ppermute(a, 'store', yf)  9.07 us
    ppermute x6, waiting for transfers between devices, fast_body(): along = lambda a, pairs: lax.ppermute(a, 'ctx', pairs)  8 us
    pallas_call x5, Pallas kernels, cut(): pl.pallas_call(functools.partial(cut_kernel, plan, len(args)), in_specs=[...  6.52 us
    pallas_call x2, Pallas kernels, attend(): pl.pallas_call(functools.partial(attend_kernel, cols // HD), grid=(1,), i...  5.97 us
    pallas_call x3, Pallas kernels, project(): pl.pallas_call(kernel, in_specs=[vmem] * len(near) + [pl.BlockSpec(memory...  5.9 us
  transfers between devices with their start and end apart: 19, of which 9 were waited for; matrix products, arithmetic and copies ran while one was open for 1% of the time, Pallas kernels for 19%

profile of v5, /device:TPU:0, one launch (start us, length us, event | category | flops | bytes accessed | tf_op | source)
XLA Modules:
  0.0 119.1 jit_solution(3172863388629846820)
XLA Ops:
  0.0 2.7 %cut.6 = bf16[1024,768]{1,0:T(8,128)(2,1)} custom-call(bf16[1024,256]{1,0:T(8,128)(2,1)} %kv.1, bf16[1024,1024]{1,0:T(8,128)(2,1)} %q.1), custom_call_target="tpu_custom_call" | custom-call | flops 1 | bytes 1 | tf_op jit(solution)/shard_map/cut/pallas_call | solution.py:181
  2.7 3.0 %collective-permute-start.5 = (bf16[1024,768]{1,0:T(8,128)(2,1)}, bf16[1024,768]{1,0:T(8,128)(2,1)}, u32[]{:S(2)}, u32[]{:S(2)}) collective-permute-start(bf16[1024,768]{1,0:T(8,128)(2,1)} %cut.6), channel_id=1, source_target_pairs={{0,8},{4,12},{8,0},{12,4},{16,24},{20,28},{24,16},{28,20},{1,9},{5... | collective-permute-start | bytes 4718600 | tf_op jit(solution)/shard_map/ppermute | solution.py:537
  5.7 1.5 %collective-permute-start.6 = (bf16[1024,768]{1,0:T(8,128)(2,1)}, bf16[1024,768]{1,0:T(8,128)(2,1)}, u32[]{:S(2)}, u32[]{:S(2)}) collective-permute-start(bf16[1024,768]{1,0:T(8,128)(2,1)} %cut.6), channel_id=1, source_target_pairs={{0,16},{4,20},{8,24},{12,28},{16,0},{20,4},{24,8},{28,12},{1,17},{... | collective-permute-start | bytes 4718600 | tf_op jit(solution)/shard_map/ppermute | solution.py:538
  7.2 0.4 norm_split.1
  7.7 0.1 collective-permute-start
  7.8 0.2 convert_reduce_fusion
  8.0 1.7 %collective-permute-done.refs_1_ = bf16[64,4096]{1,0:T(8,128)(2,1)S(1)} collective-permute-done((bf16[64,4096]{1,0:T(8,128)(2,1)S(1)}, bf16[64,4096]{1,0:T(8,128)(2,1)S(1)}, u32[]{:S(2)}, u32[]{:S(2)}) %collective-permute-start) | collective-permute-done | bytes 524320 | tf_op jit(solution)/shard_map/ppermute | solution.py:539
  9.6 0.1 cut.5.own.refs_0_
  9.7 1.6 %collective-permute-start.1 = (bf16[128,4096]{1,0:T(8,128)(2,1)S(1)}, bf16[128,4096]{1,0:T(8,128)(2,1)}, u32[]{:S(2)}, u32[]{:S(2)}) collective-permute-start(bf16[128,4096]{1,0:T(8,128)(2,1)S(1)} %cut.5.own.refs_0_), channel_id=1, source_target_pairs={{0,1},{1,0},{2,3},{3,2},{4,5},{5,4},{6,7},{7,6},{8,9},{9,8},{10,11... | collective-permute-start | bytes 3145736 | tf_op jit(solution)/shard_map/ppermute | solution.py:574
  11.4 2.6 %collective-permute-start.2 = (bf16[128,4096]{1,0:T(8,128)(2,1)S(1)}, bf16[128,4096]{1,0:T(8,128)(2,1)}, u32[]{:S(2)}, u32[]{:S(2)}) collective-permute-start(bf16[128,4096]{1,0:T(8,128)(2,1)S(1)} %cut.5.own.refs_0_), channel_id=1, source_target_pairs={{0,2},{1,3},{2,0},{3,1},{4,6},{5,7},{6,4},{7,5},{8,10},{9,11},{10,... | collective-permute-start | bytes 3145736 | tf_op jit(solution)/shard_map/ppermute | solution.py:574
  14.0 0.1 select_reduce_fusion
  14.1 0.1 copy.17
  14.2 27.7 %all_to_all.21 = s32[8,1,2]{2,1,0:T(1,128)S(1)} all-to-all(s32[8,1,2]{2,1,0:T(1,128)S(1)} %copy.17), channel_id=1, replica_groups=mesh['store'=8,'ctx'=4] {'store'}, dimensions={0} | all-to-all | bytes 128 | tf_op jit(solution)/shard_map/all_to_all | solution.py:51
  41.9 1.0 copy-done.4
  42.9 1.1 gather_blocks.1
  44.1 9.5 %all_to_all.22.refs_1_.blocks_ref = bf16[16,8,1024]{2,1,0:T(8,128)(2,1)S(1)} all-to-all(bf16[16,8,1024]{2,1,0:T(8,128)(2,1)S(1)} %gather_blocks.1), channel_id=1, replica_groups=mesh['store'=8,'ctx'=4] {'store'}, dimensions={0} | all-to-all | bytes 524288 | tf_op jit(solution)/shard_map/all_to_all | solution.py:556
  53.6 0.0 collective-permute-done.5.refs_2_.first_x.refs_1_
  53.6 1.2 cut.7.refs_0_
  54.8 0.6 collective-permute-start.7
  55.4 0.6 collective-permute-start.8
  56.0 0.6 sort_blocks.1
  56.6 0.0 copy-start.3
  56.6 0.7 copy-done.3
  57.3 4.9 %all-to-all-start.2 = ((bf16[4,128,256]{2,1,0:T(8,128)(2,1)}), bf16[4,128,256]{2,1,0:T(8,128)(2,1)S(1)}, u32[]{:S(2)}, u32[]{:S(2)}) async-start(bf16[4,128,256]{2,1,0:T(8,128)(2,1)} %copy-done.3), calls=%async_computation.2 | async-start | bytes 524288 | tf_op jit(solution)/shard_map/all_to_all | solution.py:562
  62.1 0.0 collective-permute-done.1.refs_0_.refs_1_
  62.1 0.0 collective-permute-done.2.two.refs_2_
  62.1 3.0 %relay.1 = (bf16[128,4096]{1,0:T(8,128)(2,1)}, bf16[128,4096]{1,0:T(8,128)(2,1)}) custom-call(bf16[128,4096]{1,0:T(8,128)(2,1)S(1)} %cut.5.own.refs_0_, bf16[128,4096]{1,0:T(8,128)(2,1)} %collective-permute-done.2.two.refs_2_, bf16[128,4096]{1,0:T(8,128)(2,1)} %collective-permute-done.1.refs_0_.refs_1_), custom_call_target="tpu_custom_call" | custom-call | flops 1 | bytes 1 | tf_op jit(solution)/shard_map/relay/pallas_call | solution.py:212
  65.1 1.7 %collective-permute-start.3 = (bf16[128,4096]{1,0:T(8,128)(2,1)}, bf16[128,4096]{1,0:T(8,128)(2,1)}, u32[]{:S(2)}, u32[]{:S(2)}) collective-permute-start(bf16[128,4096]{1,0:T(8,128)(2,1)} %get-tuple-element.32.refs_2_), channel_id=1, source_target_pairs={{1,2},{2,3},{5,6},{6,7},{9,10},{10,11},{13,14},{14,15},{17,18},{18... | collective-permute-start | bytes 3145736 | tf_op jit(solution)/shard_map/ppermute | solution.py:574
  66.8 1.3 %collective-permute-start.4 = (bf16[128,4096]{1,0:T(8,128)(2,1)}, bf16[128,4096]{1,0:T(8,128)(2,1)}, u32[]{:S(2)}, u32[]{:S(2)}) collective-permute-start(bf16[128,4096]{1,0:T(8,128)(2,1)} %get-tuple-element.33), channel_id=1, source_target_pairs={{2,1},{1,0},{6,5},{5,4},{10,9},{9,8},{14,13},{13,12},{18,17},{17,1... | collective-permute-start | bytes 3145736 | tf_op jit(solution)/shard_map/ppermute | solution.py:574
  68.1 2.4 %all-to-all-done.2 = bf16[4,128,256]{2,1,0:T(8,128)(2,1)S(1)} async-done(((bf16[4,128,256]{2,1,0:T(8,128)(2,1)}), bf16[4,128,256]{2,1,0:T(8,128)(2,1)S(1)}, u32[]{:S(2)}, u32[]{:S(2)}) %all-to-all-start.2) | async-done | bytes 262176 | tf_op jit(solution)/shard_map/all_to_all | solution.py:562
  70.5 1.4 %cut.9 = (bf16[512,768]{1,0:T(8,128)(2,1)S(1)}, bf16[512,768]{1,0:T(8,128)(2,1)S(1)}) custom-call(bf16[1024,768]{1,0:T(8,128)(2,1)} %collective-permute-done.6.refs_3_.first_y.refs_0_, bf16[1024,768]{1,0:T(8,128)(2,1)} %collective-permute-done.5.refs_2_.first_x.refs_1_, bf16[128,4096]{1,0:T(8,128)(2,1)} %get-tuple-element.32.refs_2_, ...), custom_call_target="tpu_custom_call" | custom-call | flops 1 | bytes 1 | tf_op jit(solution)/shard_map/cut/pallas_call | solution.py:181
  71.9 7.6 %collective-permute-done.7.last_y.refs_0_.refs_3_ = bf16[1024,512]{1,0:T(8,128)(2,1)} collective-permute-done((bf16[1024,512]{1,0:T(8,128)(2,1)}, bf16[1024,512]{1,0:T(8,128)(2,1)}, u32[]{:S(2)}, u32[]{:S(2)}) %collective-permute-start.7) | collective-permute-done | bytes 1048608 | tf_op jit(solution)/shard_map/ppermute | solution.py:538
  79.5 0.3 collective-permute-done.8.last_x.refs_1_.refs_2_
  79.8 1.2 collective-permute-start.11
  81.0 1.6 %collective-permute-start.12 = (bf16[512,768]{1,0:T(8,128)(2,1)S(1)}, bf16[512,768]{1,0:T(8,128)(2,1)S(1)}, u32[]{:S(2)}, u32[]{:S(2)}) collective-permute-start(bf16[512,768]{1,0:T(8,128)(2,1)S(1)} %get-tuple-element.42), channel_id=1, source_target_pairs={{0,16},{4,20},{8,24},{12,28},{16,0},{20,4},{24,8},{28,12},{1,17},{... | collective-permute-start | bytes 2359304 | tf_op jit(solution)/shard_map/ppermute | solution.py:538
  82.6 2.8 %load_weights.1 = (bf16[3072,1280]{1,0:T(8,128)(2,1)S(1)}, f32[8,128]{1,0:T(8,128)S(1)}) custom-call(bf16[1024,256]{1,0:T(8,128)(2,1)S(1)} %copy-done.1, bf16[1024,1024]{1,0:T(8,128)(2,1)S(1)} %copy-done, bf16[1024,768]{1,0:T(8,128)(2,1)} %collective-permute-done.5.refs_2_.first_x.refs_1_, bf16[1024,768]{1,0:T(8,128)(2,1)} %collective-permute-done.6.refs_3_.first_y.refs_0_, ...), custom_call_target="tpu_custom_call" | custom-call | flops 1 | bytes 1 | tf_op jit(solution)/shard_map/load_weights/pallas_call | solution.py:333
  85.4 1.2 %cut.8 = (bf16[512,512]{1,0:T(8,128)(2,1)S(1)}, bf16[512,512]{1,0:T(8,128)(2,1)S(1)}) custom-call(bf16[1024,512]{1,0:T(8,128)(2,1)} %collective-permute-done.7.last_y.refs_0_.refs_3_, bf16[1024,512]{1,0:T(8,128)(2,1)} %collective-permute-done.8.last_x.refs_1_.refs_2_, f32[8,128]{1,0:T(8,128)S(1)} %get-tuple-element.34.refs_2_), custom_call_target="tpu_custom_call" | custom-call | flops 1 | bytes 1 | tf_op jit(solution)/shard_map/cut/pallas_call | solution.py:181
  86.6 0.8 collective-permute-start.9
  87.4 0.6 collective-permute-start.10
  88.0 7.2 %collective-permute-done.4.refs_4_ = bf16[128,4096]{1,0:T(8,128)(2,1)} collective-permute-done((bf16[128,4096]{1,0:T(8,128)(2,1)}, bf16[128,4096]{1,0:T(8,128)(2,1)}, u32[]{:S(2)}, u32[]{:S(2)}) %collective-permute-start.4) | collective-permute-done | bytes 1048608 | tf_op jit(solution)/shard_map/ppermute | solution.py:574
  95.2 2.0 %load_rows.1.a_ref = bf16[512,4096]{1,0:T(8,128)(2,1)S(1)} custom-call(bf16[128,4096]{1,0:T(8,128)(2,1)S(1)} %cut.5.own.refs_0_, bf16[128,4096]{1,0:T(8,128)(2,1)} %collective-permute-done.1.refs_0_.refs_1_, bf16[128,4096]{1,0:T(8,128)(2,1)} %collective-permute-done.2.two.refs_2_, bf16[128,4096]{1,0:T(8,128)(2,1)} %collective-permute-done.3.refs_3_, ...), custom_call_target="tpu_custom_call" | custom-call | flops 1 | bytes 1 | tf_op jit(solution)/shard_map/load_rows/pallas_call | solution.py:302
  97.2 4.2 %project.3 = (f32[512,768]{1,0:T(8,128)S(1)}, f32[512,512]{1,0:T(8,128)S(1)}) custom-call(bf16[512,4096]{1,0:T(8,128)(2,1)S(1)} %load_rows.1.a_ref, bf16[3072,1280]{1,0:T(8,128)(2,1)S(1)} %get-tuple-element.37.w_ref), custom_call_target="tpu_custom_call" | custom-call | flops 1 | bytes 1 | tf_op jit(solution)/shard_map/project/pallas_call | solution.py:418
  101.4 0.0 collective-permute-done.12.d_y
  101.5 0.0 copy-start.5
  101.5 1.0 project.4
  102.5 0.1 collective-permute-start.13
  102.5 1.5 %collective-permute-done.13.sib = f32[256,256]{1,0:T(8,128)S(1)} collective-permute-done((f32[256,256]{1,0:T(8,128)S(1)}, f32[256,256]{1,0:T(8,128)S(1)}, u32[]{:S(2)}, u32[]{:S(2)}) %collective-permute-start.13) | collective-permute-done | bytes 262176 | tf_op jit(solution)/shard_map/ppermute | solution.py:539
  104.1 3.6 %collective-permute-start.14 = (bf16[256,128]{1,0:T(8,128)(2,1)S(1)}, bf16[256,128]{1,0:T(8,128)(2,1)S(1)}, u32[]{:S(2)}, u32[]{:S(2)}) collective-permute-start(bf16[256,128]{1,0:T(8,128)(2,1)S(1)} %get-tuple-element.46), channel_id=1, source_target_pairs={{0,1},{1,2},{2,0},{4,5},{5,6},{6,4},{8,9},{9,10},{10,8},{12,13},{1... | collective-permute-start | bytes 196616 | tf_op jit(solution)/shard_map/ppermute | solution.py:574
  107.7 0.7 collective-permute-start.15
  108.5 0.1 collective-permute-start.17
  108.5 0.4 collective-permute-done.9.d_x
  108.9 1.5 %collective-permute-done.10.d_y = bf16[512,512]{1,0:T(8,128)(2,1)S(1)} collective-permute-done((bf16[512,512]{1,0:T(8,128)(2,1)S(1)}, bf16[512,512]{1,0:T(8,128)(2,1)S(1)}, u32[]{:S(2)}, u32[]{:S(2)}) %collective-permute-start.10) | collective-permute-done | bytes 524320 | tf_op jit(solution)/shard_map/ppermute | solution.py:538
  110.4 0.7 collective-permute-done.14.refs_0_.first_ref
  111.2 0.0 collective-permute-done.15.refs_1_.second_ref
  111.2 0.7 project.5
  111.9 0.1 collective-permute-start.16
  112.0 0.1 fusion.13.refs_7_
  112.1 0.5 fusion.21
  112.6 0.1 pad_maximum_fusion
  112.7 0.4 assemble.1
  113.2 0.0 collective-permute-done.17.refs_1_
  113.2 3.0 %attend.2.refs_8_ = bf16[256,1024]{1,0:T(8,128)(2,1)} custom-call(f32[256,512]{1,0:T(8,128)S(1)} %get-tuple-element.53.refs_0_, f32[256,512]{1,0:T(8,128)S(1)} %collective-permute-done.17.refs_1_, bf16[512,128]{1,0:T(8,128)(2,1)S(1)} %get-tuple-element.51.refs_2_, bf16[128,512]{1,0:T(8,128)(2,1)S(1)} %get-tuple-element.52.refs_3_, ...), custom_call_target="tpu_custom_call" | custom-call | flops 1 | bytes 1 | tf_op jit(solution)/shard_map/attend/pallas_call | solution.py:513
  116.2 0.0 collective-permute-done.16.refs_1_
  116.2 3.0 %attend.3 = bf16[256,1024]{1,0:T(8,128)(2,1)} custom-call(f32[256,512]{1,0:T(8,128)S(1)} %get-tuple-element.48.refs_0_, f32[256,512]{1,0:T(8,128)S(1)} %collective-permute-done.16.refs_1_, bf16[512,128]{1,0:T(8,128)(2,1)S(1)} %get-tuple-element.51.refs_2_, bf16[128,512]{1,0:T(8,128)(2,1)S(1)} %get-tuple-element.52.refs_3_, ...), custom_call_target="tpu_custom_call", output_to_operand_aliasing={{}: (8, {})} | custom-call | flops 1 | bytes 1 | tf_op jit(solution)/shard_map/attend/pallas_call | solution.py:513
  (22 shorter events, 0.1 us)
Async XLA Ops:
  0.0 7.2 %copy-start.2 = (bf16[1,64,8192]{2,1,0:T(8,128)(2,1)S(1)}, bf16[1,64,8192]{2,1,0:T(8,128)(2,1)}, u32[]{:S(2)}) copy-start(bf16[1,64,8192]{2,1,0:T(8,128)(2,1)} %param.11) | copy-start | bytes 3145732
  0.0 7.7 %copy-start.7 = (s32[1,16]{1,0:T(1,128)S(1)}, s32[1,16]{1,0:T(1,128)}, u32[]{:S(2)}) copy-start(s32[1,16]{1,0:T(1,128)} %param.9) | copy-start | bytes 196
  2.7 50.9 %collective-permute-start.5 = (bf16[1024,768]{1,0:T(8,128)(2,1)}, bf16[1024,768]{1,0:T(8,128)(2,1)}, u32[]{:S(2)}, u32[]{:S(2)}) collective-permute-start(bf16[1024,768]{1,0:T(8,128)(2,1)} %cut.6), channel_id=1, source_target_pairs={{0,8},{4,12},{8,0},{12,4},{16,24},{20,28},{24,16},{28,20},{1,9},{5... | collective-permute-start | bytes 4718600 | tf_op jit(solution)/shard_map/ppermute | solution.py:537
  5.7 47.9 %collective-permute-start.6 = (bf16[1024,768]{1,0:T(8,128)(2,1)}, bf16[1024,768]{1,0:T(8,128)(2,1)}, u32[]{:S(2)}, u32[]{:S(2)}) collective-permute-start(bf16[1024,768]{1,0:T(8,128)(2,1)} %cut.6), channel_id=1, source_target_pairs={{0,16},{4,20},{8,24},{12,28},{16,0},{20,4},{24,8},{28,12},{1,17},{... | collective-permute-start | bytes 4718600 | tf_op jit(solution)/shard_map/ppermute | solution.py:538
  7.2 6.8 %copy-start.6 = (s32[1,16]{1,0:T(1,128)S(1)}, s32[1,16]{1,0:T(1,128)}, u32[]{:S(2)}) copy-start(s32[1,16]{1,0:T(1,128)} %param.8) | copy-start | bytes 196
  7.7 2.0 %collective-permute-start = (bf16[64,4096]{1,0:T(8,128)(2,1)S(1)}, bf16[64,4096]{1,0:T(8,128)(2,1)S(1)}, u32[]{:S(2)}, u32[]{:S(2)}) collective-permute-start(bf16[64,4096]{1,0:T(8,128)(2,1)S(1)} %get-tuple-element.31), channel_id=1, source_target_pairs={{0,4},{4,0},{8,12},{12,8},{16,20},{20,16},{24,28},{28,24},{1,5},{5... | collective-permute-start | bytes 1572872 | tf_op jit(solution)/shard_map/ppermute | solution.py:539
  9.6 44.0 %copy-start = (bf16[1024,1024]{1,0:T(8,128)(2,1)S(1)}, bf16[1024,1024]{1,0:T(8,128)(2,1)}, u32[]{:S(2)}) copy-start(bf16[1024,1024]{1,0:T(8,128)(2,1)} %q.1) | copy-start | bytes 6291460
  9.7 52.4 %collective-permute-start.1 = (bf16[128,4096]{1,0:T(8,128)(2,1)S(1)}, bf16[128,4096]{1,0:T(8,128)(2,1)}, u32[]{:S(2)}, u32[]{:S(2)}) collective-permute-start(bf16[128,4096]{1,0:T(8,128)(2,1)S(1)} %cut.5.own.refs_0_), channel_id=1, source_target_pairs={{0,1},{1,0},{2,3},{3,2},{4,5},{5,4},{6,7},{7,6},{8,9},{9,8},{10,11... | collective-permute-start | bytes 3145736 | tf_op jit(solution)/shard_map/ppermute | solution.py:574
  11.4 50.8 %collective-permute-start.2 = (bf16[128,4096]{1,0:T(8,128)(2,1)S(1)}, bf16[128,4096]{1,0:T(8,128)(2,1)}, u32[]{:S(2)}, u32[]{:S(2)}) collective-permute-start(bf16[128,4096]{1,0:T(8,128)(2,1)S(1)} %cut.5.own.refs_0_), channel_id=1, source_target_pairs={{0,2},{1,3},{2,0},{3,1},{4,6},{5,7},{6,4},{7,5},{8,10},{9,11},{10,... | collective-permute-start | bytes 3145736 | tf_op jit(solution)/shard_map/ppermute | solution.py:574
  41.9 1.0 copy-start.4
  54.8 24.7 %collective-permute-start.7 = (bf16[1024,512]{1,0:T(8,128)(2,1)}, bf16[1024,512]{1,0:T(8,128)(2,1)}, u32[]{:S(2)}, u32[]{:S(2)}) collective-permute-start(bf16[1024,512]{1,0:T(8,128)(2,1)} %cut.7.refs_0_), channel_id=1, source_target_pairs={{0,16},{4,20},{8,24},{12,28},{16,0},{20,4},{24,8},{28,12},{1,17},{... | collective-permute-start | bytes 3145736 | tf_op jit(solution)/shard_map/ppermute | solution.py:538
  55.4 24.4 %collective-permute-start.8 = (bf16[1024,512]{1,0:T(8,128)(2,1)}, bf16[1024,512]{1,0:T(8,128)(2,1)}, u32[]{:S(2)}, u32[]{:S(2)}) collective-permute-start(bf16[1024,512]{1,0:T(8,128)(2,1)} %cut.7.refs_0_), channel_id=1, source_target_pairs={{0,8},{4,12},{8,0},{12,4},{16,24},{20,28},{24,16},{28,20},{1,9},{5... | collective-permute-start | bytes 3145736 | tf_op jit(solution)/shard_map/ppermute | solution.py:537
  56.6 0.7 copy-start.3
  57.3 13.2 %all-to-all-start.2 = ((bf16[4,128,256]{2,1,0:T(8,128)(2,1)}), bf16[4,128,256]{2,1,0:T(8,128)(2,1)S(1)}, u32[]{:S(2)}, u32[]{:S(2)}) async-start(bf16[4,128,256]{2,1,0:T(8,128)(2,1)} %copy-done.3), calls=%async_computation.2 | async-start | bytes 524288 | tf_op jit(solution)/shard_map/all_to_all | solution.py:562
  65.1 22.3 %collective-permute-start.3 = (bf16[128,4096]{1,0:T(8,128)(2,1)}, bf16[128,4096]{1,0:T(8,128)(2,1)}, u32[]{:S(2)}, u32[]{:S(2)}) collective-permute-start(bf16[128,4096]{1,0:T(8,128)(2,1)} %get-tuple-element.32.refs_2_), channel_id=1, source_target_pairs={{1,2},{2,3},{5,6},{6,7},{9,10},{10,11},{13,14},{14,15},{17,18},{18... | collective-permute-start | bytes 3145736 | tf_op jit(solution)/shard_map/ppermute | solution.py:574
  66.8 28.4 %collective-permute-start.4 = (bf16[128,4096]{1,0:T(8,128)(2,1)}, bf16[128,4096]{1,0:T(8,128)(2,1)}, u32[]{:S(2)}, u32[]{:S(2)}) collective-permute-start(bf16[128,4096]{1,0:T(8,128)(2,1)} %get-tuple-element.33), channel_id=1, source_target_pairs={{2,1},{1,0},{6,5},{5,4},{10,9},{9,8},{14,13},{13,12},{18,17},{17,1... | collective-permute-start | bytes 3145736 | tf_op jit(solution)/shard_map/ppermute | solution.py:574
  79.8 2.8 %copy-start.1 = (bf16[1024,256]{1,0:T(8,128)(2,1)S(1)}, bf16[1024,256]{1,0:T(8,128)(2,1)}, u32[]{:S(2)}) copy-start(bf16[1024,256]{1,0:T(8,128)(2,1)} %kv.1) | copy-start | bytes 1572868
  79.8 21.6 %collective-permute-start.11 = (bf16[512,768]{1,0:T(8,128)(2,1)S(1)}, bf16[512,768]{1,0:T(8,128)(2,1)S(1)}, u32[]{:S(2)}, u32[]{:S(2)}) collective-permute-start(bf16[512,768]{1,0:T(8,128)(2,1)S(1)} %get-tuple-element.41), channel_id=1, source_target_pairs={{0,8},{4,12},{8,0},{12,4},{16,24},{20,28},{24,16},{28,20},{1,9},{5... | collective-permute-start | bytes 2359304 | tf_op jit(solution)/shard_map/ppermute | solution.py:537
  81.0 20.5 %collective-permute-start.12 = (bf16[512,768]{1,0:T(8,128)(2,1)S(1)}, bf16[512,768]{1,0:T(8,128)(2,1)S(1)}, u32[]{:S(2)}, u32[]{:S(2)}) collective-permute-start(bf16[512,768]{1,0:T(8,128)(2,1)S(1)} %get-tuple-element.42), channel_id=1, source_target_pairs={{0,16},{4,20},{8,24},{12,28},{16,0},{20,4},{24,8},{28,12},{1,17},{... | collective-permute-start | bytes 2359304 | tf_op jit(solution)/shard_map/ppermute | solution.py:538
  86.6 22.3 %collective-permute-start.9 = (bf16[512,512]{1,0:T(8,128)(2,1)S(1)}, bf16[512,512]{1,0:T(8,128)(2,1)S(1)}, u32[]{:S(2)}, u32[]{:S(2)}) collective-permute-start(bf16[512,512]{1,0:T(8,128)(2,1)S(1)} %get-tuple-element.35.refs_5_), channel_id=1, source_target_pairs={{0,8},{4,12},{8,0},{12,4},{16,24},{20,28},{24,16},{28,20},{1,9},{5... | collective-permute-start | bytes 1572872 | tf_op jit(solution)/shard_map/ppermute | solution.py:537
  87.4 23.0 %collective-permute-start.10 = (bf16[512,512]{1,0:T(8,128)(2,1)S(1)}, bf16[512,512]{1,0:T(8,128)(2,1)S(1)}, u32[]{:S(2)}, u32[]{:S(2)}) collective-permute-start(bf16[512,512]{1,0:T(8,128)(2,1)S(1)} %get-tuple-element.36), channel_id=1, source_target_pairs={{0,16},{4,20},{8,24},{12,28},{16,0},{20,4},{24,8},{28,12},{1,17},{... | collective-permute-start | bytes 1572872 | tf_op jit(solution)/shard_map/ppermute | solution.py:538
  101.5 7.0 %copy-start.5 = (s32[1,256]{1,0:T(1,128)S(1)}, s32[1,256]{1,0:T(1,128)}, u32[]{:S(2)}) copy-start(s32[1,256]{1,0:T(1,128)} %refs_6_.3) | copy-start | bytes 3076
  102.5 1.6 %collective-permute-start.13 = (f32[256,256]{1,0:T(8,128)S(1)}, f32[256,256]{1,0:T(8,128)S(1)}, u32[]{:S(2)}, u32[]{:S(2)}) collective-permute-start(f32[256,256]{1,0:T(8,128)S(1)} %get-tuple-element.45), channel_id=1, source_target_pairs={{0,4},{4,0},{8,12},{12,8},{16,20},{20,16},{24,28},{28,24},{1,5},{5... | collective-permute-start | bytes 786440 | tf_op jit(solution)/shard_map/ppermute | solution.py:539
  104.1 7.1 %collective-permute-start.14 = (bf16[256,128]{1,0:T(8,128)(2,1)S(1)}, bf16[256,128]{1,0:T(8,128)(2,1)S(1)}, u32[]{:S(2)}, u32[]{:S(2)}) collective-permute-start(bf16[256,128]{1,0:T(8,128)(2,1)S(1)} %get-tuple-element.46), channel_id=1, source_target_pairs={{0,1},{1,2},{2,0},{4,5},{5,6},{6,4},{8,9},{9,10},{10,8},{12,13},{1... | collective-permute-start | bytes 196616 | tf_op jit(solution)/shard_map/ppermute | solution.py:574
  107.7 3.4 %collective-permute-start.15 = (bf16[256,128]{1,0:T(8,128)(2,1)S(1)}, bf16[256,128]{1,0:T(8,128)(2,1)S(1)}, u32[]{:S(2)}, u32[]{:S(2)}) collective-permute-start(bf16[256,128]{1,0:T(8,128)(2,1)S(1)} %get-tuple-element.47), channel_id=1, source_target_pairs={{1,3},{2,1},{3,2},{5,7},{6,5},{7,6},{9,11},{10,9},{11,10},{13,15},... | collective-permute-start | bytes 196616 | tf_op jit(solution)/shard_map/ppermute | solution.py:574
  108.5 4.7 %collective-permute-start.17 = (f32[256,512]{1,0:T(8,128)S(1)}, f32[256,512]{1,0:T(8,128)S(1)}, u32[]{:S(2)}, u32[]{:S(2)}) collective-permute-start(f32[256,512]{1,0:T(8,128)S(1)} %get-tuple-element.54), channel_id=1, source_target_pairs={{0,4},{4,0},{8,12},{12,8},{16,20},{20,16},{24,28},{28,24},{1,5},{5... | collective-permute-start | bytes 1572872 | tf_op jit(solution)/shard_map/ppermute | solution.py:539
  111.9 4.3 %collective-permute-start.16 = (f32[256,512]{1,0:T(8,128)S(1)}, f32[256,512]{1,0:T(8,128)S(1)}, u32[]{:S(2)}, u32[]{:S(2)}) collective-permute-start(f32[256,512]{1,0:T(8,128)S(1)} %get-tuple-element.49), channel_id=1, source_target_pairs={{0,4},{4,0},{8,12},{12,8},{16,20},{20,16},{24,28},{28,24},{1,5},{5... | collective-permute-start | bytes 1572872 | tf_op jit(solution)/shard_map/ppermute | solution.py:539

commit v6 on v5

--- a/solution.py
+++ b/solution.py
@@ -224,12 +224,14 @@
     out_ref = refs[-1]
     heads = out_ref.shape[0]
     size = blocks_ref.shape[1]
-    for j in range(places_ref.shape[0]):
-        block = blocks_ref[places_ref[j]]
+    for j in range(0, places_ref.shape[0], 2):
+        pair = jnp.concatenate(
+            [blocks_ref[places_ref[j + i]].astype(F32) for i in range(2)], axis=0
+        ).astype(BF16)
+        rows = slice(j * size, (j + 2) * size)
         for h in range(heads):
-            rows = slice(j * size, (j + 1) * size)
-            out_ref[h, rows, :HD] = block[:, h * HD : (h + 1) * HD]
-            out_ref[h, rows, HD:] = block[:, (heads + h) * HD : (heads + h + 1) * HD]
+            out_ref[h, rows, :HD] = pair[:, h * HD : (h + 1) * HD]
+            out_ref[h, rows, HD:] = pair[:, (heads + h) * HD : (heads + h + 1) * HD]
 
 
 def sort_blocks(blocks, places, gates):

time: 122 us -> 122 us (level)
  no operation moved by 1% of the time
where the time goes in v6:
time: 122 us; the launch traced here: 119 us
  blocking collectives  37.2 us (30%)
  Pallas kernels  28.8 us (24%)
  starting transfers between devices  26.5 us (22%)
  waiting for transfers between devices  23.4 us (19%)
  local copies, waits for them, and re-layouts  1.85 us (2%)
    all_to_all x1, blocking collectives, swap_ids(): lax.all_to_all(wanted, 'store', split_axis=0, concat_axis=0, tiled=True)  27.7 us
    ppermute x6, starting transfers between devices, fast_body(): along = lambda a, pairs: lax.ppermute(a, 'ctx', pairs)  11.5 us
    all_to_all x1, blocking collectives, fast_body(): lax.all_to_all(gathered, 'store', split_axis=0, concat_axis=0, tiled=True)  9.53 us
    ppermute x4, waiting for transfers between devices, fast_body(): by_y = lambda a: lax.ppermute(a, 'store', yf)  9.08 us
    ppermute x6, waiting for transfers between devices, fast_body(): along = lambda a, pairs: lax.ppermute(a, 'ctx', pairs)  7.99 us
    pallas_call x5, Pallas kernels, cut(): pl.pallas_call(functools.partial(cut_kernel, plan, len(args)), in_specs=[...  6.52 us
    pallas_call x2, Pallas kernels, attend(): pl.pallas_call(functools.partial(attend_kernel, cols // HD), grid=(1,), i...  5.97 us
    pallas_call x3, Pallas kernels, project(): pl.pallas_call(kernel, in_specs=[vmem] * len(near) + [pl.BlockSpec(memory...  5.9 us
  transfers between devices with their start and end apart: 19, of which 9 were waited for; matrix products, arithmetic and copies ran while one was open for 1% of the time, Pallas kernels for 19%

profile of v6, /device:TPU:0, one launch (start us, length us, event | category | flops | bytes accessed | tf_op | source)
XLA Modules:
  0.0 119.1 jit_solution(4845364146384420584)
XLA Ops:
  0.0 2.7 %cut.6 = bf16[1024,768]{1,0:T(8,128)(2,1)} custom-call(bf16[1024,256]{1,0:T(8,128)(2,1)} %kv.1, bf16[1024,1024]{1,0:T(8,128)(2,1)} %q.1), custom_call_target="tpu_custom_call" | custom-call | flops 1 | bytes 1 | tf_op jit(solution)/shard_map/cut/pallas_call | solution.py:181
  2.7 3.0 %collective-permute-start.5 = (bf16[1024,768]{1,0:T(8,128)(2,1)}, bf16[1024,768]{1,0:T(8,128)(2,1)}, u32[]{:S(2)}, u32[]{:S(2)}) collective-permute-start(bf16[1024,768]{1,0:T(8,128)(2,1)} %cut.6), channel_id=1, source_target_pairs={{0,8},{4,12},{8,0},{12,4},{16,24},{20,28},{24,16},{28,20},{1,9},{5... | collective-permute-start | bytes 4718600 | tf_op jit(solution)/shard_map/ppermute | solution.py:539
  5.7 1.5 %collective-permute-start.6 = (bf16[1024,768]{1,0:T(8,128)(2,1)}, bf16[1024,768]{1,0:T(8,128)(2,1)}, u32[]{:S(2)}, u32[]{:S(2)}) collective-permute-start(bf16[1024,768]{1,0:T(8,128)(2,1)} %cut.6), channel_id=1, source_target_pairs={{0,16},{4,20},{8,24},{12,28},{16,0},{20,4},{24,8},{28,12},{1,17},{... | collective-permute-start | bytes 4718600 | tf_op jit(solution)/shard_map/ppermute | solution.py:540
  7.2 0.4 norm_split.1
  7.7 0.1 collective-permute-start
  7.8 0.2 convert_reduce_fusion
  8.0 1.7 %collective-permute-done.refs_1_ = bf16[64,4096]{1,0:T(8,128)(2,1)S(1)} collective-permute-done((bf16[64,4096]{1,0:T(8,128)(2,1)S(1)}, bf16[64,4096]{1,0:T(8,128)(2,1)S(1)}, u32[]{:S(2)}, u32[]{:S(2)}) %collective-permute-start) | collective-permute-done | bytes 524320 | tf_op jit(solution)/shard_map/ppermute | solution.py:541
  9.6 0.1 cut.5.own.refs_0_
  9.7 1.6 %collective-permute-start.1 = (bf16[128,4096]{1,0:T(8,128)(2,1)S(1)}, bf16[128,4096]{1,0:T(8,128)(2,1)}, u32[]{:S(2)}, u32[]{:S(2)}) collective-permute-start(bf16[128,4096]{1,0:T(8,128)(2,1)S(1)} %cut.5.own.refs_0_), channel_id=1, source_target_pairs={{0,1},{1,0},{2,3},{3,2},{4,5},{5,4},{6,7},{7,6},{8,9},{9,8},{10,11... | collective-permute-start | bytes 3145736 | tf_op jit(solution)/shard_map/ppermute | solution.py:576
  11.4 2.6 %collective-permute-start.2 = (bf16[128,4096]{1,0:T(8,128)(2,1)S(1)}, bf16[128,4096]{1,0:T(8,128)(2,1)}, u32[]{:S(2)}, u32[]{:S(2)}) collective-permute-start(bf16[128,4096]{1,0:T(8,128)(2,1)S(1)} %cut.5.own.refs_0_), channel_id=1, source_target_pairs={{0,2},{1,3},{2,0},{3,1},{4,6},{5,7},{6,4},{7,5},{8,10},{9,11},{10,... | collective-permute-start | bytes 3145736 | tf_op jit(solution)/shard_map/ppermute | solution.py:576
  14.0 0.1 select_reduce_fusion
  14.1 0.1 copy.17
  14.2 27.7 %all_to_all.21 = s32[8,1,2]{2,1,0:T(1,128)S(1)} all-to-all(s32[8,1,2]{2,1,0:T(1,128)S(1)} %copy.17), channel_id=1, replica_groups=mesh['store'=8,'ctx'=4] {'store'}, dimensions={0} | all-to-all | bytes 128 | tf_op jit(solution)/shard_map/all_to_all | solution.py:51
  41.9 1.0 copy-done.4
  42.9 1.1 gather_blocks.1
  44.1 9.5 %all_to_all.22.refs_1_.blocks_ref = bf16[16,8,1024]{2,1,0:T(8,128)(2,1)S(1)} all-to-all(bf16[16,8,1024]{2,1,0:T(8,128)(2,1)S(1)} %gather_blocks.1), channel_id=1, replica_groups=mesh['store'=8,'ctx'=4] {'store'}, dimensions={0} | all-to-all | bytes 524288 | tf_op jit(solution)/shard_map/all_to_all | solution.py:558
  53.6 0.0 collective-permute-done.5.refs_2_.first_x.refs_1_
  53.6 0.0 collective-permute-done.6.refs_3_.first_y.refs_0_
  53.6 1.2 cut.7.refs_0_
  54.8 0.6 collective-permute-start.7
  55.4 0.6 collective-permute-start.8
  56.0 0.6 sort_blocks.1
  56.6 0.0 copy-start.3
  56.6 0.7 copy-done.3
  57.3 4.9 %all-to-all-start.2 = ((bf16[4,128,256]{2,1,0:T(8,128)(2,1)}), bf16[4,128,256]{2,1,0:T(8,128)(2,1)S(1)}, u32[]{:S(2)}, u32[]{:S(2)}) async-start(bf16[4,128,256]{2,1,0:T(8,128)(2,1)} %copy-done.3), calls=%async_computation.2 | async-start | bytes 524288 | tf_op jit(solution)/shard_map/all_to_all | solution.py:564
  62.1 0.0 collective-permute-done.1.refs_0_.refs_1_
  62.1 0.0 collective-permute-done.2.two.refs_2_
  62.1 3.0 %relay.1 = (bf16[128,4096]{1,0:T(8,128)(2,1)}, bf16[128,4096]{1,0:T(8,128)(2,1)}) custom-call(bf16[128,4096]{1,0:T(8,128)(2,1)S(1)} %cut.5.own.refs_0_, bf16[128,4096]{1,0:T(8,128)(2,1)} %collective-permute-done.2.two.refs_2_, bf16[128,4096]{1,0:T(8,128)(2,1)} %collective-permute-done.1.refs_0_.refs_1_), custom_call_target="tpu_custom_call" | custom-call | flops 1 | bytes 1 | tf_op jit(solution)/shard_map/relay/pallas_call | solution.py:212
  65.1 1.7 %collective-permute-start.3 = (bf16[128,4096]{1,0:T(8,128)(2,1)}, bf16[128,4096]{1,0:T(8,128)(2,1)}, u32[]{:S(2)}, u32[]{:S(2)}) collective-permute-start(bf16[128,4096]{1,0:T(8,128)(2,1)} %get-tuple-element.32.refs_2_), channel_id=1, source_target_pairs={{1,2},{2,3},{5,6},{6,7},{9,10},{10,11},{13,14},{14,15},{17,18},{18... | collective-permute-start | bytes 3145736 | tf_op jit(solution)/shard_map/ppermute | solution.py:576
  66.8 1.3 %collective-permute-start.4 = (bf16[128,4096]{1,0:T(8,128)(2,1)}, bf16[128,4096]{1,0:T(8,128)(2,1)}, u32[]{:S(2)}, u32[]{:S(2)}) collective-permute-start(bf16[128,4096]{1,0:T(8,128)(2,1)} %get-tuple-element.33), channel_id=1, source_target_pairs={{2,1},{1,0},{6,5},{5,4},{10,9},{9,8},{14,13},{13,12},{18,17},{17,1... | collective-permute-start | bytes 3145736 | tf_op jit(solution)/shard_map/ppermute | solution.py:576
  68.1 2.4 %all-to-all-done.2 = bf16[4,128,256]{2,1,0:T(8,128)(2,1)S(1)} async-done(((bf16[4,128,256]{2,1,0:T(8,128)(2,1)}), bf16[4,128,256]{2,1,0:T(8,128)(2,1)S(1)}, u32[]{:S(2)}, u32[]{:S(2)}) %all-to-all-start.2) | async-done | bytes 262176 | tf_op jit(solution)/shard_map/all_to_all | solution.py:564
  70.5 1.4 %cut.9 = (bf16[512,768]{1,0:T(8,128)(2,1)S(1)}, bf16[512,768]{1,0:T(8,128)(2,1)S(1)}) custom-call(bf16[1024,768]{1,0:T(8,128)(2,1)} %collective-permute-done.6.refs_3_.first_y.refs_0_, bf16[1024,768]{1,0:T(8,128)(2,1)} %collective-permute-done.5.refs_2_.first_x.refs_1_, bf16[128,4096]{1,0:T(8,128)(2,1)} %get-tuple-element.32.refs_2_, ...), custom_call_target="tpu_custom_call" | custom-call | flops 1 | bytes 1 | tf_op jit(solution)/shard_map/cut/pallas_call | solution.py:181
  71.9 7.6 %collective-permute-done.7.last_y.refs_0_.refs_3_ = bf16[1024,512]{1,0:T(8,128)(2,1)} collective-permute-done((bf16[1024,512]{1,0:T(8,128)(2,1)}, bf16[1024,512]{1,0:T(8,128)(2,1)}, u32[]{:S(2)}, u32[]{:S(2)}) %collective-permute-start.7) | collective-permute-done | bytes 1048608 | tf_op jit(solution)/shard_map/ppermute | solution.py:540
  79.5 0.3 collective-permute-done.8.last_x.refs_1_.refs_2_
  79.8 1.2 collective-permute-start.11
  81.0 1.6 %collective-permute-start.12 = (bf16[512,768]{1,0:T(8,128)(2,1)S(1)}, bf16[512,768]{1,0:T(8,128)(2,1)S(1)}, u32[]{:S(2)}, u32[]{:S(2)}) collective-permute-start(bf16[512,768]{1,0:T(8,128)(2,1)S(1)} %get-tuple-element.42), channel_id=1, source_target_pairs={{0,16},{4,20},{8,24},{12,28},{16,0},{20,4},{24,8},{28,12},{1,17},{... | collective-permute-start | bytes 2359304 | tf_op jit(solution)/shard_map/ppermute | solution.py:540
  82.6 2.8 %load_weights.1 = (bf16[3072,1280]{1,0:T(8,128)(2,1)S(1)}, f32[8,128]{1,0:T(8,128)S(1)}) custom-call(bf16[1024,256]{1,0:T(8,128)(2,1)S(1)} %copy-done.1, bf16[1024,1024]{1,0:T(8,128)(2,1)S(1)} %copy-done, bf16[1024,768]{1,0:T(8,128)(2,1)} %collective-permute-done.5.refs_2_.first_x.refs_1_, bf16[1024,768]{1,0:T(8,128)(2,1)} %collective-permute-done.6.refs_3_.first_y.refs_0_, ...), custom_call_target="tpu_custom_call" | custom-call | flops 1 | bytes 1 | tf_op jit(solution)/shard_map/load_weights/pallas_call | solution.py:335
  85.4 1.2 %cut.8 = (bf16[512,512]{1,0:T(8,128)(2,1)S(1)}, bf16[512,512]{1,0:T(8,128)(2,1)S(1)}) custom-call(bf16[1024,512]{1,0:T(8,128)(2,1)} %collective-permute-done.7.last_y.refs_0_.refs_3_, bf16[1024,512]{1,0:T(8,128)(2,1)} %collective-permute-done.8.last_x.refs_1_.refs_2_, f32[8,128]{1,0:T(8,128)S(1)} %get-tuple-element.34.refs_2_), custom_call_target="tpu_custom_call" | custom-call | flops 1 | bytes 1 | tf_op jit(solution)/shard_map/cut/pallas_call | solution.py:181
  86.6 0.8 collective-permute-start.9
  87.4 0.6 collective-permute-start.10
  88.0 7.2 %collective-permute-done.4.refs_4_ = bf16[128,4096]{1,0:T(8,128)(2,1)} collective-permute-done((bf16[128,4096]{1,0:T(8,128)(2,1)}, bf16[128,4096]{1,0:T(8,128)(2,1)}, u32[]{:S(2)}, u32[]{:S(2)}) %collective-permute-start.4) | collective-permute-done | bytes 1048608 | tf_op jit(solution)/shard_map/ppermute | solution.py:576
  95.2 2.0 %load_rows.1.a_ref = bf16[512,4096]{1,0:T(8,128)(2,1)S(1)} custom-call(bf16[128,4096]{1,0:T(8,128)(2,1)S(1)} %cut.5.own.refs_0_, bf16[128,4096]{1,0:T(8,128)(2,1)} %collective-permute-done.1.refs_0_.refs_1_, bf16[128,4096]{1,0:T(8,128)(2,1)} %collective-permute-done.2.two.refs_2_, bf16[128,4096]{1,0:T(8,128)(2,1)} %collective-permute-done.3.refs_3_, ...), custom_call_target="tpu_custom_call" | custom-call | flops 1 | bytes 1 | tf_op jit(solution)/shard_map/load_rows/pallas_call | solution.py:304
  97.2 4.2 %project.3 = (f32[512,768]{1,0:T(8,128)S(1)}, f32[512,512]{1,0:T(8,128)S(1)}) custom-call(bf16[512,4096]{1,0:T(8,128)(2,1)S(1)} %load_rows.1.a_ref, bf16[3072,1280]{1,0:T(8,128)(2,1)S(1)} %get-tuple-element.37.w_ref), custom_call_target="tpu_custom_call" | custom-call | flops 1 | bytes 1 | tf_op jit(solution)/shard_map/project/pallas_call | solution.py:420
  101.4 0.0 collective-permute-done.12.d_y
  101.5 1.0 project.4
  102.4 0.1 collective-permute-start.13
  102.5 1.5 %collective-permute-done.13.sib = f32[256,256]{1,0:T(8,128)S(1)} collective-permute-done((f32[256,256]{1,0:T(8,128)S(1)}, f32[256,256]{1,0:T(8,128)S(1)}, u32[]{:S(2)}, u32[]{:S(2)}) %collective-permute-start.13) | collective-permute-done | bytes 262176 | tf_op jit(solution)/shard_map/ppermute | solution.py:541
  104.1 3.6 %collective-permute-start.14 = (bf16[256,128]{1,0:T(8,128)(2,1)S(1)}, bf16[256,128]{1,0:T(8,128)(2,1)S(1)}, u32[]{:S(2)}, u32[]{:S(2)}) collective-permute-start(bf16[256,128]{1,0:T(8,128)(2,1)S(1)} %get-tuple-element.46), channel_id=1, source_target_pairs={{0,1},{1,2},{2,0},{4,5},{5,6},{6,4},{8,9},{9,10},{10,8},{12,13},{1... | collective-permute-start | bytes 196616 | tf_op jit(solution)/shard_map/ppermute | solution.py:576
  107.7 0.7 collective-permute-start.15
  108.5 0.1 collective-permute-start.17
  108.5 0.4 collective-permute-done.9.d_x
  108.9 1.5 %collective-permute-done.10.d_y = bf16[512,512]{1,0:T(8,128)(2,1)S(1)} collective-permute-done((bf16[512,512]{1,0:T(8,128)(2,1)S(1)}, bf16[512,512]{1,0:T(8,128)(2,1)S(1)}, u32[]{:S(2)}, u32[]{:S(2)}) %collective-permute-start.10) | collective-permute-done | bytes 524320 | tf_op jit(solution)/shard_map/ppermute | solution.py:540
  110.4 0.7 collective-permute-done.14.refs_0_.first_ref
  111.2 0.0 collective-permute-done.15.refs_1_.second_ref
  111.2 0.7 project.5
  111.9 0.1 collective-permute-start.16
  112.0 0.1 fusion.13.refs_7_
  112.1 0.5 fusion.21
  112.6 0.1 pad_maximum_fusion
  112.7 0.4 assemble.1
  113.2 0.0 collective-permute-done.17.refs_1_
  113.2 3.0 %attend.2.refs_8_ = bf16[256,1024]{1,0:T(8,128)(2,1)} custom-call(f32[256,512]{1,0:T(8,128)S(1)} %get-tuple-element.53.refs_0_, f32[256,512]{1,0:T(8,128)S(1)} %collective-permute-done.17.refs_1_, bf16[512,128]{1,0:T(8,128)(2,1)S(1)} %get-tuple-element.51.refs_2_, bf16[128,512]{1,0:T(8,128)(2,1)S(1)} %get-tuple-element.52.refs_3_, ...), custom_call_target="tpu_custom_call" | custom-call | flops 1 | bytes 1 | tf_op jit(solution)/shard_map/attend/pallas_call | solution.py:515
  116.2 0.0 collective-permute-done.16.refs_1_
  116.2 3.0 %attend.3 = bf16[256,1024]{1,0:T(8,128)(2,1)} custom-call(f32[256,512]{1,0:T(8,128)S(1)} %get-tuple-element.48.refs_0_, f32[256,512]{1,0:T(8,128)S(1)} %collective-permute-done.16.refs_1_, bf16[512,128]{1,0:T(8,128)(2,1)S(1)} %get-tuple-element.51.refs_2_, bf16[128,512]{1,0:T(8,128)(2,1)S(1)} %get-tuple-element.52.refs_3_, ...), custom_call_target="tpu_custom_call", output_to_operand_aliasing={{}: (8, {})} | custom-call | flops 1 | bytes 1 | tf_op jit(solution)/shard_map/attend/pallas_call | solution.py:515
  (22 shorter events, 0.1 us)
Async XLA Ops:
  0.0 7.2 %copy-start.2 = (bf16[1,64,8192]{2,1,0:T(8,128)(2,1)S(1)}, bf16[1,64,8192]{2,1,0:T(8,128)(2,1)}, u32[]{:S(2)}) copy-start(bf16[1,64,8192]{2,1,0:T(8,128)(2,1)} %param.11) | copy-start | bytes 3145732
  0.0 7.7 %copy-start.7 = (s32[1,16]{1,0:T(1,128)S(1)}, s32[1,16]{1,0:T(1,128)}, u32[]{:S(2)}) copy-start(s32[1,16]{1,0:T(1,128)} %param.9) | copy-start | bytes 196
  2.7 50.9 %collective-permute-start.5 = (bf16[1024,768]{1,0:T(8,128)(2,1)}, bf16[1024,768]{1,0:T(8,128)(2,1)}, u32[]{:S(2)}, u32[]{:S(2)}) collective-permute-start(bf16[1024,768]{1,0:T(8,128)(2,1)} %cut.6), channel_id=1, source_target_pairs={{0,8},{4,12},{8,0},{12,4},{16,24},{20,28},{24,16},{28,20},{1,9},{5... | collective-permute-start | bytes 4718600 | tf_op jit(solution)/shard_map/ppermute | solution.py:539
  5.7 47.9 %collective-permute-start.6 = (bf16[1024,768]{1,0:T(8,128)(2,1)}, bf16[1024,768]{1,0:T(8,128)(2,1)}, u32[]{:S(2)}, u32[]{:S(2)}) collective-permute-start(bf16[1024,768]{1,0:T(8,128)(2,1)} %cut.6), channel_id=1, source_target_pairs={{0,16},{4,20},{8,24},{12,28},{16,0},{20,4},{24,8},{28,12},{1,17},{... | collective-permute-start | bytes 4718600 | tf_op jit(solution)/shard_map/ppermute | solution.py:540
  7.2 6.8 %copy-start.6 = (s32[1,16]{1,0:T(1,128)S(1)}, s32[1,16]{1,0:T(1,128)}, u32[]{:S(2)}) copy-start(s32[1,16]{1,0:T(1,128)} %param.8) | copy-start | bytes 196
  7.7 2.0 %collective-permute-start = (bf16[64,4096]{1,0:T(8,128)(2,1)S(1)}, bf16[64,4096]{1,0:T(8,128)(2,1)S(1)}, u32[]{:S(2)}, u32[]{:S(2)}) collective-permute-start(bf16[64,4096]{1,0:T(8,128)(2,1)S(1)} %get-tuple-element.31), channel_id=1, source_target_pairs={{0,4},{4,0},{8,12},{12,8},{16,20},{20,16},{24,28},{28,24},{1,5},{5... | collective-permute-start | bytes 1572872 | tf_op jit(solution)/shard_map/ppermute | solution.py:541
  9.6 44.0 %copy-start = (bf16[1024,1024]{1,0:T(8,128)(2,1)S(1)}, bf16[1024,1024]{1,0:T(8,128)(2,1)}, u32[]{:S(2)}) copy-start(bf16[1024,1024]{1,0:T(8,128)(2,1)} %q.1) | copy-start | bytes 6291460
  9.7 52.4 %collective-permute-start.1 = (bf16[128,4096]{1,0:T(8,128)(2,1)S(1)}, bf16[128,4096]{1,0:T(8,128)(2,1)}, u32[]{:S(2)}, u32[]{:S(2)}) collective-permute-start(bf16[128,4096]{1,0:T(8,128)(2,1)S(1)} %cut.5.own.refs_0_), channel_id=1, source_target_pairs={{0,1},{1,0},{2,3},{3,2},{4,5},{5,4},{6,7},{7,6},{8,9},{9,8},{10,11... | collective-permute-start | bytes 3145736 | tf_op jit(solution)/shard_map/ppermute | solution.py:576
  11.4 50.8 %collective-permute-start.2 = (bf16[128,4096]{1,0:T(8,128)(2,1)S(1)}, bf16[128,4096]{1,0:T(8,128)(2,1)}, u32[]{:S(2)}, u32[]{:S(2)}) collective-permute-start(bf16[128,4096]{1,0:T(8,128)(2,1)S(1)} %cut.5.own.refs_0_), channel_id=1, source_target_pairs={{0,2},{1,3},{2,0},{3,1},{4,6},{5,7},{6,4},{7,5},{8,10},{9,11},{10,... | collective-permute-start | bytes 3145736 | tf_op jit(solution)/shard_map/ppermute | solution.py:576
  41.9 1.0 copy-start.4
  54.8 24.7 %collective-permute-start.7 = (bf16[1024,512]{1,0:T(8,128)(2,1)}, bf16[1024,512]{1,0:T(8,128)(2,1)}, u32[]{:S(2)}, u32[]{:S(2)}) collective-permute-start(bf16[1024,512]{1,0:T(8,128)(2,1)} %cut.7.refs_0_), channel_id=1, source_target_pairs={{0,16},{4,20},{8,24},{12,28},{16,0},{20,4},{24,8},{28,12},{1,17},{... | collective-permute-start | bytes 3145736 | tf_op jit(solution)/shard_map/ppermute | solution.py:540
  55.4 24.4 %collective-permute-start.8 = (bf16[1024,512]{1,0:T(8,128)(2,1)}, bf16[1024,512]{1,0:T(8,128)(2,1)}, u32[]{:S(2)}, u32[]{:S(2)}) collective-permute-start(bf16[1024,512]{1,0:T(8,128)(2,1)} %cut.7.refs_0_), channel_id=1, source_target_pairs={{0,8},{4,12},{8,0},{12,4},{16,24},{20,28},{24,16},{28,20},{1,9},{5... | collective-permute-start | bytes 3145736 | tf_op jit(solution)/shard_map/ppermute | solution.py:539
  56.6 0.7 copy-start.3
  57.3 13.2 %all-to-all-start.2 = ((bf16[4,128,256]{2,1,0:T(8,128)(2,1)}), bf16[4,128,256]{2,1,0:T(8,128)(2,1)S(1)}, u32[]{:S(2)}, u32[]{:S(2)}) async-start(bf16[4,128,256]{2,1,0:T(8,128)(2,1)} %copy-done.3), calls=%async_computation.2 | async-start | bytes 524288 | tf_op jit(solution)/shard_map/all_to_all | solution.py:564
  65.1 22.3 %collective-permute-start.3 = (bf16[128,4096]{1,0:T(8,128)(2,1)}, bf16[128,4096]{1,0:T(8,128)(2,1)}, u32[]{:S(2)}, u32[]{:S(2)}) collective-permute-start(bf16[128,4096]{1,0:T(8,128)(2,1)} %get-tuple-element.32.refs_2_), channel_id=1, source_target_pairs={{1,2},{2,3},{5,6},{6,7},{9,10},{10,11},{13,14},{14,15},{17,18},{18... | collective-permute-start | bytes 3145736 | tf_op jit(solution)/shard_map/ppermute | solution.py:576
  66.8 28.4 %collective-permute-start.4 = (bf16[128,4096]{1,0:T(8,128)(2,1)}, bf16[128,4096]{1,0:T(8,128)(2,1)}, u32[]{:S(2)}, u32[]{:S(2)}) collective-permute-start(bf16[128,4096]{1,0:T(8,128)(2,1)} %get-tuple-element.33), channel_id=1, source_target_pairs={{2,1},{1,0},{6,5},{5,4},{10,9},{9,8},{14,13},{13,12},{18,17},{17,1... | collective-permute-start | bytes 3145736 | tf_op jit(solution)/shard_map/ppermute | solution.py:576
  79.8 2.8 %copy-start.1 = (bf16[1024,256]{1,0:T(8,128)(2,1)S(1)}, bf16[1024,256]{1,0:T(8,128)(2,1)}, u32[]{:S(2)}) copy-start(bf16[1024,256]{1,0:T(8,128)(2,1)} %kv.1) | copy-start | bytes 1572868
  79.8 21.6 %collective-permute-start.11 = (bf16[512,768]{1,0:T(8,128)(2,1)S(1)}, bf16[512,768]{1,0:T(8,128)(2,1)S(1)}, u32[]{:S(2)}, u32[]{:S(2)}) collective-permute-start(bf16[512,768]{1,0:T(8,128)(2,1)S(1)} %get-tuple-element.41), channel_id=1, source_target_pairs={{0,8},{4,12},{8,0},{12,4},{16,24},{20,28},{24,16},{28,20},{1,9},{5... | collective-permute-start | bytes 2359304 | tf_op jit(solution)/shard_map/ppermute | solution.py:539
  81.0 20.5 %collective-permute-start.12 = (bf16[512,768]{1,0:T(8,128)(2,1)S(1)}, bf16[512,768]{1,0:T(8,128)(2,1)S(1)}, u32[]{:S(2)}, u32[]{:S(2)}) collective-permute-start(bf16[512,768]{1,0:T(8,128)(2,1)S(1)} %get-tuple-element.42), channel_id=1, source_target_pairs={{0,16},{4,20},{8,24},{12,28},{16,0},{20,4},{24,8},{28,12},{1,17},{... | collective-permute-start | bytes 2359304 | tf_op jit(solution)/shard_map/ppermute | solution.py:540
  86.6 22.3 %collective-permute-start.9 = (bf16[512,512]{1,0:T(8,128)(2,1)S(1)}, bf16[512,512]{1,0:T(8,128)(2,1)S(1)}, u32[]{:S(2)}, u32[]{:S(2)}) collective-permute-start(bf16[512,512]{1,0:T(8,128)(2,1)S(1)} %get-tuple-element.35.refs_5_), channel_id=1, source_target_pairs={{0,8},{4,12},{8,0},{12,4},{16,24},{20,28},{24,16},{28,20},{1,9},{5... | collective-permute-start | bytes 1572872 | tf_op jit(solution)/shard_map/ppermute | solution.py:539
  87.4 23.0 %collective-permute-start.10 = (bf16[512,512]{1,0:T(8,128)(2,1)S(1)}, bf16[512,512]{1,0:T(8,128)(2,1)S(1)}, u32[]{:S(2)}, u32[]{:S(2)}) collective-permute-start(bf16[512,512]{1,0:T(8,128)(2,1)S(1)} %get-tuple-element.36), channel_id=1, source_target_pairs={{0,16},{4,20},{8,24},{12,28},{16,0},{20,4},{24,8},{28,12},{1,17},{... | collective-permute-start | bytes 1572872 | tf_op jit(solution)/shard_map/ppermute | solution.py:540
  101.5 7.0 %copy-start.5 = (s32[1,256]{1,0:T(1,128)S(1)}, s32[1,256]{1,0:T(1,128)}, u32[]{:S(2)}) copy-start(s32[1,256]{1,0:T(1,128)} %refs_6_.3) | copy-start | bytes 3076
  102.4 1.6 %collective-permute-start.13 = (f32[256,256]{1,0:T(8,128)S(1)}, f32[256,256]{1,0:T(8,128)S(1)}, u32[]{:S(2)}, u32[]{:S(2)}) collective-permute-start(f32[256,256]{1,0:T(8,128)S(1)} %get-tuple-element.45), channel_id=1, source_target_pairs={{0,4},{4,0},{8,12},{12,8},{16,20},{20,16},{24,28},{28,24},{1,5},{5... | collective-permute-start | bytes 786440 | tf_op jit(solution)/shard_map/ppermute | solution.py:541
  104.1 7.1 %collective-permute-start.14 = (bf16[256,128]{1,0:T(8,128)(2,1)S(1)}, bf16[256,128]{1,0:T(8,128)(2,1)S(1)}, u32[]{:S(2)}, u32[]{:S(2)}) collective-permute-start(bf16[256,128]{1,0:T(8,128)(2,1)S(1)} %get-tuple-element.46), channel_id=1, source_target_pairs={{0,1},{1,2},{2,0},{4,5},{5,6},{6,4},{8,9},{9,10},{10,8},{12,13},{1... | collective-permute-start | bytes 196616 | tf_op jit(solution)/shard_map/ppermute | solution.py:576
  107.7 3.4 %collective-permute-start.15 = (bf16[256,128]{1,0:T(8,128)(2,1)S(1)}, bf16[256,128]{1,0:T(8,128)(2,1)S(1)}, u32[]{:S(2)}, u32[]{:S(2)}) collective-permute-start(bf16[256,128]{1,0:T(8,128)(2,1)S(1)} %get-tuple-element.47), channel_id=1, source_target_pairs={{1,3},{2,1},{3,2},{5,7},{6,5},{7,6},{9,11},{10,9},{11,10},{13,15},... | collective-permute-start | bytes 196616 | tf_op jit(solution)/shard_map/ppermute | solution.py:576
  108.5 4.7 %collective-permute-start.17 = (f32[256,512]{1,0:T(8,128)S(1)}, f32[256,512]{1,0:T(8,128)S(1)}, u32[]{:S(2)}, u32[]{:S(2)}) collective-permute-start(f32[256,512]{1,0:T(8,128)S(1)} %get-tuple-element.54), channel_id=1, source_target_pairs={{0,4},{4,0},{8,12},{12,8},{16,20},{20,16},{24,28},{28,24},{1,5},{5... | collective-permute-start | bytes 1572872 | tf_op jit(solution)/shard_map/ppermute | solution.py:541
  111.9 4.3 %collective-permute-start.16 = (f32[256,512]{1,0:T(8,128)S(1)}, f32[256,512]{1,0:T(8,128)S(1)}, u32[]{:S(2)}, u32[]{:S(2)}) collective-permute-start(f32[256,512]{1,0:T(8,128)S(1)} %get-tuple-element.49), channel_id=1, source_target_pairs={{0,4},{4,0},{8,12},{12,8},{16,20},{20,16},{24,28},{28,24},{1,5},{5... | collective-permute-start | bytes 1572872 | tf_op jit(solution)/shard_map/ppermute | solution.py:541
